TPU v7x, 32 devices: a whole 2x2x4 slice. The times are simulated.
32 devices in a mesh: ep: 16 (over z, y, x), dp: 2 (over core).
Axes of the slice: x: 2, y: 2, z: 4, core: 2. Of those that a mesh axis runs over, the one named last changes fastest.
Arguments:
- patches: bfloat16 [32768, 768], P(('ep', 'dp')), may hold values from -6 to 6
- labels: int32 [32768, 256], P(('ep', 'dp')), may hold values from 0 to 39
- pixel_mask: int32 [32768, 256], P(('ep', 'dp')), may hold values from 0 to 1
- patch_valid: int32 [32768], P(('ep', 'dp')), may hold values from 0 to 1, as said below
- tasks: int32 [32], P(('ep', 'dp')), may hold values from 0 to 3
- routes: int32 [32768, 4], P(('ep', 'dp')), may hold values from 0 to 15, all different within a row; in each aligned block of 1024 rows (0 to 1023, 1024 to 2047, ...) at most 384 rows name the same one
- dense_weight: float32 [4468992], P('ep'), may hold values from -2 to 2
- dense_first: float32 [4468992], P('ep'), may hold values from -5.722046e-06 to 5.722046e-06
- dense_second: float32 [4468992], P('ep'), may hold values from 1.7135494e-13 to 6.8541977e-13
- dense_average: float32 [4468992], P('ep'), may hold values from -2 to 2
- expert_in: float32 [16, 384, 1536], P('ep', None, 'dp'), may hold values from -0.3125 to 0.3125
- in_first: float32 [16, 384, 1536], P('ep', None, 'dp'), may hold values from -5.722046e-06 to 5.722046e-06
- in_second: float32 [16, 384, 1536], P('ep', None, 'dp'), may hold values from 1.0709684e-14 to 4.2838735e-14
- in_average: float32 [16, 384, 1536], P('ep', None, 'dp'), may hold values from -0.3125 to 0.3125
- expert_out: float32 [16, 1536, 384], P('ep', 'dp'), may hold values from -0.15625 to 0.15625
- out_first: float32 [16, 1536, 384], P('ep', 'dp'), may hold values from -5.722046e-06 to 5.722046e-06
- out_second: float32 [16, 1536, 384], P('ep', 'dp'), may hold values from 1.7135494e-13 to 6.8541977e-13
- out_average: float32 [16, 1536, 384], P('ep', 'dp'), may hold values from -0.15625 to 0.15625
Outputs:
- loss: float32 [1], replicated
- grad_norm: float32 [1], replicated
- block_norms: float32 [46, 2], replicated
- dense_new: float32 [4468992], P('ep')
- dense_first_new: float32 [4468992], P('ep')
- dense_second_new: float32 [4468992], P('ep')
- dense_average_new: float32 [4468992], P('ep')
- dense_low: bfloat16 [4468992], P('ep')
- in_new: float32 [16, 384, 1536], P('ep', None, 'dp')
- in_first_new: float32 [16, 384, 1536], P('ep', None, 'dp')
- in_second_new: float32 [16, 384, 1536], P('ep', None, 'dp')
- in_average_new: float32 [16, 384, 1536], P('ep', None, 'dp')
- in_low: bfloat16 [16, 384, 1536], P('ep', None, 'dp')
- out_new: float32 [16, 1536, 384], P('ep', 'dp')
- out_first_new: float32 [16, 1536, 384], P('ep', 'dp')
- out_second_new: float32 [16, 1536, 384], P('ep', 'dp')
- out_average_new: float32 [16, 1536, 384], P('ep', 'dp')
- out_low: bfloat16 [16, 1536, 384], P('ep', 'dp')
Inputs may be any that keep to these rules, and one draw needn't show every extreme that they name: `routes`: in the rows of one device each expert is named by at most 384 choices, a bound that some block reaches. `patch_valid`: the valid slots of an image are its first 392 or all 1024; both kinds occur.
All inputs are finite; a program needn't handle non-finite values.
Results may differ from a plain program's by a relative error of at most 0.0055.
The roundings to bfloat16 on the way count: a program that leaves them out, or rounds other values in their place, can miss the bound.
Values may be sent and summed in bfloat16 or wider, within the bound.
No kernel may reach another device: no remote copies, remote signals or barrier semaphores. Data moves between devices by JAX's collectives and lax.ppermute only.
A program may use at most 384 MiB of HBM per device.

v0:
```python
import math

import jax
import jax.numpy as jnp
from jax import lax
from jax.sharding import PartitionSpec as P

D = 384
HEADS = 6
HD = 64
FF = 1536
TOP = 4
C = 40
PIX = 768
TASKS = 4


EPS_NORM = 1e-05
CLIP_NORM = 0.002
RATE = 0.3
DECAY_ONE = 0.5
DECAY_TWO = 0.5
WEIGHT_DECAY = 0.01
EPS_ADAM = 1e-09
AVERAGE = 0.9
SCALE = 0.125
LOWTYPE = jnp.bfloat16
FULLTYPE = jnp.float32


def plain(left, right):
    return jnp.dot(left, right, preferred_element_type=FULLTYPE)


def left_t(left, right):
    return lax.dot_general(left, right, (((0,), (0,)), ((), ())), preferred_element_type=FULLTYPE)


def right_t(left, right):
    return lax.dot_general(left, right, (((1,), (1,)), ((), ())), preferred_element_type=FULLTYPE)


def segment_sizes(experts):
    return (
        [PIX * D]
        + [3 * D * D] * 3
        + [D * D] * 3
        + [D * FF] * 2
        + [FF * D] * 2
        + [TASKS * D * experts, D * C, 14 * D]
    )


def unpack(flat, experts):
    shapes = [
        (PIX, D),
        (3, D, 3 * D),
        (3, D, D),
        (2, D, FF),
        (2, FF, D),
        (TASKS, D, experts),
        (D, C),
        (2, 7, D),
    ]
    pieces = []
    start = 0
    for shape in shapes:
        count = math.prod(shape)
        pieces.append(flat[start : start + count].reshape(shape))
        start += count
    return pieces


def segment_onehot(start, count, experts):
    index = start + jnp.arange(count, dtype=jnp.int32)
    sizes = segment_sizes(experts)
    label = jnp.zeros((count,), jnp.int32)
    edge = 0
    for size in sizes[:-1]:
        edge += size
        label = label + (index >= edge).astype(jnp.int32)
    return label[:, None] == jnp.arange(len(sizes), dtype=jnp.int32)[None, :]


def layer_norm(x, gain, bias):
    mean = jnp.mean(x, -1, keepdims=True)
    cent = x - mean
    var = jnp.mean(cent * cent, -1, keepdims=True)
    return cent * lax.rsqrt(var + EPS_NORM) * gain + bias


def norm_back(x, gain, bias, grad):
    return jax.vjp(layer_norm, x, gain, bias)[1](grad)


def gelu(hidden):
    return jax.nn.gelu(hidden, approximate=False)


def split_heads(qkv16):
    parts = qkv16.reshape(qkv16.shape[0], 3, HEADS, HD)
    return (parts[:, 0], parts[:, 1], parts[:, 2])


def blocks(values, block):
    return values.reshape((values.shape[0] // block, block) + values.shape[1:])


def masked_scores(query, keys, valid):
    scores = jnp.einsum("qhd,khd->hqk", query, keys, preferred_element_type=FULLTYPE) * SCALE
    return jnp.where(valid[None, None, :] > 0, scores, -1e30)


def attend(qkv16, valid):
    query, keys, values = split_heads(qkv16)
    block = min(512, query.shape[0])

    def one(query_block):
        scores = masked_scores(query_block, keys, valid)
        top = jnp.max(scores, -1, keepdims=True)
        total = top + jnp.log(jnp.sum(jnp.exp(scores - top), -1, keepdims=True))
        probs = jnp.exp(scores - total).astype(LOWTYPE)
        return (
            jnp.einsum("hqk,khd->qhd", probs, values, preferred_element_type=FULLTYPE).astype(
                LOWTYPE
            ),
            total,
        )

    out, totals = lax.map(one, blocks(query, block))
    return (out.reshape(qkv16.shape[0], D), totals)


def attend_back(qkv16, valid, totals, grad16):
    query, keys, values = split_heads(qkv16)
    seq = qkv16.shape[0]
    block = min(512, seq)

    def one(item):
        query_block, total, grad_block = item
        scores = masked_scores(query_block, keys, valid)
        probs = jnp.exp(scores - total)
        d_values = jnp.einsum(
            "hqk,qhd->khd", probs.astype(LOWTYPE), grad_block, preferred_element_type=FULLTYPE
        )
        d_probs = jnp.einsum("qhd,khd->hqk", grad_block, values, preferred_element_type=FULLTYPE)
        d_scores = (probs * (d_probs - jnp.sum(probs * d_probs, -1, keepdims=True))).astype(LOWTYPE)
        d_query = (
            jnp.einsum("hqk,khd->qhd", d_scores, keys, preferred_element_type=FULLTYPE) * SCALE
        )
        d_keys = (
            jnp.einsum("hqk,qhd->khd", d_scores, query_block, preferred_element_type=FULLTYPE)
            * SCALE
        )
        return (d_query, d_keys, d_values)

    grads = grad16.reshape(seq, HEADS, HD)
    d_query, d_keys, d_values = lax.map(one, (blocks(query, block), totals, blocks(grads, block)))
    stacked = jnp.stack(
        [d_query.reshape(seq, HEADS, HD), jnp.sum(d_keys, 0), jnp.sum(d_values, 0)], 1
    )
    return stacked.reshape(seq, 3 * D)


def attn_forward(x, w_qkv, w_attn, gains, valid):
    normed16 = layer_norm(x, gains[0], gains[1]).astype(LOWTYPE)
    qkv16 = plain(normed16, w_qkv).astype(LOWTYPE)
    out16, totals = attend(qkv16, valid)
    return (x + plain(out16, w_attn), (qkv16, out16, totals))


def attn_backward(x, w_qkv, w_attn, gains, valid, kept, grad):
    qkv16, out16, totals = kept
    grad16 = grad.astype(LOWTYPE)
    d_attn = left_t(out16, grad16)
    d_out16 = right_t(grad16, w_attn).astype(LOWTYPE)
    d_qkv16 = attend_back(qkv16, valid, totals, d_out16).astype(LOWTYPE)
    normed16 = layer_norm(x, gains[0], gains[1]).astype(LOWTYPE)
    d_qkvw = left_t(normed16, d_qkv16)
    d_x, d_gain, d_bias = norm_back(x, gains[0], gains[1], right_t(d_qkv16, w_qkv))
    return (grad + d_x, d_qkvw, d_attn, d_gain, d_bias)


def feed_forward(rows16, w_up, w_back):
    hidden = plain(rows16, w_up)
    return (plain(gelu(hidden).astype(LOWTYPE), w_back), hidden)


def feed_backward(rows16, hidden, grad16, w_up, w_back):
    act16 = gelu(hidden).astype(LOWTYPE)
    d_back = left_t(act16, grad16)
    d_act = right_t(grad16, w_back)
    d_hidden = jax.vjp(gelu, hidden)[1](d_act)[0].astype(LOWTYPE)
    return (right_t(d_hidden, w_up), (left_t(rows16, d_hidden), d_back))


def make_slots(routes, experts, capacity):
    flat = routes.reshape(-1)
    hot = (flat[:, None] == jnp.arange(experts, dtype=jnp.int32)[None, :]).astype(jnp.int32)
    rank = jnp.sum((jnp.cumsum(hot, 0) - hot) * hot, 1)
    slot = flat * capacity + rank
    assign = (
        jnp.zeros((experts * capacity,), jnp.int32)
        .at[slot]
        .set(jnp.arange(flat.shape[0], dtype=jnp.int32))
    )
    used = jnp.zeros((experts * capacity,), jnp.int32).at[slot].set(1)
    return (slot, assign, used)


def to_experts(buffer):
    return lax.all_to_all(buffer, "ep", split_axis=0, concat_axis=0, tiled=True)


def from_experts(buffer):
    return lax.all_to_all(
        buffer.astype(jnp.bfloat16), "ep", split_axis=0, concat_axis=0, tiled=True
    ).astype(buffer.dtype)


def per_device(
    patches,
    labels,
    pixel_mask,
    patch_valid,
    tasks,
    routes,
    dense_weight,
    dense_first,
    dense_second,
    dense_average,
    expert_in,
    in_first,
    in_second,
    in_average,
    expert_out,
    out_first,
    out_second,
    out_average,
):
    ep_count = lax.axis_size("ep")
    experts = min(16, ep_count)
    copies = ep_count // experts
    groups = lax.axis_size("dp")
    ep_place = lax.axis_index("ep")
    dp_place = lax.axis_index("dp")
    own_expert = ep_place // copies
    seq = patches.shape[0]
    capacity = 3 * seq * TOP // (2 * experts)
    gathered = lax.all_gather(dense_weight.astype(LOWTYPE), "ep", axis=0, tiled=True)
    w_patch, w_qkv, w_attn, w_up, w_down, w_router, w_head, norms16 = unpack(gathered, experts)
    norms = norms16.astype(FULLTYPE)
    own_in, own_out = (
        lax.all_gather(expert_in.astype(LOWTYPE), "dp", axis=2, tiled=True),
        lax.all_gather(expert_out.astype(LOWTYPE), "dp", axis=1, tiled=True),
    )
    own_in = own_in[0]
    own_out = own_out[0]
    task = tasks[0]
    router = lax.dynamic_index_in_dim(w_router, task, 0, keepdims=False)
    slot, assign, used = make_slots(routes, experts, capacity)
    route_hot = (routes[:, :, None] == jnp.arange(experts, dtype=jnp.int32)[None, None, :]).astype(
        FULLTYPE
    )

    def dispatch(send):
        buffer = jnp.repeat(send.reshape(experts, capacity, D), copies, axis=0)
        return to_experts(buffer)

    def combine(partial_value):
        back = from_experts(partial_value).reshape(experts, copies, capacity, D)
        summed = jnp.sum(back, 1).astype(LOWTYPE).reshape(experts * capacity, D)
        return summed[slot].reshape(seq, TOP, D).astype(FULLTYPE)

    def expert_backward(arrived, rows, hidden):
        d_rows, (d_in, d_out) = feed_backward(rows, hidden, arrived.reshape(-1, D), own_in, own_out)
        d_in_own, d_out_own = (
            lax.psum_scatter(
                d_in[None].astype(jnp.bfloat16), "dp", scatter_dimension=2, tiled=True
            ).astype(jnp.float32),
            lax.psum_scatter(
                d_out[None].astype(jnp.bfloat16), "dp", scatter_dimension=1, tiled=True
            ).astype(jnp.float32),
        )
        return (d_rows.reshape(arrived.shape), d_in_own, d_out_own)

    def layer_backward(grad, layer, saved):
        x, x_mid, kept_attn, kept = saved
        gain_two, bias_two = (norms[0, 2 * layer + 1], norms[1, 2 * layer + 1])
        c16 = layer_norm(x_mid, gain_two, bias_two).astype(LOWTYPE)
        if layer == 1:
            gates, picks, rows, hidden = kept
            d_gates = jnp.sum(grad[:, None, :] * picks, -1)
            d_picked = gates * (d_gates - jnp.sum(gates * d_gates, -1, keepdims=True))
            d_logits = jnp.sum(route_hot * d_picked[:, :, None], 1).astype(LOWTYPE)
            task_hot = (jnp.arange(TASKS, dtype=jnp.int32) == task)[:, None, None]
            d_router = jnp.where(task_hot, left_t(c16, d_logits)[None], 0.0)
            d_c = right_t(d_logits, router)
            d_picks = (gates[:, :, None] * grad[:, None, :]).astype(LOWTYPE).reshape(seq * TOP, D)
            send = jnp.where(used[:, None] > 0, d_picks[assign], jnp.zeros((), LOWTYPE))
            d_rows, d_in_own, d_out_own = expert_backward(dispatch(send), rows, hidden)
            d_c = d_c + jnp.sum(combine(d_rows), 1)
            mats = (d_router, d_in_own, d_out_own)
        else:
            d_c, mats = feed_backward(
                c16, kept, grad.astype(LOWTYPE), w_up[layer // 2], w_down[layer // 2]
            )
        d_mid, d_gain_two, d_bias_two = norm_back(x_mid, gain_two, bias_two, d_c)
        d_x, d_qkvw, d_attn, d_gain_one, d_bias_one = attn_backward(
            x,
            w_qkv[layer],
            w_attn[layer],
            norms[:, 2 * layer],
            patch_valid,
            kept_attn,
            grad + d_mid,
        )
        return (d_x, (d_qkvw, d_attn, mats, (d_gain_one, d_gain_two), (d_bias_one, d_bias_two)))

    x = plain(patches, w_patch)
    saves = []
    for layer in range(3):
        layer_x_mid, layer_kept_attn = attn_forward(
            x, w_qkv[layer], w_attn[layer], norms[:, 2 * layer], patch_valid
        )
        layer_c16 = layer_norm(
            layer_x_mid, norms[0, 2 * layer + 1], norms[1, 2 * layer + 1]
        ).astype(LOWTYPE)
        if layer == 1:
            layer_logits = plain(layer_c16, router)
            layer_gates = jax.nn.softmax(jnp.sum(route_hot * layer_logits[:, None, :], -1), -1)
            layer_send = jnp.where(
                used[:, None] > 0, layer_c16[assign // TOP], jnp.zeros((), LOWTYPE)
            )
            expert_arrived = dispatch(layer_send)
            expert_rows = expert_arrived.reshape(-1, D)
            out, expert_hidden = feed_forward(expert_rows, own_in, own_out)
            layer_partial_value = out.reshape(expert_arrived.shape)
            layer_hidden = expert_hidden
            layer_picks = combine(layer_partial_value)
            x_next = layer_x_mid + jnp.sum(layer_gates[:, :, None] * layer_picks, 1)
            layer_kept = (layer_gates, layer_picks, expert_rows, layer_hidden)
        else:
            layer_out, layer_hidden = feed_forward(layer_c16, w_up[layer // 2], w_down[layer // 2])
            x_next = layer_x_mid + layer_out
            layer_kept = layer_hidden
        x, saved = (x_next, (x, layer_x_mid, layer_kept_attn, layer_kept))
        saves.append(saved)
    f16 = layer_norm(x, norms[0, 6], norms[1, 6]).astype(LOWTYPE)
    logits = plain(f16, w_head)
    weight_pix = (pixel_mask * patch_valid[:, None]).astype(FULLTYPE)
    count_tok = jnp.sum(weight_pix, 1)
    class_hot = labels[:, :, None] == jnp.arange(C, dtype=jnp.int32)[None, None, :]
    counts = jnp.sum(jnp.where(class_hot, weight_pix[:, :, None], 0.0), 1)
    top = jnp.max(logits, -1, keepdims=True)
    lse = top[:, 0] + jnp.log(jnp.sum(jnp.exp(logits - top), -1))
    local = jnp.sum(count_tok * lse) - jnp.sum(counts * logits)
    loss_sum, total = lax.psum((local, jnp.sum(count_tok)), ("ep", "dp"))
    loss = loss_sum / total
    d_logits = ((count_tok[:, None] * jax.nn.softmax(logits, -1) - counts) / total).astype(LOWTYPE)
    d_head = left_t(f16, d_logits)
    grad, d_gain_f, d_bias_f = norm_back(x, norms[0, 6], norms[1, 6], right_t(d_logits, w_head))
    d_qkv_list = [None] * 3
    d_attn_list = [None] * 3
    d_up_list = [None] * 2
    d_down_list = [None] * 2
    gain_list = [None] * 7
    bias_list = [None] * 7
    gain_list[6] = d_gain_f
    bias_list[6] = d_bias_f
    for layer in (2, 1, 0):
        grad, pieces = layer_backward(grad, layer, saves[layer])
        d_qkv_list[layer], d_attn_list[layer] = (pieces[0], pieces[1])
        gain_list[2 * layer], gain_list[2 * layer + 1] = pieces[3]
        bias_list[2 * layer], bias_list[2 * layer + 1] = pieces[4]
        if layer == 1:
            d_router, d_in, d_out = pieces[2]
        else:
            d_up_list[layer // 2], d_down_list[layer // 2] = pieces[2]
    d_patch = left_t(patches, grad.astype(LOWTYPE))
    d_norms = jnp.stack([jnp.stack(gain_list), jnp.stack(bias_list)])
    listed = [
        d_patch,
        jnp.stack(d_qkv_list),
        jnp.stack(d_attn_list),
        jnp.stack(d_up_list),
        jnp.stack(d_down_list),
        d_router,
        d_head,
        d_norms,
    ]
    flat_grad = jnp.concatenate([piece.reshape(-1) for piece in listed])
    shard = dense_weight.shape[0]
    summed = lax.psum(flat_grad, ("ep", "dp"))
    dense_grad = lax.dynamic_slice_in_dim(summed, ep_place * shard, shard)
    piece = shard // groups
    part_hot = segment_onehot(ep_place * shard + dp_place * piece, piece, experts)
    expert_hot = (jnp.arange(experts, dtype=jnp.int32) == own_expert).astype(FULLTYPE)

    def block_sums(dense_vals, in_vals, out_vals):
        part = lax.dynamic_slice_in_dim(dense_vals, dp_place * piece, piece)
        dense_part = jnp.sum(jnp.where(part_hot, (part * part)[:, None], 0.0), 0)
        return jnp.concatenate(
            [
                dense_part,
                expert_hot * jnp.sum(in_vals * in_vals),
                expert_hot * jnp.sum(out_vals * out_vals),
            ]
        )

    grad_total, weight_total = lax.psum(
        (
            jnp.sum(block_sums(dense_grad, d_in, d_out)),
            block_sums(dense_weight, expert_in, expert_out),
        ),
        ("ep", "dp"),
    )
    grad_norm = jnp.sqrt(grad_total)
    clip = CLIP_NORM / jnp.maximum(grad_norm, CLIP_NORM)

    def moments(weight, first, second, gradient):
        gradient = gradient * clip
        first_new = DECAY_ONE * first + (1.0 - DECAY_ONE) * gradient
        second_new = DECAY_TWO * second + (1.0 - DECAY_TWO) * gradient * gradient
        return (
            first_new,
            second_new,
            first_new / (jnp.sqrt(second_new) + EPS_ADAM) + WEIGHT_DECAY * weight,
        )

    dense_m, dense_v, dense_step = moments(dense_weight, dense_first, dense_second, dense_grad)
    in_m, in_v, in_step = moments(expert_in, in_first, in_second, d_in)
    out_m, out_v, out_step = moments(expert_out, out_first, out_second, d_out)
    update_total = lax.psum(block_sums(dense_step, in_step, out_step), ("ep", "dp"))
    weight_norm = jnp.sqrt(weight_total)
    update_norm = jnp.sqrt(update_total)
    ratio = weight_norm / (update_norm + EPS_NORM)
    whole_hot = segment_onehot(ep_place * shard, shard, experts)
    dense_ratio = jnp.sum(jnp.where(whole_hot, ratio[None, :14], 0.0), 1)
    in_ratio = lax.dynamic_index_in_dim(ratio, 14 + own_expert, 0, keepdims=False)
    out_ratio = lax.dynamic_index_in_dim(ratio, 14 + experts + own_expert, 0, keepdims=False)

    def finish(weight, average, step, rate):
        new = weight - RATE * rate * step
        return (new, AVERAGE * average + (1.0 - AVERAGE) * new, new.astype(LOWTYPE))

    dense_new, dense_avg, dense_low = finish(dense_weight, dense_average, dense_step, dense_ratio)
    in_new, in_avg, in_low = finish(expert_in, in_average, in_step, in_ratio)
    out_new, out_avg, out_low = finish(expert_out, out_average, out_step, out_ratio)
    block_norms = jnp.stack([weight_norm, update_norm], 1)
    return (
        loss.reshape(1),
        grad_norm.reshape(1),
        block_norms,
        dense_new,
        dense_m,
        dense_v,
        dense_avg,
        dense_low,
        in_new,
        in_m,
        in_v,
        in_avg,
        in_low,
        out_new,
        out_m,
        out_v,
        out_avg,
        out_low,
    )


def solution(mesh):
    in_specs = (
        P(("ep", "dp"), None),
        P(("ep", "dp"), None),
        P(("ep", "dp"), None),
        P(("ep", "dp")),
        P(("ep", "dp")),
        P(("ep", "dp"), None),
        P("ep"),
        P("ep"),
        P("ep"),
        P("ep"),
        P("ep", None, "dp"),
        P("ep", None, "dp"),
        P("ep", None, "dp"),
        P("ep", None, "dp"),
        P("ep", "dp", None),
        P("ep", "dp", None),
        P("ep", "dp", None),
        P("ep", "dp", None),
    )
    out_specs = (
        P(),
        P(),
        P(),
        P("ep"),
        P("ep"),
        P("ep"),
        P("ep"),
        P("ep"),
        P("ep", None, "dp"),
        P("ep", None, "dp"),
        P("ep", None, "dp"),
        P("ep", None, "dp"),
        P("ep", None, "dp"),
        P("ep", "dp", None),
        P("ep", "dp", None),
        P("ep", "dp", None),
        P("ep", "dp", None),
        P("ep", "dp", None),
    )
    return jax.shard_map(
        per_device, mesh=mesh, in_specs=in_specs, out_specs=out_specs, check_vma=False
    )
```

profile of v0, /device:TPU:0, one launch (start us, length us, event | category | flops | bytes accessed | tf_op | source)
XLA Modules:
  0.0 2231.7 jit_solution(1088285622490761204)
XLA Ops:
  15.5 9.6 dynamic-update-slice
  32.9 15.5 scatter_custom_fusion.1
  48.4 15.5 scatter_custom_fusion
  65.3 233.7 %all-reduce.7.cloned.1.call-done = bf16[4468992]{0:T(1024)(128)(2,1)} async-done(((bf16[4468992]{0:T(1024)(128)(2,1)}), bf16[4468992]{0:T(1024)(128)(2,1)}) %all-reduce.7.cloned.1.call-update) | async-done | bytes 8938000
  326.2 21.7 while.78
  369.9 19.1 multiply_convert_fusion.6
  409.6 22.8 %while.79 = (s32[]{:T(128)}, bf16[2,512,6,64]{1,3,2,0:T(8,128)(2,1)}, f32[2,6,512,1]{2,1,3,0:T(8,128)}, s32[1024]{0:T(1024)S(1)}, bf16[2,512,6,64]{1,3,2,0:T(8,1...) while((s32[]{:T(128)}, bf16[2,512,6,64]{1,3,2,0:T(8,128)(2,1)}, ...), condition=%wide.region_14.15_spmd, body=%wide.region_11.14_spmd.sunk | while | flops 840103936 | bytes 40220244 | solution.py:130
  440.4 25.1 %gather_fusion = bf16[6144,384]{1,0:T(8,128)(2,1)} fusion(bf16[1024,384]{1,0:T(8,128)(2,1)S(1)} %copy.211, s32[6144]{0:T(1024)S(1)} %copy-done.142), kind=kCustom, calls=%fused_computation | custom fusion | bytes 9461760 | tf_op jit(solution)/shard_map/gather | solution.py:333
  479.5 9.8 all-gather.3.cloned.1.call-done
  489.2 76.2 %all-to-all-done = bf16[16,384,384]{2,1,0:T(8,128)(2,1)} async-done(((bf16[16,384,384]{2,1,0:T(8,128)(2,1)}), bf16[16,384,384]{2,1,0:T(8,128)(2,1)}, u32[]{:S(2)}, u32[]{:S(2)}) %all-to-all-start) | async-done | bytes 4718624 | tf_op jit(solution)/shard_map/all_to_all | solution.py:212
  565.5 88.9 %multiply_convert_fusion.3 = (bf16[6144,1536]{1,0:T(8,128)(2,1)}, f32[6144,1536]{1,0:T(8,128)}, f32[6144,1536]{1,0:T(8,128)}) fusion(bf16[6144,384]{1,0:T(8,128)(2,1)} %bitcast.53, bf16[1,384,1536]{2,1,0:T(8,128)(2,1)} %all-gather.3.cloned.1.call-done), kind=kOutput, calls=%fused_computation.149 | convolution fusion | flops 7861174272 | bytes 100270080 | tf_op jit(solution)/shard_map/dot_general | solution.py:32
  654.3 15.5 convolution_convert_fusion.4
  669.8 22.5 %all-to-all-start.1 = ((bf16[16,384,384]{2,1,0:T(8,128)(2,1)}), bf16[16,384,384]{2,1,0:T(8,128)(2,1)}, u32[]{:S(2)}, u32[]{:S(2)}) async-start(bf16[16,384,384]{2,1,0:T(8,128)(2,1)} %convolution_convert_fusion.4), calls=%async_computation.1 | async-start | bytes 9437184 | tf_op jit(solution)/shard_map/all_to_all | solution.py:216
  694.6 123.0 %psum.43 = f32[]{:T(128)} all-reduce(f32[]{:T(128)} %get-tuple-element.562), channel_id=1, replica_groups=mesh['ep'=16,'dp'=2] {'ep','dp'}, use_global_device_ids=true, to_apply=%region_43.44 | all-reduce | flops 1 | bytes 8 | tf_op jit(solution)/shard_map/psum | solution.py:358
  818.3 15.8 select_reduce_fusion
  848.9 19.6 gather_fusion.1
  875.2 9.2 multiply_reduce_fusion.4
  903.7 21.7 while.80
  929.2 18.0 multiply_convert_fusion.5
  988.3 88.0 %while.81 = (s32[]{:T(128)}, bf16[2,512,6,64]{1,0,3,2:T(2,128)(2,1)}, f32[2,1024,6,64]{1,3,2,0:T(8,128)}, f32[2,1024,6,64]{1,3,2,0:T(8,128)}, s32[1024]{0:T(1024...) while((s32[]{:T(128)}, ...), condition=%wide.region_50.51_spmd, body=%wide.region_48.50_spmd.sunk | while | flops 2061236224 | bytes 185302256 | solution.py:158
  1009.8 14.1 dynamic_update_slice.84
  1023.8 8.6 bitcast_dynamic-update-slice_fusion.22
  1053.7 14.1 dynamic_update_slice.84
  1067.8 8.5 bitcast_dynamic-update-slice_fusion.22
  1106.6 7.7 mul.1062
  1118.7 26.8 %gather_fusion.2 = bf16[6144,384]{1,0:T(8,128)(2,1)} fusion(bf16[4096,384]{1,0:T(8,128)(2,1)} %multiply_convert_fusion.4, s32[6144]{0:T(1024)S(1)} %copy-done.141), kind=kCustom, calls=%fused_computation.2 | custom fusion | bytes 9461760 | tf_op jit(solution)/shard_map/gather | solution.py:300
  1149.1 109.5 %all_to_all.20 = bf16[16,384,384]{2,1,0:T(8,128)(2,1)} all-to-all(bf16[16,384,384]{2,1,0:T(8,128)(2,1)S(1)} %broadcast_select_fusion), channel_id=1, replica_groups=mesh['ep'=16,'dp'=2] {'ep'}, dimensions={0} | all-to-all | bytes 9437184 | tf_op jit(solution)/shard_map/all_to_all | solution.py:212
  1258.6 37.8 %add_convert_fusion = bf16[6144,1536]{1,0:T(8,128)(2,1)} fusion(f32[6144,1536]{1,0:T(8,128)} %get-tuple-element.719, f32[6144,1536]{1,0:T(8,128)} %get-tuple-element.770, bf16[6144,384]{1,0:T(8,128)(2,1)} %bitcast.501, bf16[1,1536,384]{2,1,0:T(8,128)(2,1)} %all-gather.5.cloned.1.call-done), kind=kOutput, calls=%fused_computation.148 | convolution fusion | flops 7379877888 | bytes 100270080 | tf_op jit(solution)/shard_map/dot_general | solution.py:40
  1296.5 15.7 convolution_convert_fusion.3
  1349.7 13.7 fusion.123
  1371.2 16.2 fusion.124
  1387.9 15.7 all-to-all-done.3
  1403.6 19.6 gather_fusion.3
  1429.9 7.7 reduce_sum.783
  1454.3 89.4 %while.82 = (s32[]{:T(128)}, bf16[2,512,6,64]{1,0,3,2:T(2,128)(2,1)}, f32[2,1024,6,64]{1,3,2,0:T(8,128)}, f32[2,1024,6,64]{1,3,2,0:T(8,128)}, s32[1024]{0:T(1024...) while((s32[]{:T(128)}, ...), condition=%wide.region_63.64_spmd, body=%wide.region_61.63_spmd.sunk | while | flops 2061236224 | bytes 185302256 | solution.py:158
  1476.4 14.1 dynamic_update_slice.87
  1490.5 8.5 bitcast_dynamic-update-slice_fusion.24
  1521.0 14.1 dynamic_update_slice.87
  1535.1 8.6 bitcast_dynamic-update-slice_fusion.24
  1599.9 88.0 %while.83 = (s32[]{:T(128)}, bf16[2,512,6,64]{1,0,3,2:T(2,128)(2,1)}, f32[2,1024,6,64]{1,3,2,0:T(8,128)}, f32[2,1024,6,64]{1,3,2,0:T(8,128)}, s32[1024]{0:T(1024...) while((s32[]{:T(128)}, ...), condition=%wide.region_72.73_spmd, body=%wide.region_70.72_spmd.sunk | while | flops 2061236224 | bytes 185302256 | solution.py:158
  1621.3 14.1 dynamic_update_slice.90
  1635.4 8.6 bitcast_dynamic-update-slice_fusion.26
  1665.2 14.1 dynamic_update_slice.90
  1679.3 8.6 bitcast_dynamic-update-slice_fusion.26
  1783.9 295.5 %all-reduce.5.cloned.1.call-done = f32[4468992]{0:T(1024)} async-done(((f32[4468992]{0:T(1024)}), f32[4468992]{0:T(1024)}) %all-reduce.5.cloned.1.call-update) | async-done | bytes 17875984 | tf_op jit(solution)/shard_map/psum | solution.py:394
  2087.7 40.1 %psum.45 = f32[]{:T(128)} all-reduce(f32[]{:T(128)S(6)} %reduce_sum.840), channel_id=1, replica_groups=mesh['ep'=16,'dp'=2] {'ep','dp'}, use_global_device_ids=true, to_apply=%region_99.100 | all-reduce | flops 1 | bytes 8 | tf_op jit(solution)/shard_map/psum | solution.py:411
  2147.4 39.9 %all-reduce.1 = (f32[]{:T(128)}, f32[46]{0:T(128)S(1)}, f32[46]{0:T(128)S(1)}) all-reduce(f32[]{:T(128)S(6)} %sub.195, f32[46]{0:T(128)S(1)} %pad_maximum_fusion.7, f32[46]{0:T(128)S(1)} %pad_maximum_fusion.6), channel_id=1, replica_groups=mesh['ep'=16,'dp'=2] {'ep','dp'}, use_global_device_ids=true, to_apply=%region_41.42 | all-reduce | flops 93 | bytes 744 | tf_op jit(solution)/shard_map/psum | solution.py:358
  2189.2 17.9 select_reduce_fusion.1
  (909 shorter events, 685.2 us)
Async XLA Ops:
  8.0 293.2 %copy-start = (bf16[1024,768]{1,0:T(8,128)(2,1)S(1)}, bf16[1024,768]{1,0:T(8,128)(2,1)}, u32[]{:S(2)}) copy-start(bf16[1024,768]{1,0:T(8,128)(2,1)} %param.30) | copy-start | bytes 4718596
  8.0 290.9 %all-reduce.7.cloned.1.call-start = ((), (), s32[]{:S(2)}) async-start(), calls=%async_computation.11 | async-start | bytes 17879040
  32.9 32.4 %copy-start.149 = (s32[4096,1]{0,1:T(1,128)}, s32[4096,1]{0,1:T(1,128)S(1)}, u32[]{:S(2)}) copy-start(s32[4096,1]{0,1:T(1,128)S(1)} %compare_select_fusion) | copy-start | bytes 49156
  303.1 9.0 copy-start.22
  303.1 9.0 copy-start.146
  305.5 64.3 %copy-start.201 = (f32[384]{0:T(512)}, f32[384]{0:T(512)S(1)}, u32[]{:S(2)}) copy-start(f32[384]{0:T(512)S(1)} %get-tuple-element.579) | copy-start | bytes 4612
  305.5 64.3 %copy-start.227 = (f32[384]{0:T(512)}, f32[384]{0:T(512)S(1)}, u32[]{:S(2)}) copy-start(f32[384]{0:T(512)S(1)} %get-tuple-element.578) | copy-start | bytes 4612
  305.5 89.1 %copy-start.198 = (f32[384]{0:T(512)}, f32[384]{0:T(512)S(1)}, u32[]{:S(2)}) copy-start(f32[384]{0:T(512)S(1)} %get-tuple-element.577) | copy-start | bytes 4612
  305.5 89.1 %copy-start.223 = (f32[384]{0:T(512)}, f32[384]{0:T(512)S(1)}, u32[]{:S(2)}) copy-start(f32[384]{0:T(512)S(1)} %get-tuple-element.576) | copy-start | bytes 4612
  356.6 13.2 copy-start.153
  358.6 11.3 copy-start.188
  369.8 19.2 copy-start.31
  369.9 19.2 copy-start.104
  440.0 25.5 %copy-start.54 = (bf16[1024,384]{0,1:T(8,128)(2,1)}, bf16[1024,384]{0,1:T(8,128)(2,1)S(1)}, u32[]{:S(2)}) copy-start(bf16[1024,384]{0,1:T(8,128)(2,1)S(1)} %add_convert_fusion.7) | copy-start | bytes 2359300
  440.4 25.1 %copy-start.159 = (pred[16,384]{1,0:T(8,128)(4,1)S(1)}, pred[16,384]{1,0:T(8,128)(4,1)}, u32[]{:S(2)}) copy-start(pred[16,384]{1,0:T(8,128)(4,1)} %broadcast_in_dim.326) | copy-start | bytes 18436
  471.4 94.1 %all-to-all-start = ((bf16[16,384,384]{2,1,0:T(8,128)(2,1)}), bf16[16,384,384]{2,1,0:T(8,128)(2,1)}, u32[]{:S(2)}, u32[]{:S(2)}) async-start(bf16[16,384,384]{2,1,0:T(8,128)(2,1)} %broadcast_select_fusion.1), calls=%async_computation | async-start | bytes 9437184 | tf_op jit(solution)/shard_map/all_to_all | solution.py:212
  476.2 13.0 all-gather.3.cloned.1.call-start
  478.5 175.8 %all-gather.5.cloned.1.call-start = ((), (), s32[]{:S(2)}) async-start(), calls=%async_computation.7 | async-start | bytes 1769472 | tf_op jit(solution)/shard_map/all_gather | solution.py:255
  669.8 22.5 %copy-start.80 = (s32[1024]{0:T(1024)S(1)}, s32[1024]{0:T(1024)}, u32[]{:S(2)}) copy-start(s32[1024]{0:T(1024)} %copy-done.79) | copy-start | bytes 12292
  669.8 179.0 %all-to-all-start.1 = ((bf16[16,384,384]{2,1,0:T(8,128)(2,1)}), bf16[16,384,384]{2,1,0:T(8,128)(2,1)}, u32[]{:S(2)}, u32[]{:S(2)}) async-start(bf16[16,384,384]{2,1,0:T(8,128)(2,1)} %convolution_convert_fusion.4), calls=%async_computation.1 | async-start | bytes 9437184 | tf_op jit(solution)/shard_map/all_to_all | solution.py:216
  692.4 143.6 %copy-start.150 = (s32[4096,1]{0,1:T(1,128)S(1)}, s32[4096,1]{0,1:T(1,128)}, u32[]{:S(2)}) copy-start(s32[4096,1]{0,1:T(1,128)} %copy-done.149) | copy-start | bytes 49156
  692.4 143.6 %slice-start.4 = ((bf16[4468992]{0:T(1024)(128)(2,1)}), bf16[24576]{0:T(1024)(128)(2,1)S(1)}, s32[]{:S(2)}) async-start(bf16[4468992]{0:T(1024)(128)(2,1)} %all-reduce.7.cloned.1.call-done), calls=%async_computation.16 | async-start | bytes 98304 | tf_op jit(solution)/shard_map/slice | solution.py:69
  694.6 256.8 %copy-start.167 = (f32[1024]{0:T(1024)}, f32[1024]{0:T(1024)S(1)}, u32[]{:S(2)}) copy-start(f32[1024]{0:T(1024)S(1)} %get-tuple-element.563) | copy-start | bytes 12292
  694.6 141.7 %copy-start.55 = (bf16[1024,384]{0,1:T(8,128)(2,1)S(1)}, bf16[1024,384]{0,1:T(8,128)(2,1)}, u32[]{:S(2)}) copy-start(bf16[1024,384]{0,1:T(8,128)(2,1)} %copy-done.54) | copy-start | bytes 2359300
  818.3 18.3 copy-start.127
  836.0 12.9 copy-start.130
  836.7 9.1 copy-start.137
  928.3 49.3 %copy-start.33 = (f32[1024,384]{0,1:T(8,128)}, f32[1024,384]{0,1:T(8,128)S(1)}, u32[]{:S(2)}) copy-start(f32[1024,384]{0,1:T(8,128)S(1)} %get-tuple-element.772) | copy-start | bytes 4718596
  928.3 49.2 %copy-start.157 = (f32[1024]{0:T(1024)}, f32[1024]{0:T(1024)S(1)}, u32[]{:S(2)}) copy-start(f32[1024]{0:T(1024)S(1)} %broadcast_multiply_fusion.2) | copy-start | bytes 12292
  928.6 49.0 %copy-start.190 = (f32[1024]{0:T(1024)}, f32[1024]{0:T(1024)S(1)}, u32[]{:S(2)}) copy-start(f32[1024]{0:T(1024)S(1)} %fusion.195) | copy-start | bytes 12292
  929.2 18.0 copy-start.108
  960.8 17.2 copy-start.163
  1118.7 26.8 %copy-start.160 = (pred[16,384]{1,0:T(8,128)(4,1)S(1)}, pred[16,384]{1,0:T(8,128)(4,1)}, u32[]{:S(2)}) copy-start(pred[16,384]{1,0:T(8,128)(4,1)} %broadcast_in_dim.326) | copy-start | bytes 18436
  1312.1 91.4 %all-to-all-start.3 = ((bf16[16,384,384]{2,1,0:T(8,128)(2,1)}), bf16[16,384,384]{2,1,0:T(8,128)(2,1)}, u32[]{:S(2)}, u32[]{:S(2)}) async-start(bf16[16,384,384]{2,1,0:T(8,128)(2,1)} %convolution_convert_fusion.3), calls=%async_computation.3 | async-start | bytes 9437184 | tf_op jit(solution)/shard_map/all_to_all | solution.py:216
  1316.7 460.8 %reduce-scatter.3.cloned.1.call-start = ((), (), s32[]{:S(2)}) async-start(), calls=%async_computation.9 | async-start | bytes 1769472 | tf_op jit(solution)/shard_map/reduce_scatter | solution.py:278
  1317.5 14.8 copy-start.98
  1317.5 14.8 copy-start.100
  1317.5 14.8 copy-start.144
  1317.5 14.8 copy-start.168
  1317.5 14.8 copy-start.171
  1323.5 13.3 copy-start.122
  1323.5 13.3 copy-start.138
  1323.5 13.3 copy-start.152
  1323.5 13.3 copy-start.128
  1363.4 417.3 %reduce-scatter.5.cloned.1.call-start = ((), (), s32[]{:S(2)}) async-start(), calls=%async_computation.10 | async-start | bytes 1769472 | tf_op jit(solution)/shard_map/reduce_scatter | solution.py:281
  1371.2 32.4 %copy-start.131 = (s32[4096]{0:T(1024)S(1)}, s32[4096]{0:T(1024)}, u32[]{:S(2)}) copy-start(s32[4096]{0:T(1024)} %copy-done.130) | copy-start | bytes 49156
  1387.4 692.0 %all-reduce.5.cloned.1.call-start = ((), (), s32[]{:S(2)}) async-start(), calls=%async_computation.8 | async-start | bytes 35758080 | tf_op jit(solution)/shard_map/psum | solution.py:394
  2187.3 19.9 copy-start.68
  (222 other events, 742.4 us)
Sparse Core Ops, SparseCore 0:
  25.3 273.6 all-reduce.6
Sparse Core Ops, SparseCore 1:
  478.8 10.3 all-gather.2
  491.3 10.3 all-gather.4
  1363.5 9.8 reduce-scatter.2
  1387.5 9.8 reduce-scatter.4
  1771.5 307.8 all-reduce.4
where the time goes:
time: 2250 us; the launch traced here: 2230 us
  waiting for transfers between devices  631 us (28%)
  matrix products  512 us (23%)
  local copies, waits for them, and re-layouts  472 us (21%)
  blocking collectives  312 us (14%)
  other arithmetic  242 us (11%)
  starting transfers between devices  32.8 us (1%)
  between operations  28.7 us (1%)
    psum x1, waiting for transfers between devices, per_device(): summed = lax.psum(flat_grad, ('ep', 'dp'))  295 us
    unnamed x7, waiting for transfers between devices  234 us
    psum x2, blocking collectives, per_device(): loss_sum, total = lax.psum((local, jnp.sum(count_tok)), ('ep', 'dp'))  163 us
    dot_general x15, matrix products, plain(): return jnp.dot(left, right, preferred_element_type=FULLTYPE)  163 us
    all_to_all x1, blocking collectives, to_experts(): return lax.all_to_all(buffer, 'ep', split_axis=0, concat_axis=0, tiled=True)  109 us
    dynamic_update_slice x12, local copies, waits for them, and re-layouts, attend_back(): lax.map(one, (blocks(query, block), totals, blocks(grads, block)))  88.2 us
    dot_general x14, matrix products, right_t(): lax.dot_general(left, right, (((1,), (1,)), ((), ())), preferred_element_...  87.9 us
    all_to_all x1, waiting for transfers between devices, to_experts(): return lax.all_to_all(buffer, 'ep', split_axis=0, concat_axis=0, tiled=True)  76.2 us
  transfers between devices with their start and end apart: 9, of which 5 were waited for; matrix products, arithmetic and copies ran while one was open for 27% of the time, Pallas kernels for 0%

commit v1 on v0

v1 whole, which is shorter than its diff:
```python
import functools
import math

import jax
import jax.numpy as jnp
from jax import lax
from jax.experimental import pallas as pl
from jax.experimental.pallas import tpu as pltpu
from jax.sharding import PartitionSpec as P

D = 384
HEADS = 6
HD = 64
FF = 1536
TOP = 4
C = 40
PIX = 768
TASKS = 4


EPS_NORM = 1e-05
CLIP_NORM = 0.002
RATE = 0.3
DECAY_ONE = 0.5
DECAY_TWO = 0.5
WEIGHT_DECAY = 0.01
EPS_ADAM = 1e-09
AVERAGE = 0.9
SCALE = 0.125
LOWTYPE = jnp.bfloat16
FULLTYPE = jnp.float32


def plain(left, right):
    return jnp.dot(left, right, preferred_element_type=FULLTYPE)


def left_t(left, right):
    return lax.dot_general(left, right, (((0,), (0,)), ((), ())), preferred_element_type=FULLTYPE)


def right_t(left, right):
    return lax.dot_general(left, right, (((1,), (1,)), ((), ())), preferred_element_type=FULLTYPE)


def segment_sizes(experts):
    return (
        [PIX * D]
        + [3 * D * D] * 3
        + [D * D] * 3
        + [D * FF] * 2
        + [FF * D] * 2
        + [TASKS * D * experts, D * C, 14 * D]
    )


def unpack(flat, experts):
    shapes = [
        (PIX, D),
        (3, D, 3 * D),
        (3, D, D),
        (2, D, FF),
        (2, FF, D),
        (TASKS, D, experts),
        (D, C),
        (2, 7, D),
    ]
    pieces = []
    start = 0
    for shape in shapes:
        count = math.prod(shape)
        pieces.append(flat[start : start + count].reshape(shape))
        start += count
    return pieces


def segment_onehot(start, count, experts):
    index = start + jnp.arange(count, dtype=jnp.int32)
    sizes = segment_sizes(experts)
    label = jnp.zeros((count,), jnp.int32)
    edge = 0
    for size in sizes[:-1]:
        edge += size
        label = label + (index >= edge).astype(jnp.int32)
    return label[:, None] == jnp.arange(len(sizes), dtype=jnp.int32)[None, :]


def layer_norm(x, gain, bias):
    mean = jnp.mean(x, -1, keepdims=True)
    cent = x - mean
    var = jnp.mean(cent * cent, -1, keepdims=True)
    return cent * lax.rsqrt(var + EPS_NORM) * gain + bias


def norm_back(x, gain, bias, grad):
    return jax.vjp(layer_norm, x, gain, bias)[1](grad)


def gelu(hidden):
    return jax.nn.gelu(hidden, approximate=False)


VMEM_LIMIT = 56 * 2**20
ROWS = 256
NEG = -1e30


def rows_of(index, size=ROWS):
    return pl.ds(pl.multiple_of(index * size, size), size)


def norm_parts(x):
    cent = x - jnp.mean(x, -1, keepdims=True)
    scale = lax.rsqrt(jnp.mean(cent * cent, -1, keepdims=True) + EPS_NORM)
    return (cent * scale, scale)


def norm_low(x, gain, bias):
    return (norm_parts(x)[0] * gain + bias).astype(LOWTYPE)


def norm_pull(x, gain, grad):
    unit, scale = norm_parts(x)
    inner = grad * gain
    d_x = scale * (
        inner
        - jnp.mean(inner, -1, keepdims=True)
        - unit * jnp.mean(inner * unit, -1, keepdims=True)
    )
    return (d_x, jnp.sum(grad * unit, 0, keepdims=True), jnp.sum(grad, 0, keepdims=True))


def gelu_pair(h):
    z = jnp.abs(h) * 0.7071067811865476
    t = 1.0 / (1.0 + 0.3275911 * z)
    poly = t * (
        0.127414796
        + t * (-0.142248368 + t * (0.7107068705 + t * (-0.7265760135 + t * 0.5307027145)))
    )
    e = jnp.exp(-(z * z))
    tail = poly * e
    cdf = jnp.where(h < 0, tail, 1.0 - tail)
    return (h * cdf, cdf + h * (e * 0.3989422804014327))


def half_masks(scale):
    lane = lax.broadcasted_iota(jnp.int32, (1, 128), 1)
    return [jnp.where((lane < HD) == (h == 0), scale, 0.0).astype(LOWTYPE) for h in (0, 1)]


def attend_rows(qkv_ref, bias_ref, o_ref, lse_ref):
    seq = qkv_ref.shape[0]
    masks = half_masks(SCALE)
    lane = lax.broadcasted_iota(jnp.int32, (ROWS, 128), 1)

    for pair in range(HEADS // 2):
        cols = pl.ds(pair * 128, 128)

        def body(i, carry, pair=pair, cols=cols):
            rows = rows_of(i)
            query = qkv_ref[rows, cols]
            keys = qkv_ref[:, pl.ds(D + pair * 128, 128)]
            values = qkv_ref[:, pl.ds(2 * D + pair * 128, 128)]
            outs = []
            for h in (0, 1):
                s = right_t(query * masks[h], keys) + bias_ref[...]
                top = jnp.max(s, -1, keepdims=True)
                e = jnp.exp(s - top)
                total = jnp.sum(e, -1, keepdims=True)
                probs = (e * (1.0 / total)).astype(LOWTYPE)
                outs.append(plain(probs, values))
                lse = jnp.broadcast_to(top + jnp.log(total), (ROWS, 128)).T
                lse_ref[pl.ds(2 * pair + h, 1), rows] = lse[0:1, :]
            o_ref[rows, cols] = jnp.where(lane < HD, outs[0], outs[1]).astype(LOWTYPE)
            return carry

        lax.fori_loop(0, seq // ROWS, body, 0)


def forward_kernel(has_patch, has_ff, *refs):
    refs = list(refs)
    x_in = refs.pop(0)
    if has_patch:
        w_patch = refs.pop(0)
    w_qkv, w_attn, norms, bias = refs[:4]
    refs = refs[4:]
    if has_ff:
        w_up, w_down = refs[:2]
        refs = refs[2:]
    if has_patch:
        x_ref = refs.pop(0)
    else:
        x_ref = x_in
    mid_ref, c_ref, qkv_ref, o_ref, lse_ref = refs[:5]
    refs = refs[5:]
    if has_ff:
        next_ref, act_ref, slope_ref = refs
    seq = x_ref.shape[0]

    def project(i, carry):
        rows = rows_of(i)
        if has_patch:
            x_ref[rows, :] = plain(x_in[rows, :], w_patch[...])
        a16 = norm_low(x_ref[rows, :], norms[0:1, :], norms[1:2, :])
        qkv_ref[rows, :] = plain(a16, w_qkv[...]).astype(LOWTYPE)
        return carry

    lax.fori_loop(0, seq // ROWS, project, 0)
    lse_ref[...] = jnp.zeros_like(lse_ref)
    attend_rows(qkv_ref, bias, o_ref, lse_ref)

    def finish(i, carry):
        rows = rows_of(i)
        mid = x_ref[rows, :] + plain(o_ref[rows, :], w_attn[...])
        mid_ref[rows, :] = mid
        c16 = norm_low(mid, norms[2:3, :], norms[3:4, :])
        c_ref[rows, :] = c16
        if has_ff:
            act, slope = gelu_pair(plain(c16, w_up[...]))
            act16 = act.astype(LOWTYPE)
            act_ref[rows, :] = act16
            slope_ref[rows, :] = slope
            next_ref[rows, :] = mid + plain(act16, w_down[...])
        return carry

    lax.fori_loop(0, seq // ROWS, finish, 0)


def in_vmem(count):
    return [pl.BlockSpec(memory_space=pltpu.VMEM)] * count


def local_call(kernel, outs, args, flops, scratch=()):
    moved = sum(math.prod(a.shape) * a.dtype.itemsize for a in (*args, *outs))
    return pl.pallas_call(
        kernel,
        out_shape=outs,
        in_specs=in_vmem(len(args)),
        out_specs=in_vmem(len(outs)),
        scratch_shapes=scratch,
        compiler_params=pltpu.CompilerParams(vmem_limit_bytes=VMEM_LIMIT),
        cost_estimate=pl.CostEstimate(flops=flops, bytes_accessed=moved, transcendentals=0),
    )(*args)


def shaped(shape, dtype):
    return jax.ShapeDtypeStruct(shape, dtype)


def layer_forward(x, w_patch, w_qkv, w_attn, norms, bias, w_up, w_down):
    seq = x.shape[0]
    has_patch, has_ff = (w_patch is not None, w_up is not None)
    args = [x] + [w_patch] * has_patch + [w_qkv, w_attn, norms, bias] + [w_up, w_down] * has_ff
    outs = [shaped((seq, D), FULLTYPE)] * has_patch
    outs += [
        shaped((seq, D), FULLTYPE),
        shaped((seq, D), LOWTYPE),
        shaped((seq, 3 * D), LOWTYPE),
        shaped((seq, D), LOWTYPE),
        shaped((8, seq), FULLTYPE),
    ]
    if has_ff:
        outs += [
            shaped((seq, D), FULLTYPE),
            shaped((seq, FF), LOWTYPE),
            shaped((seq, FF), FULLTYPE),
        ]
    flops = 2 * seq * D * (4 * D + 4 * seq + 2 * FF * has_ff)
    return local_call(functools.partial(forward_kernel, has_patch, has_ff), outs, args, flops)


def attend_pull(qkv_ref, do_ref, lse_ref, valid_ref, dqkv_ref, dk_ref, dv_ref):
    seq = qkv_ref.shape[0]
    scaled, ones = (half_masks(SCALE), half_masks(1.0))
    lane = lax.broadcasted_iota(jnp.int32, (ROWS, 128), 1)

    for pair in range(HEADS // 2):
        cols = pl.ds(pair * 128, 128)
        dk_ref[...] = jnp.zeros_like(dk_ref)
        dv_ref[...] = jnp.zeros_like(dv_ref)

        def body(i, carry, pair=pair, cols=cols):
            rows = rows_of(i)
            query = qkv_ref[rows, cols]
            keys = qkv_ref[:, pl.ds(D + pair * 128, 128)]
            values = qkv_ref[:, pl.ds(2 * D + pair * 128, 128)]
            d_out = do_ref[rows, cols]
            d_query = []
            for h in (0, 1):
                own_q = query * scaled[h]
                own_d = d_out * ones[h]
                s = right_t(keys, own_q) + valid_ref[...]
                probs = jnp.exp(s - lse_ref[pl.ds(2 * pair + h, 1), rows])
                dv_ref[...] += plain(probs.astype(LOWTYPE), own_d)
                d_probs = right_t(values, own_d)
                delta = jnp.sum(probs * d_probs, 0, keepdims=True)
                d_s = (probs * (d_probs - delta)).astype(LOWTYPE)
                dk_ref[...] += plain(d_s, own_q)
                d_query.append(left_t(d_s, keys))
            picked = jnp.where(lane < HD, d_query[0], d_query[1]) * SCALE
            dqkv_ref[rows, cols] = picked.astype(LOWTYPE)
            return carry

        lax.fori_loop(0, seq // ROWS, body, 0)
        dqkv_ref[:, pl.ds(D + pair * 128, 128)] = dk_ref[...].astype(LOWTYPE)
        dqkv_ref[:, pl.ds(2 * D + pair * 128, 128)] = dv_ref[...].astype(LOWTYPE)


def weight_pull(left_ref, right_ref, out_ref, tile=128):
    def body(j, carry):
        cols = rows_of(j, tile)
        out_ref[cols, :] = left_t(left_ref[:, cols], right_ref[...])
        return carry

    lax.fori_loop(0, left_ref.shape[1] // tile, body, 0)


def backward_kernel(has_patch, has_ff, *refs):
    refs = list(refs)
    grad, x_ref, mid_ref, qkv, o_ref, lse, w_qkv, w_attn, norms, valid = refs[:10]
    refs = refs[10:]
    if has_ff:
        c_ref, act, slope, w_up, w_down = refs[:5]
        refs = refs[5:]
    else:
        d_c_ref = refs.pop(0)
    if has_patch:
        patches = refs.pop(0)
    d_qkvw, d_attn, d_norms = refs[:3]
    refs = refs[3:]
    if has_ff:
        d_up, d_down = refs[:2]
        refs = refs[2:]
    if has_patch:
        d_patch = refs.pop(0)
    else:
        dx_ref = refs.pop(0)
    gmid, low, do_ref, dqkv, dk, dv = refs[:6]
    refs = refs[6:]
    if has_ff:
        dh_ref = refs.pop(0)
    seq = grad.shape[0]
    blocks_count = seq // ROWS
    d_norms[...] = jnp.zeros_like(d_norms)

    def feed(i, carry):
        rows = rows_of(i)
        g = grad[rows, :]
        if has_ff:
            g16 = g.astype(LOWTYPE)
            low[rows, :] = g16
            dh16 = (right_t(g16, w_down[...]) * slope[rows, :]).astype(LOWTYPE)
            dh_ref[rows, :] = dh16
            d_c = right_t(dh16, w_up[...])
        else:
            d_c = d_c_ref[rows, :]
        d_x, d_gain, d_bias = norm_pull(mid_ref[rows, :], norms[2:3, :], d_c)
        gmid[rows, :] = g + d_x
        d_norms[2:3, :] += d_gain
        d_norms[3:4, :] += d_bias
        return carry

    lax.fori_loop(0, blocks_count, feed, 0)
    if has_ff:
        weight_pull(act, low, d_down)
        weight_pull(c_ref, dh_ref, d_up)

    def out_pull(i, carry):
        rows = rows_of(i)
        g16 = gmid[rows, :].astype(LOWTYPE)
        low[rows, :] = g16
        do_ref[rows, :] = right_t(g16, w_attn[...]).astype(LOWTYPE)
        return carry

    lax.fori_loop(0, blocks_count, out_pull, 0)
    weight_pull(o_ref, low, d_attn)
    attend_pull(qkv, do_ref, lse, valid, dqkv, dk, dv)

    def in_pull(i, carry):
        rows = rows_of(i)
        d_a = right_t(dqkv[rows, :], w_qkv[...])
        x = x_ref[rows, :]
        d_x, d_gain, d_bias = norm_pull(x, norms[0:1, :], d_a)
        total = gmid[rows, :] + d_x
        if has_patch:
            gmid[rows, :] = total
        else:
            dx_ref[rows, :] = total
        low[rows, :] = norm_low(x, norms[0:1, :], norms[1:2, :])
        d_norms[0:1, :] += d_gain
        d_norms[1:2, :] += d_bias
        return carry

    lax.fori_loop(0, blocks_count, in_pull, 0)
    weight_pull(low, dqkv, d_qkvw)
    if has_patch:

        def lower(i, carry):
            rows = rows_of(i)
            low[rows, :] = gmid[rows, :].astype(LOWTYPE)
            return carry

        lax.fori_loop(0, blocks_count, lower, 0)
        weight_pull(patches, low, d_patch)


def layer_backward(grad, x, kept, w_qkv, w_attn, norms, valid, ff, d_c, patches):
    seq = grad.shape[0]
    mid, c16, qkv16, o16, lse = kept[:5]
    has_ff, has_patch = (ff is not None, patches is not None)
    args = [grad, x, mid, qkv16, o16, lse, w_qkv, w_attn, norms, valid]
    args += [c16, *kept[5:], *ff] if has_ff else [d_c]
    args += [patches] * has_patch
    outs = [
        shaped((D, 3 * D), FULLTYPE),
        shaped((D, D), FULLTYPE),
        shaped((8, D), FULLTYPE),
    ]
    if has_ff:
        outs += [shaped((D, FF), FULLTYPE), shaped((FF, D), FULLTYPE)]
    outs += [shaped((PIX, D), FULLTYPE) if has_patch else shaped((seq, D), FULLTYPE)]
    scratch = [
        pltpu.VMEM((seq, D), FULLTYPE),
        pltpu.VMEM((seq, D), LOWTYPE),
        pltpu.VMEM((seq, D), LOWTYPE),
        pltpu.VMEM((seq, 3 * D), LOWTYPE),
        pltpu.VMEM((seq, 128), FULLTYPE),
        pltpu.VMEM((seq, 128), FULLTYPE),
    ] + [pltpu.VMEM((seq, FF), LOWTYPE)] * has_ff
    flops = 2 * seq * D * (8 * D + 10 * seq + 4 * FF * has_ff + PIX * has_patch)
    return local_call(
        functools.partial(backward_kernel, has_patch, has_ff), outs, args, flops, scratch
    )


def head_kernel(x_ref, norms, w_head, counts, count, total, loss, d_head, d_norms, grad, f_ref, dl_ref):
    seq = x_ref.shape[0]
    d_norms[...] = jnp.zeros_like(d_norms)
    loss[...] = jnp.zeros_like(loss)
    real = lax.broadcasted_iota(jnp.int32, (1, 128), 1) < C

    def body(i, carry):
        rows = rows_of(i)
        x = x_ref[rows, :]
        f16 = norm_low(x, norms[0:1, :], norms[1:2, :])
        f_ref[rows, :] = f16
        logits = plain(f16, w_head[...])
        shown = jnp.where(real, logits, NEG)
        top = jnp.max(shown, -1, keepdims=True)
        e = jnp.exp(shown - top)
        under = jnp.sum(e, -1, keepdims=True)
        weight = count[rows, :]
        classes = counts[rows, :]
        part = weight * (top + jnp.log(under)) - jnp.sum(classes * logits, -1, keepdims=True)
        loss[...] += jnp.broadcast_to(jnp.sum(part, 0, keepdims=True), loss.shape)
        d_logits = ((weight * (e * (1.0 / under)) - classes) / total[...]).astype(LOWTYPE)
        dl_ref[rows, :] = d_logits
        d_x, d_gain, d_bias = norm_pull(x, norms[0:1, :], right_t(d_logits, w_head[...]))
        grad[rows, :] = d_x
        d_norms[0:1, :] += d_gain
        d_norms[1:2, :] += d_bias
        return carry

    lax.fori_loop(0, seq // ROWS, body, 0)
    weight_pull(f_ref, dl_ref, d_head)


def head_call(x, norms, w_head, counts, count, total):
    seq = x.shape[0]
    outs = [
        shaped((1, 128), FULLTYPE),
        shaped((D, 128), FULLTYPE),
        shaped((8, D), FULLTYPE),
        shaped((seq, D), FULLTYPE),
    ]
    args = [
        x,
        norms,
        jnp.pad(w_head, ((0, 0), (0, 128 - C))),
        jnp.pad(counts, ((0, 0), (0, 128 - C))),
        count.reshape(seq, 1),
        total.reshape(1, 1),
    ]
    scratch = [pltpu.VMEM((seq, D), LOWTYPE), pltpu.VMEM((seq, 128), LOWTYPE)]
    return local_call(head_kernel, outs, args, 6 * seq * D * 128, scratch)


def feed_forward(rows16, w_up, w_back):
    hidden = plain(rows16, w_up)
    return (plain(gelu(hidden).astype(LOWTYPE), w_back), hidden)


def feed_backward(rows16, hidden, grad16, w_up, w_back):
    act16 = gelu(hidden).astype(LOWTYPE)
    d_back = left_t(act16, grad16)
    d_act = right_t(grad16, w_back)
    d_hidden = jax.vjp(gelu, hidden)[1](d_act)[0].astype(LOWTYPE)
    return (right_t(d_hidden, w_up), (left_t(rows16, d_hidden), d_back))


def make_slots(routes, experts, capacity):
    flat = routes.reshape(-1)
    seq = routes.shape[0]
    named = (routes[:, :, None] == jnp.arange(experts, dtype=jnp.int32)[None, None, :]).astype(LOWTYPE)
    earlier = jnp.arange(seq)[:, None] > jnp.arange(seq)[None, :]
    before = plain(earlier.astype(LOWTYPE), jnp.sum(named, 1))
    rank = jnp.sum(before[:, None, :] * named, 2).astype(jnp.int32).reshape(-1)
    slot = flat * capacity + rank
    assign = (
        jnp.zeros((experts * capacity,), jnp.int32)
        .at[slot]
        .set(jnp.arange(flat.shape[0], dtype=jnp.int32))
    )
    used = jnp.zeros((experts * capacity,), jnp.int32).at[slot].set(1)
    return (slot, assign, used)


def swap_dp(value):
    return lax.ppermute(value, "dp", [(0, 1), (1, 0)])


def join_dp(value, place):
    groups = lax.axis_size("dp")
    if groups != 2:
        return lax.all_gather(value, "dp")
    other = swap_dp(value)
    first = place == 0
    return jnp.stack([jnp.where(first, value, other), jnp.where(first, other, value)])


def sum_scatter_dp(parts, place):
    groups = lax.axis_size("dp")
    if groups != 2:
        return lax.psum_scatter(parts, "dp", scatter_dimension=0, tiled=True)[0]
    first = place == 0
    mine = jnp.where(first, parts[0], parts[1])
    return mine + swap_dp(jnp.where(first, parts[1], parts[0]))


def sum_all(value):
    for axis in ("dp", "ep"):
        count = lax.axis_size(axis)
        step = 1
        while step < count:
            value = value + lax.ppermute(value, axis, [(i, i ^ step) for i in range(count)])
            step *= 2
    return value


def to_experts(buffer):
    return lax.all_to_all(buffer, "ep", split_axis=0, concat_axis=0, tiled=True)


def from_experts(buffer):
    return lax.all_to_all(
        buffer.astype(jnp.bfloat16), "ep", split_axis=0, concat_axis=0, tiled=True
    ).astype(buffer.dtype)


def per_device(
    patches,
    labels,
    pixel_mask,
    patch_valid,
    tasks,
    routes,
    dense_weight,
    dense_first,
    dense_second,
    dense_average,
    expert_in,
    in_first,
    in_second,
    in_average,
    expert_out,
    out_first,
    out_second,
    out_average,
):
    ep_count = lax.axis_size("ep")
    experts = min(16, ep_count)
    copies = ep_count // experts
    groups = lax.axis_size("dp")
    ep_place = lax.axis_index("ep")
    dp_place = lax.axis_index("dp")
    own_expert = ep_place // copies
    seq = patches.shape[0]
    capacity = 3 * seq * TOP // (2 * experts)
    shard = dense_weight.shape[0]
    part_rows = -(-shard // (groups * 1024)) * 8
    padded = part_rows * 128 * groups
    low_parts = jnp.pad(dense_weight.astype(LOWTYPE), (0, padded - shard)).reshape(
        groups, part_rows, 128
    )
    own_part = lax.dynamic_index_in_dim(low_parts, dp_place, 0, keepdims=False)
    parts = join_dp(lax.all_gather(own_part, "ep"), dp_place)
    gathered = jnp.swapaxes(parts, 0, 1).reshape(ep_count, padded)[:, :shard].reshape(-1)
    w_patch, w_qkv, w_attn, w_up, w_down, w_router, w_head, norms16 = unpack(gathered, experts)
    norms = norms16.astype(FULLTYPE)
    own_in, own_out = (
        lax.all_gather(expert_in.astype(LOWTYPE), "dp", axis=2, tiled=True),
        lax.all_gather(expert_out.astype(LOWTYPE), "dp", axis=1, tiled=True),
    )
    own_in = own_in[0]
    own_out = own_out[0]
    task = tasks[0]
    router = lax.dynamic_index_in_dim(w_router, task, 0, keepdims=False)
    slot, assign, used = make_slots(routes, experts, capacity)
    route_hot = (routes[:, :, None] == jnp.arange(experts, dtype=jnp.int32)[None, None, :]).astype(
        FULLTYPE
    )

    def dispatch(send):
        buffer = jnp.repeat(send.reshape(experts, capacity, D), copies, axis=0)
        return to_experts(buffer)

    def combine(partial_value):
        back = from_experts(partial_value).reshape(experts, copies, capacity, D)
        summed = jnp.sum(back, 1).astype(LOWTYPE).reshape(experts * capacity, D)
        return summed[slot].reshape(seq, TOP, D).astype(FULLTYPE)

    def expert_backward(arrived, rows, hidden):
        d_rows, (d_in, d_out) = feed_backward(rows, hidden, arrived.reshape(-1, D), own_in, own_out)
        d_in_own, d_out_own = (
            lax.psum_scatter(
                d_in[None].astype(jnp.bfloat16), "dp", scatter_dimension=2, tiled=True
            ).astype(jnp.float32),
            lax.psum_scatter(
                d_out[None].astype(jnp.bfloat16), "dp", scatter_dimension=1, tiled=True
            ).astype(jnp.float32),
        )
        return (d_rows.reshape(arrived.shape), d_in_own, d_out_own)

    def norm_rows(layer):
        rows = [norms[0, 2 * layer], norms[1, 2 * layer]]
        if layer < 3:
            rows += [norms[0, 2 * layer + 1], norms[1, 2 * layer + 1]]
        return jnp.pad(jnp.stack(rows), ((0, 8 - len(rows)), (0, 0)))

    bias = jnp.where(patch_valid > 0, 0.0, NEG).astype(FULLTYPE)
    across, down = (bias.reshape(1, seq), bias.reshape(seq, 1))
    weight_pix = (pixel_mask * patch_valid[:, None]).astype(FULLTYPE)
    count_tok = jnp.sum(weight_pix, 1)
    class_hot = labels[:, :, None] == jnp.arange(C, dtype=jnp.int32)[None, None, :]
    counts = jnp.sum(jnp.where(class_hot, weight_pix[:, :, None], 0.0), 1)
    total = sum_all(jnp.sum(count_tok).reshape(1))[0]

    x0, *kept0, x1, act0, slope0 = layer_forward(
        patches, w_patch, w_qkv[0], w_attn[0], norm_rows(0), across, w_up[0], w_down[0]
    )
    mid1, c16, *kept1 = layer_forward(
        x1, None, w_qkv[1], w_attn[1], norm_rows(1), across, None, None
    )
    logits = plain(c16, router)
    gates = jax.nn.softmax(jnp.sum(route_hot * logits[:, None, :], -1), -1)
    send = jnp.where(used[:, None] > 0, c16[assign // TOP], jnp.zeros((), LOWTYPE))
    arrived = dispatch(send)
    rows = arrived.reshape(-1, D)
    out, hidden = feed_forward(rows, own_in, own_out)
    picks = combine(out.reshape(arrived.shape))
    x2 = mid1 + jnp.sum(gates[:, :, None] * picks, 1)
    *kept2, x3, act2, slope2 = layer_forward(
        x2, None, w_qkv[2], w_attn[2], norm_rows(2), across, w_up[1], w_down[1]
    )
    loss_lanes, d_head, d_normf, grad = head_call(
        x3, norm_rows(3), w_head, counts, count_tok, total
    )
    local = loss_lanes[0, 0]
    d_qkv2, d_attn2, d_norm2, d_up1, d_down1, grad = layer_backward(
        grad, x2, (*kept2, act2, slope2), w_qkv[2], w_attn[2], norm_rows(2), down,
        (w_up[1], w_down[1]), None, None,
    )
    d_gates = jnp.sum(grad[:, None, :] * picks, -1)
    d_picked = gates * (d_gates - jnp.sum(gates * d_gates, -1, keepdims=True))
    d_logits = jnp.sum(route_hot * d_picked[:, :, None], 1).astype(LOWTYPE)
    task_hot = (jnp.arange(TASKS, dtype=jnp.int32) == task)[:, None, None]
    d_router = jnp.where(task_hot, left_t(c16, d_logits)[None], 0.0)
    d_picks = (gates[:, :, None] * grad[:, None, :]).astype(LOWTYPE).reshape(seq * TOP, D)
    send = jnp.where(used[:, None] > 0, d_picks[assign], jnp.zeros((), LOWTYPE))
    d_rows, d_in, d_out = expert_backward(dispatch(send), rows, hidden)
    d_c = right_t(d_logits, router) + jnp.sum(combine(d_rows), 1)
    d_qkv1, d_attn1, d_norm1, grad = layer_backward(
        grad, x1, (mid1, c16, *kept1), w_qkv[1], w_attn[1], norm_rows(1), down, None, d_c, None
    )
    d_qkv0, d_attn0, d_norm0, d_up0, d_down0, d_patch = layer_backward(
        grad, x0, (*kept0, act0, slope0), w_qkv[0], w_attn[0], norm_rows(0), down,
        (w_up[0], w_down[0]), None, patches,
    )
    d_head = d_head[:, :C]
    each = [d_norm0, d_norm1, d_norm2]
    gain_list = [n[k] for n in each for k in (0, 2)] + [d_normf[0]]
    bias_list = [n[k] for n in each for k in (1, 3)] + [d_normf[1]]
    d_qkv_list = [d_qkv0, d_qkv1, d_qkv2]
    d_attn_list = [d_attn0, d_attn1, d_attn2]
    d_up_list = [d_up0, d_up1]
    d_down_list = [d_down0, d_down1]
    d_norms = jnp.stack([jnp.stack(gain_list), jnp.stack(bias_list)])
    listed = [
        d_patch,
        jnp.stack(d_qkv_list),
        jnp.stack(d_attn_list),
        jnp.stack(d_up_list),
        jnp.stack(d_down_list),
        d_router,
        d_head,
        d_norms,
    ]
    flat_grad = jnp.concatenate([piece.reshape(-1) for piece in listed])
    by_owner = jnp.pad(flat_grad.reshape(ep_count, shard), ((0, 0), (0, padded - shard)))
    by_part = jnp.swapaxes(by_owner.reshape(ep_count, groups, part_rows, 128), 0, 1)
    own_sum = lax.psum_scatter(
        sum_scatter_dp(by_part, dp_place), "ep", scatter_dimension=0, tiled=True
    )[0]
    dense_grad = join_dp(own_sum, dp_place).reshape(padded)[:shard]
    piece = shard // groups
    part_hot = segment_onehot(ep_place * shard + dp_place * piece, piece, experts)
    expert_hot = (jnp.arange(experts, dtype=jnp.int32) == own_expert).astype(FULLTYPE)

    def block_sums(dense_vals, in_vals, out_vals):
        part = lax.dynamic_slice_in_dim(dense_vals, dp_place * piece, piece)
        dense_part = jnp.sum(jnp.where(part_hot, (part * part)[:, None], 0.0), 0)
        return jnp.concatenate(
            [
                dense_part,
                expert_hot * jnp.sum(in_vals * in_vals),
                expert_hot * jnp.sum(out_vals * out_vals),
            ]
        )

    sums = sum_all(
        jnp.concatenate(
            [
                local.reshape(1),
                jnp.sum(block_sums(dense_grad, d_in, d_out)).reshape(1),
                block_sums(dense_weight, expert_in, expert_out),
            ]
        )
    )
    loss, grad_total, weight_total = (sums[0] / total, sums[1], sums[2:])
    grad_norm = jnp.sqrt(grad_total)
    clip = CLIP_NORM / jnp.maximum(grad_norm, CLIP_NORM)

    def moments(weight, first, second, gradient):
        gradient = gradient * clip
        first_new = DECAY_ONE * first + (1.0 - DECAY_ONE) * gradient
        second_new = DECAY_TWO * second + (1.0 - DECAY_TWO) * gradient * gradient
        return (
            first_new,
            second_new,
            first_new / (jnp.sqrt(second_new) + EPS_ADAM) + WEIGHT_DECAY * weight,
        )

    dense_m, dense_v, dense_step = moments(dense_weight, dense_first, dense_second, dense_grad)
    in_m, in_v, in_step = moments(expert_in, in_first, in_second, d_in)
    out_m, out_v, out_step = moments(expert_out, out_first, out_second, d_out)
    update_total = sum_all(block_sums(dense_step, in_step, out_step))
    weight_norm = jnp.sqrt(weight_total)
    update_norm = jnp.sqrt(update_total)
    ratio = weight_norm / (update_norm + EPS_NORM)
    whole_hot = segment_onehot(ep_place * shard, shard, experts)
    dense_ratio = jnp.sum(jnp.where(whole_hot, ratio[None, :14], 0.0), 1)
    in_ratio = lax.dynamic_index_in_dim(ratio, 14 + own_expert, 0, keepdims=False)
    out_ratio = lax.dynamic_index_in_dim(ratio, 14 + experts + own_expert, 0, keepdims=False)

    def finish(weight, average, step, rate):
        new = weight - RATE * rate * step
        return (new, AVERAGE * average + (1.0 - AVERAGE) * new, new.astype(LOWTYPE))

    dense_new, dense_avg, dense_low = finish(dense_weight, dense_average, dense_step, dense_ratio)
    in_new, in_avg, in_low = finish(expert_in, in_average, in_step, in_ratio)
    out_new, out_avg, out_low = finish(expert_out, out_average, out_step, out_ratio)
    block_norms = jnp.stack([weight_norm, update_norm], 1)
    return (
        loss.reshape(1),
        grad_norm.reshape(1),
        block_norms,
        dense_new,
        dense_m,
        dense_v,
        dense_avg,
        dense_low,
        in_new,
        in_m,
        in_v,
        in_avg,
        in_low,
        out_new,
        out_m,
        out_v,
        out_avg,
        out_low,
    )


def solution(mesh):
    in_specs = (
        P(("ep", "dp"), None),
        P(("ep", "dp"), None),
        P(("ep", "dp"), None),
        P(("ep", "dp")),
        P(("ep", "dp")),
        P(("ep", "dp"), None),
        P("ep"),
        P("ep"),
        P("ep"),
        P("ep"),
        P("ep", None, "dp"),
        P("ep", None, "dp"),
        P("ep", None, "dp"),
        P("ep", None, "dp"),
        P("ep", "dp", None),
        P("ep", "dp", None),
        P("ep", "dp", None),
        P("ep", "dp", None),
    )
    out_specs = (
        P(),
        P(),
        P(),
        P("ep"),
        P("ep"),
        P("ep"),
        P("ep"),
        P("ep"),
        P("ep", None, "dp"),
        P("ep", None, "dp"),
        P("ep", None, "dp"),
        P("ep", None, "dp"),
        P("ep", None, "dp"),
        P("ep", "dp", None),
        P("ep", "dp", None),
        P("ep", "dp", None),
        P("ep", "dp", None),
        P("ep", "dp", None),
    )
    return jax.shard_map(
        per_device, mesh=mesh, in_specs=in_specs, out_specs=out_specs, check_vma=False
    )
```

time: 2250 us -> 1690 us (0.75)
  matrix products: 512 us -> 189 us
  Pallas kernels: 0 us -> 262 us
  blocking collectives: 312 us -> 110 us
  local copies, waits for them, and re-layouts: 472 us -> 303 us
  waiting for transfers between devices: 631 us -> 502 us
  starting transfers between devices: 32.8 us -> 107 us
  other arithmetic: 242 us -> 183 us
    psum x1 -> x0, waiting for transfers between devices: 295 us -> none  [per_device(): summed = lax.psum(flat_grad, ('ep', 'dp'))]
    pallas_call x0 -> x7, Pallas kernels: none -> 262 us  [local_call(): pl.pallas_call(kernel, out_shape=outs, in_specs=in_vmem(len(args)), out_s...]
    psum x3 -> x0, blocking collectives: 203 us -> none  [the longest x2 163 us: per_device(): loss_sum, total = lax.psum((local, jnp.sum(count_tok)), ('ep', 'dp'))]
    dot_general x42 -> x0, matrix products: 193 us -> none  [the longest x6 51.4 us: one(): jnp.einsum('hqk,qhd->khd', probs.astype(LOWTYPE), grad_block, preferred_e...]
    dynamic_update_slice x12 -> x0, local copies, waits for them, and re-layouts: 88.2 us -> none  [attend_back(): lax.map(one, (blocks(query, block), totals, blocks(grads, block)))]
    all_gather x0 -> x1, waiting for transfers between devices: none -> 83 us  [per_device(): parts = join_dp(lax.all_gather(own_part, 'ep'), dp_place)]
    ppermute x0 -> x18, starting transfers between devices: none -> 74.3 us  [the longest x15 74.3 us: sum_all(): lax.ppermute(value, axis, [(i, i ^ step) for i in range(count)])]
    all_to_all x2, waiting for transfers between devices: 15.7 us -> 78.6 us  [from_experts(): lax.all_to_all(buffer.astype(jnp.bfloat16), 'ep', split_axis=0, concat_ax...]
  transfers between devices with their start and end apart: 9 -> 27, of which waited for: 5 -> 21; matrix products, arithmetic and copies ran while one was open for 27% -> 10% of each run, Pallas kernels for 0% -> 0%
where the time goes in v1:
time: 1690 us; the launch traced here: 1680 us
  waiting for transfers between devices  502 us (30%)
  local copies, waits for them, and re-layouts  303 us (18%)
  Pallas kernels  262 us (16%)
  matrix products  189 us (11%)
  other arithmetic  183 us (11%)
  blocking collectives  110 us (7%)
  starting transfers between devices  107 us (6%)
  between operations  27.5 us (2%)
    pallas_call x7, Pallas kernels, local_call(): pl.pallas_call(kernel, out_shape=outs, in_specs=in_vmem(len(args)), out_s...  262 us
    unnamed x7, waiting for transfers between devices  175 us
    all_to_all x1, blocking collectives, to_experts(): return lax.all_to_all(buffer, 'ep', split_axis=0, concat_axis=0, tiled=True)  110 us
    dot_general x4, matrix products, plain(): return jnp.dot(left, right, preferred_element_type=FULLTYPE)  106 us
    all_gather x1, waiting for transfers between devices, per_device(): parts = join_dp(lax.all_gather(own_part, 'ep'), dp_place)  83 us
    all_to_all x2, waiting for transfers between devices, from_experts(): lax.all_to_all(buffer.astype(jnp.bfloat16), 'ep', split_axis=0, concat_ax...  78.6 us
    all_to_all x1, waiting for transfers between devices, to_experts(): return lax.all_to_all(buffer, 'ep', split_axis=0, concat_axis=0, tiled=True)  78 us
    ppermute x15, starting transfers between devices, sum_all(): lax.ppermute(value, axis, [(i, i ^ step) for i in range(count)])  74.3 us
  transfers between devices with their start and end apart: 27, of which 21 were waited for; matrix products, arithmetic and copies ran while one was open for 10% of the time, Pallas kernels for 0%

profile of v1, /device:TPU:0, one launch (start us, length us, event | category | flops | bytes accessed | tf_op | source)
XLA Modules:
  0.0 1682.9 jit_solution(13092122869848948732)
XLA Ops:
  10.2 83.0 %all-gather.4.cloned.1.call-done = bf16[16,1096,128]{2,1,0:T(8,128)(2,1)} async-done(((bf16[1,1096,128]{2,1,0:T(8,128)(2,1)}), bf16[16,1096,128]{2,1,0:T(8,128)(2,1)}) %all-gather.4.cloned.1.call-update) | async-done | bytes 4489232 | tf_op jit(solution)/shard_map/all_gather | solution.py:596
  101.1 7.7 select_bitcast_fusion.2
  108.8 8.0 maximum_bitcast_fusion
  116.8 7.6 copy.95
  124.4 13.3 copy.115
  141.7 20.2 %reshape.529 = bf16[4468992]{0:T(1024)(128)(2,1)} reshape(bf16[16,279312]{1,0:T(8,128)(2,1)} %slice.273) | data formatting | bytes 17875968
  162.6 14.5 slice.213
  197.4 37.3 %shard_map.313 = (f32[1024,384]{1,0:T(8,128)}, f32[1024,384]{1,0:T(8,128)}, bf16[1024,384]{1,0:T(8,128)(2,1)}, bf16[1024,1152]{1,0:T(8,128)(2,1)}, bf16[1024,384...) custom-call(bf16[1024,768]{1,0:T(8,128)(2,1)} %refs_15_.1, ...), custom_call_target="tpu_custom_call" | custom-call | flops 6845104128 | bytes 23838720 | tf_op jit(solution)/shard_map/pallas_call | solution.py:235
  234.7 25.1 %shard_map.314 = (f32[1024,384]{1,0:T(8,128)}, bf16[1024,384]{1,0:T(8,128)(2,1)}, bf16[1024,1152]{1,0:T(8,128)(2,1)}, bf16[1024,384]{1,0:T(8,128)(2,1)}, f32[8,1024]{1,0:T(8,128)}) custom-call(f32[1024,384]{1,0:T(8,128)} %get-tuple-element.60.refs_0_.refs_1_, bf16[384,1152]{1,0:T(8,128)(2,1)} %squeeze.28.refs_1_.refs_6_, ...), custom_call_target="tpu_custom_call" | custom-call | flops 4429185024 | bytes 8306688 | tf_op jit(solution)/shard_map/pallas_call | solution.py:235
  262.7 15.5 scatter_custom_fusion.1
  278.9 25.1 %gather_fusion = bf16[6144,384]{1,0:T(8,128)(2,1)} fusion(bf16[1024,384]{1,0:T(8,128)(2,1)S(1)} %copy-done, s32[6144]{0:T(1024)S(1)} %get-tuple-element.145), kind=kCustom, calls=%fused_computation | custom fusion | bytes 9461760 | tf_op jit(solution)/shard_map/gather | solution.py:656
  303.9 15.5 scatter_custom_fusion
  334.2 9.5 all-gather.6.cloned.1.call-done
  343.7 78.0 %all-to-all-done = bf16[16,384,384]{2,1,0:T(8,128)(2,1)} async-done(((bf16[16,384,384]{2,1,0:T(8,128)(2,1)}), bf16[16,384,384]{2,1,0:T(8,128)(2,1)}, u32[]{:S(2)}, u32[]{:S(2)}) %all-to-all-start) | async-done | bytes 4718624 | tf_op jit(solution)/shard_map/all_to_all | solution.py:551
  421.7 88.6 %multiply_convert_fusion = (bf16[6144,1536]{1,0:T(8,128)(2,1)}, f32[6144,1536]{1,0:T(8,128)}, f32[6144,1536]{1,0:T(8,128)}) fusion(bf16[6144,384]{1,0:T(8,128)(2,1)} %bitcast.17, bf16[1,384,1536]{2,1,0:T(8,128)(2,1)} %all-gather.6.cloned.1.call-done), kind=kOutput, calls=%fused_computation.11 | convolution fusion | flops 7861174272 | bytes 100270080 | tf_op jit(solution)/shard_map/dot_general | solution.py:35
  510.3 15.6 convolution_convert_fusion.1
  525.9 23.0 %all-to-all-start.1 = ((bf16[16,384,384]{2,1,0:T(8,128)(2,1)}), bf16[16,384,384]{2,1,0:T(8,128)(2,1)}, u32[]{:S(2)}, u32[]{:S(2)}) async-start(bf16[16,384,384]{2,1,0:T(8,128)(2,1)} %convolution_convert_fusion.1), calls=%async_computation.1 | async-start | bytes 9437184 | tf_op jit(solution)/shard_map/all_to_all | solution.py:555
  553.3 15.1 select_reduce_fusion
  578.9 46.8 %collective-permute-start.4 = (f32[1]{0:T(128)}, f32[1]{0:T(128)}, u32[]{:S(2)}, u32[]{:S(2)}) collective-permute-start(f32[1]{0:T(128)} %add.401), channel_id=1, source_target_pairs={{0,8},{2,10},{4,12},{6,14},{8,0},{10,2},{12,4},{14,6},{16,24},{18,... | collective-permute-start | bytes 20 | tf_op jit(solution)/shard_map/ppermute | solution.py:545
  630.9 21.8 %collective-permute-done.5 = f32[1]{0:T(128)} collective-permute-done((f32[1]{0:T(128)}, f32[1]{0:T(128)}, u32[]{:S(2)}, u32[]{:S(2)}) %collective-permute-start.5) | collective-permute-done | bytes 36 | tf_op jit(solution)/shard_map/ppermute | solution.py:545
  660.6 17.0 %gather_fusion.1 = bf16[4096,384]{1,0:T(8,128)(2,1)S(1)} fusion(bf16[6144,384]{1,0:T(8,128)(2,1)} %bitcast.22, s32[4096]{0:T(1024)S(1)} %broadcast_clamp_fusion), kind=kCustom, calls=%fused_computation.1 | custom fusion | bytes 6307840 | tf_op jit(solution)/shard_map/gather | solution.py:620
  681.2 18.1 %multiply_reduce_fusion.1 = f32[1024,384]{1,0:T(8,128)S(1)} fusion(f32[1024,4,384]{2,1,0:T(4,128)} %reshape.470, f32[1024,4]{1,0:T(8,128)} %copy-done.12), kind=kLoop, calls=%fused_computation.40 | loop fusion | flops 2752512 | bytes 7880704 | tf_op jit(solution)/shard_map/reduce_sum | solution.py:661
  700.7 35.9 %shard_map.315 = (f32[1024,384]{1,0:T(8,128)}, bf16[1024,384]{1,0:T(8,128)(2,1)}, bf16[1024,1152]{1,0:T(8,128)(2,1)}, bf16[1024,384]{1,0:T(8,128)(2,1)}, f32[8,1...) custom-call(f32[1024,384]{1,0:T(8,128)} %add.398.refs_0_.refs_1_, ...), custom_call_target="tpu_custom_call" | custom-call | flops 6845104128 | bytes 21676032 | tf_op jit(solution)/shard_map/pallas_call | solution.py:235
  736.5 6.9 shard_map.316
  743.4 56.1 %shard_map.317 = (f32[384,1152]{1,0:T(8,128)}, f32[384,384]{1,0:T(8,128)}, f32[8,384]{1,0:T(8,128)}, f32[384,1536]{1,0:T(8,128)}, f32[1536,384]{1,0:T(8,128)}, /*index=5*/f32[1024,384]{1,0:T(8,128)}) custom-call(f32[1024,384]{1,0:T(8,128)} %get-tuple-element.65.refs_0_, f32[1024,384]{1,0:T(8,128)} %add.398.refs_0_.refs_1_, ...), custom_call_target="tpu_custom_call" | custom-call | flops 15300820992 | bytes 30339072 | tf_op jit(solution)/shard_map/pallas_call | solution.py:235
  804.7 7.7 mul.364
  815.6 25.1 %gather_fusion.2 = bf16[6144,384]{1,0:T(8,128)(2,1)} fusion(bf16[4096,384]{1,0:T(8,128)(2,1)S(1)} %multiply_convert_fusion.1, s32[6144]{0:T(1024)S(1)} %copy-done.43), kind=kCustom, calls=%fused_computation.2 | custom fusion | bytes 9461760 | tf_op jit(solution)/shard_map/gather | solution.py:679
  844.4 110.0 %all_to_all.20 = bf16[16,384,384]{2,1,0:T(8,128)(2,1)} all-to-all(bf16[16,384,384]{2,1,0:T(8,128)(2,1)S(1)} %broadcast_select_fusion), channel_id=1, replica_groups=mesh['ep'=16,'dp'=2] {'ep'}, dimensions={0} | all-to-all | bytes 9437184 | tf_op jit(solution)/shard_map/all_to_all | solution.py:551
  954.4 34.4 %add_convert_fusion = bf16[6144,1536]{1,0:T(8,128)(2,1)} fusion(f32[6144,1536]{1,0:T(8,128)} %get-tuple-element.125, f32[6144,1536]{1,0:T(8,128)} %get-tuple-element.181, bf16[6144,384]{1,0:T(8,128)(2,1)} %bitcast.164, bf16[1,1536,384]{2,1,0:T(8,128)(2,1)S(1)} %copy-done.57), kind=kOutput, calls=%fused_computation.10 | convolution fusion | flops 7379877888 | bytes 100270080 | tf_op jit(solution)/shard_map/dot_general | solution.py:43
  988.8 15.3 convolution_convert_fusion
  1017.0 78.6 %all-to-all-done.3 = bf16[16,384,384]{2,1,0:T(8,128)(2,1)} async-done(((bf16[16,384,384]{2,1,0:T(8,128)(2,1)}), bf16[16,384,384]{2,1,0:T(8,128)(2,1)}, u32[]{:S(2)}, u32[]{:S(2)}) %all-to-all-start.3) | async-done | bytes 4718624 | tf_op jit(solution)/shard_map/all_to_all | solution.py:555
  1095.6 17.5 %gather_fusion.3 = bf16[4096,384]{1,0:T(8,128)(2,1)S(1)} fusion(bf16[6144,384]{1,0:T(8,128)(2,1)} %bitcast.38, s32[4096]{0:T(1024)S(1)} %broadcast_clamp_fusion), kind=kCustom, calls=%fused_computation.3 | custom fusion | bytes 6307840 | tf_op jit(solution)/shard_map/gather | solution.py:620
  1116.7 6.5 reduce_sum.240
  1125.7 42.3 %shard_map.318 = (f32[384,1152]{1,0:T(8,128)}, f32[384,384]{1,0:T(8,128)}, f32[8,384]{1,0:T(8,128)}, f32[1024,384]{1,0:T(8,128)}) custom-call(f32[1024,384]{1,0:T(8,128)} %get-tuple-element.73.refs_0_, f32[1024,384]{1,0:T(8,128)} %get-tuple-element.60.refs_0_.refs_1_, f32[1024,384]{1,0:T(8,128)} %get-tuple-element.61.refs_2_, ...), custom_call_target="tpu_custom_call" | custom-call | flops 10468982784 | bytes 14610432 | tf_op jit(solution)/shard_map/pallas_call | solution.py:235
  1168.0 58.7 %shard_map.319 = (f32[384,1152]{1,0:T(8,128)}, f32[384,384]{1,0:T(8,128)}, f32[8,384]{1,0:T(8,128)}, f32[384,1536]{1,0:T(8,128)}, f32[1536,384]{1,0:T(8,128)}, /*index=5*/f32[768,384]{1,0:T(8,128)}) custom-call(f32[1024,384]{1,0:T(8,128)} %get-tuple-element.77.refs_0_, f32[1024,384]{1,0:T(8,128)} %get-tuple-element.78.refs_1_, ...), custom_call_target="tpu_custom_call" | custom-call | flops 15904800768 | bytes 31518720 | tf_op jit(solution)/shard_map/pallas_call | solution.py:235
  1253.7 6.6 reshape.459
  1276.4 22.1 %reshape.465 = f32[16,279312]{1,0:T(8,128)} reshape(f32[4468992]{0:T(1024)} %constant_dynamic-update-slice_fusion) | data formatting | bytes 35751936 | tf_op jit(solution)/shard_map/reshape | solution.py:709
  1298.5 7.0 pad_bitcast_fusion
  1305.6 7.9 copy.113
  1313.5 10.6 select_bitcast_fusion
  1324.1 14.2 collective-permute-done.6
  1338.3 10.7 fusion.7
  1349.1 14.0 fusion.9
  1363.4 16.0 fusion.10
  1379.4 175.3 %reduce-scatter.11.cloned.1.call-done = f32[1,1096,128]{2,1,0:T(8,128)} async-done(((f32[16,1096,128]{2,1,0:T(8,128)}), f32[1,1096,128]{2,1,0:T(8,128)}) %reduce-scatter.11.cloned.1.call-update) | async-done | bytes 561168
  1556.9 12.1 reduce-scatter.7.cloned.1.call-done
  1572.2 9.3 reduce-scatter.9.cloned.1.call-done
  1645.8 17.9 %select_reduce_fusion.1 = f32[279312]{0:T(1024)S(1)} fusion(f32[14]{0:T(128)S(1)} %bitcast.189, s32[279312]{0:T(1024)} %convert_add_fusion), kind=kLoop, calls=%fused_computation.26 | loop fusion | flops 11451792 | bytes 2234552 | tf_op jit(solution)/shard_map/reduce_sum | solution.py:761
  (312 shorter events, 230.5 us)
Async XLA Ops:
  8.0 85.1 %all-gather.4.cloned.1.call-start = ((), (), s32[]{:S(2)}) async-start(), calls=%async_computation.7 | async-start | bytes 4769792 | tf_op jit(solution)/shard_map/all_gather | solution.py:596
  93.1 7.9 collective-permute-start
  196.1 63.7 %copy-start.33 = (bf16[4,384,16]{2,1,0:T(8,128)(2,1)}, bf16[4,384,16]{2,1,0:T(8,128)(2,1)S(1)}, u32[]{:S(2)}) copy-start(bf16[4,384,16]{2,1,0:T(8,128)(2,1)S(1)} %reshape.451) | copy-start | bytes 147460
  234.7 26.6 %copy-start.39 = (s32[1024,4]{0,1:T(4,128)S(1)}, s32[1024,4]{0,1:T(4,128)}, u32[]{:S(2)}) copy-start(s32[1024,4]{0,1:T(4,128)} %param.23) | copy-start | bytes 49156
  259.8 19.1 %copy-start = (bf16[1024,384]{1,0:T(8,128)(2,1)S(1)}, bf16[1024,384]{1,0:T(8,128)(2,1)}, u32[]{:S(2)}) copy-start(bf16[1024,384]{1,0:T(8,128)(2,1)} %get-tuple-element.62) | copy-start | bytes 2359300
  262.7 41.3 %copy-start.45 = (s32[4096,1]{0,1:T(1,128)}, s32[4096,1]{0,1:T(1,128)S(1)}, u32[]{:S(2)}) copy-start(s32[4096,1]{0,1:T(1,128)S(1)} %compare_select_fusion) | copy-start | bytes 49156
  326.0 95.7 %all-to-all-start = ((bf16[16,384,384]{2,1,0:T(8,128)(2,1)}), bf16[16,384,384]{2,1,0:T(8,128)(2,1)}, u32[]{:S(2)}, u32[]{:S(2)}) async-start(bf16[16,384,384]{2,1,0:T(8,128)(2,1)} %broadcast_select_fusion.1), calls=%async_computation | async-start | bytes 9437184 | tf_op jit(solution)/shard_map/all_to_all | solution.py:551
  330.7 12.9 all-gather.6.cloned.1.call-start
  332.5 177.8 %all-gather.8.cloned.1.call-start = ((), (), s32[]{:S(2)}) async-start(), calls=%async_computation.9 | async-start | bytes 1769472 | tf_op jit(solution)/shard_map/all_gather | solution.py:602
  525.9 23.0 %copy-start.49 = (s32[1024]{0:T(1024)S(1)}, s32[1024]{0:T(1024)}, u32[]{:S(2)}) copy-start(s32[1024]{0:T(1024)} %param.21) | copy-start | bytes 12292
  525.9 26.3 %copy-start.50 = (f32[1024]{0:T(1024)S(1)}, f32[1024]{0:T(1024)}, u32[]{:S(2)}) copy-start(f32[1024]{0:T(1024)} %compare_select_fusion.2) | copy-start | bytes 12292
  525.9 134.7 %all-to-all-start.1 = ((bf16[16,384,384]{2,1,0:T(8,128)(2,1)}), bf16[16,384,384]{2,1,0:T(8,128)(2,1)}, u32[]{:S(2)}, u32[]{:S(2)}) async-start(bf16[16,384,384]{2,1,0:T(8,128)(2,1)} %convolution_convert_fusion.1), calls=%async_computation.1 | async-start | bytes 9437184 | tf_op jit(solution)/shard_map/all_to_all | solution.py:555
  548.8 104.5 %copy-start.37 = (f32[1024,4]{0,1:T(4,128)S(1)}, f32[1024,4]{0,1:T(4,128)}, u32[]{:S(2)}) copy-start(f32[1024,4]{0,1:T(4,128)} %get-tuple-element.106) | copy-start | bytes 49156
  548.9 107.8 %copy-start.15 = (bf16[589824]{0:T(1024)(128)(2,1)S(1)}, bf16[589824]{0:T(1024)(128)(2,1)}, u32[]{:S(2)}) copy-start(bf16[589824]{0:T(1024)(128)(2,1)} %get-tuple-element.130) | copy-start | bytes 3538948
  551.2 18.0 %collective-permute-start.1 = (f32[1]{0:T(128)}, f32[1]{0:T(128)}, u32[]{:S(2)}, u32[]{:S(2)}) collective-permute-start(f32[1]{0:T(128)} %bitcast.30), channel_id=1, source_target_pairs={{0,1},{1,0},{2,3},{3,2},{4,5},{5,4},{6,7},{7,6},{8,9},{9,8},{10,11... | collective-permute-start | bytes 20 | tf_op jit(solution)/shard_map/ppermute | solution.py:545
  553.3 105.6 %slice-start.1 = ((bf16[4468992]{0:T(1024)(128)(2,1)}), bf16[15360]{0:T(1024)(128)(2,1)S(1)}, s32[]{:S(2)}) async-start(bf16[4468992]{0:T(1024)(128)(2,1)} %reshape.529), calls=%async_computation.14 | async-start | bytes 61440 | tf_op jit(solution)/shard_map/slice | solution.py:72
  553.3 106.7 %copy-start.51 = (f32[1,384]{1,0:T(1,128)S(1)}, f32[1,384]{1,0:T(1,128)}, u32[]{:S(2)}) copy-start(f32[1,384]{1,0:T(1,128)} %get-tuple-element.146) | copy-start | bytes 4612
  553.3 106.7 %copy-start.52 = (f32[1,384]{1,0:T(1,128)S(1)}, f32[1,384]{1,0:T(1,128)}, u32[]{:S(2)}) copy-start(f32[1,384]{1,0:T(1,128)} %get-tuple-element.147) | copy-start | bytes 4612
  553.3 107.3 %copy-start.46 = (s32[4096,1]{0,1:T(1,128)S(1)}, s32[4096,1]{0,1:T(1,128)}, u32[]{:S(2)}) copy-start(s32[4096,1]{0,1:T(1,128)} %copy-done.45) | copy-start | bytes 49156
  570.4 3.7 collective-permute-start.2
  574.6 3.7 collective-permute-start.3
  578.9 46.8 %collective-permute-start.4 = (f32[1]{0:T(128)}, f32[1]{0:T(128)}, u32[]{:S(2)}, u32[]{:S(2)}) collective-permute-start(f32[1]{0:T(128)} %add.401), channel_id=1, source_target_pairs={{0,8},{2,10},{4,12},{6,14},{8,0},{10,2},{12,4},{14,6},{16,24},{18,... | collective-permute-start | bytes 20 | tf_op jit(solution)/shard_map/ppermute | solution.py:545
  626.2 26.5 %collective-permute-start.5 = (f32[1]{0:T(128)}, f32[1]{0:T(128)}, u32[]{:S(2)}, u32[]{:S(2)}) collective-permute-start(f32[1]{0:T(128)} %add.402), channel_id=1, source_target_pairs={{0,16},{2,18},{4,20},{6,22},{8,24},{10,26},{12,28},{14,30},{16,0},... | collective-permute-start | bytes 20 | tf_op jit(solution)/shard_map/ppermute | solution.py:545
  681.2 18.1 %copy-start.25 = (f32[1024,384]{1,0:T(8,128)S(1)}, f32[1024,384]{1,0:T(8,128)}, u32[]{:S(2)}) copy-start(f32[1024,384]{1,0:T(8,128)} %get-tuple-element.61.refs_2_) | copy-start | bytes 4718596
  815.6 25.1 %copy-start.48 = (pred[16,384]{1,0:T(8,128)(4,1)S(1)}, pred[16,384]{1,0:T(8,128)(4,1)}, u32[]{:S(2)}) copy-start(pred[16,384]{1,0:T(8,128)(4,1)} %copy-done.47) | copy-start | bytes 18436
  844.3 110.0 %copy-start.57 = (bf16[1,1536,384]{2,1,0:T(8,128)(2,1)S(1)}, bf16[1,1536,384]{2,1,0:T(8,128)(2,1)}, u32[]{:S(2)}) copy-start(bf16[1,1536,384]{2,1,0:T(8,128)(2,1)} %all-gather.8.cloned.1.call-done) | copy-start | bytes 3538948
  954.4 34.4 %copy-start.56 = (bf16[1,384,1536]{2,1,0:T(8,128)(2,1)S(1)}, bf16[1,384,1536]{2,1,0:T(8,128)(2,1)}, u32[]{:S(2)}) copy-start(bf16[1,384,1536]{2,1,0:T(8,128)(2,1)} %all-gather.6.cloned.1.call-done) | copy-start | bytes 3538948
  1004.1 91.5 %all-to-all-start.3 = ((bf16[16,384,384]{2,1,0:T(8,128)(2,1)}), bf16[16,384,384]{2,1,0:T(8,128)(2,1)}, u32[]{:S(2)}, u32[]{:S(2)}) async-start(bf16[16,384,384]{2,1,0:T(8,128)(2,1)} %convolution_convert_fusion), calls=%async_computation.3 | async-start | bytes 9437184 | tf_op jit(solution)/shard_map/all_to_all | solution.py:555
  1008.8 546.0 %reduce-scatter.11.cloned.1.call-start = ((), (), s32[]{:S(2)}) async-start(), calls=%async_computation.12 | async-start | bytes 9539584
  1168.0 59.6 %copy-start.54 = (f32[8,384]{1,0:T(8,128)S(1)}, f32[8,384]{1,0:T(8,128)}, u32[]{:S(2)}) copy-start(f32[8,384]{1,0:T(8,128)} %get-tuple-element.99) | copy-start | bytes 36868
  1168.0 60.3 %copy-start.24 = (f32[1536,384]{1,0:T(8,128)S(1)}, f32[1536,384]{1,0:T(8,128)}, u32[]{:S(2)}) copy-start(f32[1536,384]{1,0:T(8,128)} %get-tuple-element.96) | copy-start | bytes 7077892
  1324.1 14.2 collective-permute-start.6
  1349.0 220.0 %reduce-scatter.7.cloned.1.call-start = ((), (), s32[]{:S(2)}) async-start(), calls=%async_computation.10 | async-start | bytes 1769472 | tf_op jit(solution)/shard_map/reduce_scatter | solution.py:625
  1363.1 218.5 %reduce-scatter.9.cloned.1.call-start = ((), (), s32[]{:S(2)}) async-start(), calls=%async_computation.11 | async-start | bytes 1769472 | tf_op jit(solution)/shard_map/reduce_scatter | solution.py:628
  1554.8 30.0 %collective-permute-start.7 = (f32[1096,128]{1,0:T(8,128)}, f32[1096,128]{1,0:T(8,128)S(1)}, u32[]{:S(2)}, u32[]{:S(2)}) collective-permute-start(f32[1096,128]{1,0:T(8,128)} %bitcast.177), channel_id=1, source_target_pairs={{0,1},{1,0},{2,3},{3,2},{4,5},{5,4},{6,7},{7,6},{8,9},{9,8},{10,11... | collective-permute-start | bytes 1683464 | tf_op jit(solution)/shard_map/ppermute | solution.py:519
  1555.5 30.8 %copy-start.10 = (s32[139656]{0:T(1024)}, s32[139656]{0:T(1024)S(1)}, u32[]{:S(2)}) copy-start(s32[139656]{0:T(1024)S(1)} %convert_add_fusion.1) | copy-start | bytes 1675876
  1592.8 1.1 collective-permute-start.8
  1593.9 3.5 collective-permute-start.9
  1597.5 3.5 collective-permute-start.10
  1601.0 3.5 collective-permute-start.11
  1604.6 4.4 collective-permute-start.12
  1626.2 2.5 collective-permute-start.13
  1628.7 3.5 collective-permute-start.14
  1632.3 3.5 collective-permute-start.15
  1635.8 3.5 collective-permute-start.16
  1639.4 4.4 collective-permute-start.17
  1642.0 24.1 %copy-start.18 = (f32[1,768,384]{2,1,0:T(8,128)S(1)}, f32[1,768,384]{2,1,0:T(8,128)}, u32[]{:S(2)}) copy-start(f32[1,768,384]{2,1,0:T(8,128)} %get-tuple-element.121) | copy-start | bytes 3538948
  1642.0 24.1 %copy-start.19 = (f32[1,768,384]{2,1,0:T(8,128)S(1)}, f32[1,768,384]{2,1,0:T(8,128)}, u32[]{:S(2)}) copy-start(f32[1,768,384]{2,1,0:T(8,128)} %get-tuple-element.122) | copy-start | bytes 3538948
  (43 other events, 246.7 us)
Sparse Core Ops, SparseCore 0:
  12.3 80.8 all-gather.3
  1349.1 205.5 reduce-scatter.10
  1557.7 11.2 reduce-scatter.6
  1571.6 9.8 reduce-scatter.8
Sparse Core Ops, SparseCore 1:
  333.3 10.3 all-gather.5
  345.6 10.3 all-gather.7

commit v2 on v1

--- a/solution.py
+++ b/solution.py
@@ -54,50 +54,19 @@
     )
 
 
-def unpack(flat, experts):
-    shapes = [
-        (PIX, D),
-        (3, D, 3 * D),
-        (3, D, D),
-        (2, D, FF),
-        (2, FF, D),
-        (TASKS, D, experts),
-        (D, C),
-        (2, 7, D),
-    ]
-    pieces = []
-    start = 0
-    for shape in shapes:
-        count = math.prod(shape)
-        pieces.append(flat[start : start + count].reshape(shape))
-        start += count
-    return pieces
-
-
-def segment_onehot(start, count, experts):
-    index = start + jnp.arange(count, dtype=jnp.int32)
-    sizes = segment_sizes(experts)
-    label = jnp.zeros((count,), jnp.int32)
-    edge = 0
-    for size in sizes[:-1]:
+def owner_blocks(edges, shard, owners):
+    firsts = [sum(edge <= shard * i for edge in edges) for i in range(owners)]
+    lasts = [sum(edge < shard * (i + 1) for edge in edges) for i in range(owners)]
+    span = max(b - a + 1 for a, b in zip(firsts, lasts))
+    return (span, jnp.array(firsts, jnp.int32))
+
+
+def segment_edges(experts):
+    edges, edge = [], 0
+    for size in segment_sizes(experts)[:-1]:
         edge += size
-        label = label + (index >= edge).astype(jnp.int32)
-    return label[:, None] == jnp.arange(len(sizes), dtype=jnp.int32)[None, :]
-
-
-def layer_norm(x, gain, bias):
-    mean = jnp.mean(x, -1, keepdims=True)
-    cent = x - mean
-    var = jnp.mean(cent * cent, -1, keepdims=True)
-    return cent * lax.rsqrt(var + EPS_NORM) * gain + bias
-
-
-def norm_back(x, gain, bias, grad):
-    return jax.vjp(layer_norm, x, gain, bias)[1](grad)
-
-
-def gelu(hidden):
-    return jax.nn.gelu(hidden, approximate=False)
+        edges.append(edge)
+    return edges
 
 
 VMEM_LIMIT = 56 * 2**20
@@ -131,15 +100,8 @@
 
 
 def gelu_pair(h):
-    z = jnp.abs(h) * 0.7071067811865476
-    t = 1.0 / (1.0 + 0.3275911 * z)
-    poly = t * (
-        0.127414796
-        + t * (-0.142248368 + t * (0.7107068705 + t * (-0.7265760135 + t * 0.5307027145)))
-    )
-    e = jnp.exp(-(z * z))
-    tail = poly * e
-    cdf = jnp.where(h < 0, tail, 1.0 - tail)
+    cdf = 0.5 + 0.5 * lax.erf(h * 0.7071067811865476)
+    e = jnp.exp((h * h) * -0.5)
     return (h * cdf, cdf + h * (e * 0.3989422804014327))
 
 
@@ -485,34 +447,465 @@
     return local_call(head_kernel, outs, args, 6 * seq * D * 128, scratch)
 
 
-def feed_forward(rows16, w_up, w_back):
-    hidden = plain(rows16, w_up)
-    return (plain(gelu(hidden).astype(LOWTYPE), w_back), hidden)
-
-
-def feed_backward(rows16, hidden, grad16, w_up, w_back):
-    act16 = gelu(hidden).astype(LOWTYPE)
-    d_back = left_t(act16, grad16)
-    d_act = right_t(grad16, w_back)
-    d_hidden = jax.vjp(gelu, hidden)[1](d_act)[0].astype(LOWTYPE)
-    return (right_t(d_hidden, w_up), (left_t(rows16, d_hidden), d_back))
-
-
-def make_slots(routes, experts, capacity):
-    flat = routes.reshape(-1)
-    seq = routes.shape[0]
-    named = (routes[:, :, None] == jnp.arange(experts, dtype=jnp.int32)[None, None, :]).astype(LOWTYPE)
-    earlier = jnp.arange(seq)[:, None] > jnp.arange(seq)[None, :]
-    before = plain(earlier.astype(LOWTYPE), jnp.sum(named, 1))
-    rank = jnp.sum(before[:, None, :] * named, 2).astype(jnp.int32).reshape(-1)
-    slot = flat * capacity + rank
-    assign = (
-        jnp.zeros((experts * capacity,), jnp.int32)
-        .at[slot]
-        .set(jnp.arange(flat.shape[0], dtype=jnp.int32))
-    )
-    used = jnp.zeros((experts * capacity,), jnp.int32).at[slot].set(1)
-    return (slot, assign, used)
+SLOTS = 128
+
+
+def by_load(load, capacity, work):
+    for count in range(SLOTS, capacity + 1, SLOTS):
+        inside = load > count - SLOTS if count > SLOTS else load >= 0
+        if count < capacity:
+            inside = inside & (load <= count)
+        pl.when(inside)(functools.partial(work, count))
+
+
+def slot_select(place, count):
+    row = lax.broadcasted_iota(jnp.int32, (count, place.shape[1]), 0).astype(FULLTYPE)
+    return jnp.where(place == row, 1.0, 0.0).astype(LOWTYPE)
+
+
+def column_of(table, expert):
+    lane = lax.broadcasted_iota(jnp.int32, table.shape, 1)
+    return jnp.sum(jnp.where(lane == expert, table, 0.0), -1, keepdims=True)
+
+
+def patch_select(spread, count):
+    lane = lax.broadcasted_iota(jnp.int32, (1, 128), 1).astype(FULLTYPE)
+    return jnp.concatenate(
+        [
+            jnp.where(spread == lane + first, 1.0, 0.0).astype(LOWTYPE)
+            for first in range(0, count, 128)
+        ],
+        1,
+    )
+
+
+def moe_up_kernel(
+    loads, c_ref, router, table, place, w_in,
+    gates_ref, spread_place, spread_gate, rows_ref, act_ref, slope_ref,
+):
+    expert = pl.program_id(0)
+    seq, capacity, parts = (c_ref.shape[0], rows_ref.shape[0], w_in.shape[1])
+    width = w_in.shape[3]
+
+    @pl.when(expert == 0)
+    def _():
+        def start(i, carry):
+            rows = rows_of(i)
+            z = plain(c_ref[rows, :], router[...])
+            named = table[rows, :] >= 0
+            shown = jnp.where(named, z, NEG)
+            e = jnp.where(named, jnp.exp(shown - jnp.max(shown, -1, keepdims=True)), 0.0)
+            gates_ref[rows, :] = e / jnp.sum(e, -1, keepdims=True)
+            return carry
+
+        lax.fori_loop(0, seq // ROWS, start, 0)
+
+    def fan(i, carry):
+        rows = rows_of(i)
+        for source, out in ((table, spread_place), (gates_ref, spread_gate)):
+            out[0, rows, :] = jnp.broadcast_to(column_of(source[rows, :], expert), (ROWS, 128))
+        return carry
+
+    lax.fori_loop(0, seq // ROWS, fan, 0)
+
+    def work(count):
+        at = pl.ds(0, count)
+        rows = plain(slot_select(place[0], count), c_ref[...]).astype(LOWTYPE)
+        rows_ref[at, :] = rows
+        for part in range(parts):
+            step = width // 3 if width % 384 == 0 else width
+            for first in range(0, width, step):
+                act, slope = gelu_pair(plain(rows, w_in[0, part, :, pl.ds(first, step)]))
+                units = pl.ds(part * width + first, step)
+                slope_ref[at, units] = slope
+                act_ref[at, units] = act.astype(LOWTYPE)
+        if count < capacity:
+            rows_ref[pl.ds(count, capacity - count), :] = jnp.zeros((capacity - count, D), LOWTYPE)
+
+    by_load(loads[expert], capacity, work)
+
+
+def moe_down_kernel(loads, mid_ref, spread_place, spread_gate, act_ref, w_out, next_ref, y_ref):
+    expert = pl.program_id(0)
+    seq, capacity = (mid_ref.shape[0], act_ref.shape[0])
+
+    @pl.when(expert == 0)
+    def _():
+        next_ref[...] = mid_ref[...]
+
+    def work(count):
+        at = pl.ds(0, count)
+        y_ref[at, :] = plain(act_ref[at, :], w_out[0]).astype(LOWTYPE)
+        if count < capacity:
+            y_ref[pl.ds(count, capacity - count), :] = jnp.zeros((capacity - count, D), LOWTYPE)
+
+        def add(i, carry):
+            rows = rows_of(i)
+            taken = plain(patch_select(spread_place[0, rows, :], count), y_ref[at, :])
+            for first in range(0, D, 128):
+                lanes = pl.ds(first, 128)
+                next_ref[rows, lanes] += spread_gate[0, rows, :] * taken[:, first : first + 128]
+            return carry
+
+        lax.fori_loop(0, seq // ROWS, add, 0)
+
+    by_load(loads[expert], capacity, work)
+
+
+def moe_gate_kernel(
+    loads, grad_ref, c_ref, router, gates, place, spread_place, spread_gate, y_ref,
+    d_router, d_c, dy_ref, low_ref, dz_ref, d_gates,
+):
+    expert = pl.program_id(0)
+    seq, capacity = (grad_ref.shape[0], y_ref.shape[0])
+    lane = lax.broadcasted_iota(jnp.int32, (ROWS, d_gates.shape[1]), 1)
+
+    @pl.when(expert == 0)
+    def _():
+        d_gates[...] = jnp.zeros_like(d_gates)
+
+    def work(count):
+        at = pl.ds(0, count)
+
+        def one(i, carry):
+            rows = rows_of(i)
+            grad = grad_ref[rows, :]
+            gate = spread_gate[0, rows, :]
+            taken = plain(patch_select(spread_place[0, rows, :], count), y_ref[at, :])
+            d_gate = jnp.sum(grad * taken, -1, keepdims=True)
+            d_gates[rows, :] += jnp.where(lane == expert, d_gate, 0.0)
+            for first in range(0, D, 128):
+                lanes = pl.ds(first, 128)
+                low_ref[rows, lanes] = (gate * grad[:, first : first + 128]).astype(LOWTYPE)
+            return carry
+
+        lax.fori_loop(0, seq // ROWS, one, 0)
+        dy_ref[at, :] = plain(slot_select(place[0], count), low_ref[...]).astype(LOWTYPE)
+        if count < capacity:
+            dy_ref[pl.ds(count, capacity - count), :] = jnp.zeros((capacity - count, D), LOWTYPE)
+
+    by_load(loads[expert], capacity, work)
+
+    @pl.when(expert == pl.num_programs(0) - 1)
+    def _():
+        def last(i, carry):
+            rows = rows_of(i)
+            gate = gates[rows, :]
+            d_gate = d_gates[rows, :]
+            d_z = gate * (d_gate - jnp.sum(gate * d_gate, -1, keepdims=True))
+            dz_ref[rows, :] = d_z.astype(LOWTYPE)
+            d_c[rows, :] = right_t(dz_ref[rows, :], router[...])
+            return carry
+
+        lax.fori_loop(0, seq // ROWS, last, 0)
+        d_router[...] = left_t(c_ref[...], dz_ref[...])
+
+
+def moe_backward_kernel(loads, start_ref, spread_place, w_in, w_out, dy_ref, slope_ref, d_c, back_ref):
+    expert = pl.program_id(0)
+    seq, capacity, parts = (d_c.shape[0], dy_ref.shape[0], w_in.shape[1])
+    width = w_in.shape[3]
+
+    @pl.when(expert == 0)
+    def _():
+        d_c[...] = start_ref[...]
+
+    def work(count):
+        at = pl.ds(0, count)
+        d_y = dy_ref[at, :]
+        back = jnp.zeros((count, D), FULLTYPE)
+        for part in range(parts):
+            units = pl.ds(part * width, width)
+            d_act = right_t(d_y, w_out[0, units, :])
+            d_h = (d_act * slope_ref[at, units]).astype(LOWTYPE)
+            back += right_t(d_h, w_in[0, part])
+        back_ref[at, :] = back.astype(LOWTYPE)
+
+        def add(i, carry):
+            rows = rows_of(i)
+            d_c[rows, :] += plain(patch_select(spread_place[0, rows, :], count), back_ref[at, :])
+            return carry
+
+        lax.fori_loop(0, seq // ROWS, add, 0)
+
+    by_load(loads[expert], capacity, work)
+
+
+def moe_weight_kernel(count, *refs):
+    rows_refs, dy_refs = (refs[:count], refs[count : 2 * count])
+    w_in, w_out, d_in, d_out = refs[2 * count :]
+
+    @pl.when(pl.program_id(0) == 0)
+    def _():
+        d_in[...] = jnp.zeros_like(d_in)
+        d_out[...] = jnp.zeros_like(d_out)
+
+    width = w_in.shape[1]
+    step = 384 if width % 384 == 0 else width
+    for rows_ref, dy_ref in zip(rows_refs, dy_refs):
+        rows, d_y = (rows_ref[...], dy_ref[...])
+        for first in range(0, width, step):
+            units = pl.ds(first, step)
+            act, slope = gelu_pair(plain(rows, w_in[:, units]))
+            d_h = (right_t(d_y, w_out[units, :]) * slope).astype(LOWTYPE)
+            d_out[units, :] += left_t(act.astype(LOWTYPE), d_y)
+            d_in[:, units] += left_t(rows, d_h)
+
+
+def whole(shape):
+    return pl.BlockSpec(shape, lambda e: (0,) * len(shape))
+
+
+def gridded(kernel, steps, in_specs, outs, out_specs, args, flops, scratch=()):
+    moved = sum(math.prod(a.shape) * a.dtype.itemsize for a in (*args, *outs))
+    return pl.pallas_call(
+        kernel,
+        grid=(steps,),
+        out_shape=outs,
+        in_specs=in_specs,
+        out_specs=out_specs,
+        scratch_shapes=scratch,
+        compiler_params=pltpu.CompilerParams(vmem_limit_bytes=VMEM_LIMIT),
+        cost_estimate=pl.CostEstimate(flops=flops, bytes_accessed=moved, transcendentals=0),
+    )(*args)
+
+
+SCALARS = pl.BlockSpec(memory_space=pltpu.SMEM)
+
+
+def in_spec(w_in):
+    return pl.BlockSpec((1,) + w_in.shape[1:], lambda e: (e, 0, 0, 0))
+
+
+def out_spec(w_out):
+    return pl.BlockSpec((1,) + w_out.shape[1:], lambda e: (e, 0, 0))
+
+
+def spread_spec(seq):
+    return pl.BlockSpec((1, seq, 128), lambda e: (e, 0, 0))
+
+
+def moe_up(loads, c16, router, table, place, w_in, capacity):
+    seq, experts = table.shape
+    hidden = w_in.shape[1] * w_in.shape[3]
+    per = lambda width: pl.BlockSpec((capacity, width), lambda e: (e, 0))
+    return gridded(
+        moe_up_kernel,
+        experts,
+        [SCALARS, whole((seq, D)), whole((D, experts)), whole((seq, experts))]
+        + [pl.BlockSpec((1, 1, seq), lambda e: (e, 0, 0)), in_spec(w_in)],
+        [
+            shaped((seq, experts), FULLTYPE),
+            shaped((experts, seq, 128), FULLTYPE),
+            shaped((experts, seq, 128), FULLTYPE),
+            shaped((experts * capacity, D), LOWTYPE),
+            shaped((experts * capacity, hidden), LOWTYPE),
+            shaped((experts * capacity, hidden), FULLTYPE),
+        ],
+        [whole((seq, experts)), spread_spec(seq), spread_spec(seq), per(D), per(hidden), per(hidden)],
+        [loads, c16, router, table, place, w_in],
+        2 * experts * capacity * D * (hidden + seq),
+    )
+
+
+def moe_down(loads, mid, spread_place, spread_gate, act, w_out):
+    seq, experts = (mid.shape[0], w_out.shape[0])
+    capacity, hidden = (act.shape[0] // experts, act.shape[1])
+    per = lambda width: pl.BlockSpec((capacity, width), lambda e: (e, 0))
+    return gridded(
+        moe_down_kernel,
+        experts,
+        [SCALARS, whole((seq, D)), spread_spec(seq), spread_spec(seq), per(hidden), out_spec(w_out)],
+        [shaped((seq, D), FULLTYPE), shaped((experts * capacity, D), LOWTYPE)],
+        [whole((seq, D)), per(D)],
+        [loads, mid, spread_place, spread_gate, act, w_out],
+        2 * experts * capacity * D * (hidden + seq),
+    )
+
+
+def moe_gate_backward(loads, grad, c16, router, gates, place, spread_place, spread_gate, y16):
+    seq, experts = gates.shape
+    capacity = y16.shape[0] // experts
+    per = pl.BlockSpec((capacity, D), lambda e: (e, 0))
+    return gridded(
+        moe_gate_kernel,
+        experts,
+        [SCALARS, whole((seq, D)), whole((seq, D)), whole((D, experts)), whole((seq, experts))]
+        + [pl.BlockSpec((1, 1, seq), lambda e: (e, 0, 0)), spread_spec(seq), spread_spec(seq), per],
+        [
+            shaped((D, experts), FULLTYPE),
+            shaped((seq, D), FULLTYPE),
+            shaped((experts * capacity, D), LOWTYPE),
+        ],
+        [whole((D, experts)), whole((seq, D)), per],
+        [loads, grad, c16, router, gates, place, spread_place, spread_gate, y16],
+        4 * experts * capacity * D * seq,
+        [
+            pltpu.VMEM((seq, D), LOWTYPE),
+            pltpu.VMEM((seq, experts), LOWTYPE),
+            pltpu.VMEM((seq, experts), FULLTYPE),
+        ],
+    )
+
+
+def moe_backward(loads, start, spread_place, w_in, w_out, dy16, slope):
+    seq, experts = (start.shape[0], w_out.shape[0])
+    capacity, hidden = (dy16.shape[0] // experts, w_out.shape[1])
+    per = lambda width: pl.BlockSpec((capacity, width), lambda e: (e, 0))
+    return gridded(
+        moe_backward_kernel,
+        experts,
+        [SCALARS, whole((seq, D)), spread_spec(seq), in_spec(w_in), out_spec(w_out)]
+        + [per(D), per(hidden)],
+        [shaped((seq, D), FULLTYPE)],
+        [whole((seq, D))],
+        [loads, start, spread_place, w_in, w_out, dy16, slope],
+        2 * experts * capacity * D * (2 * hidden + seq),
+        [pltpu.VMEM((capacity, D), LOWTYPE)],
+    )[0]
+
+
+def moe_weight_backward(rows, dy, w_in, w_out):
+    count, width = (rows[0].shape[0], w_in.shape[1])
+    step = 512
+    per = pl.BlockSpec((step, D), lambda i: (i, 0))
+    return gridded(
+        functools.partial(moe_weight_kernel, len(rows)),
+        count // step,
+        [per] * (2 * len(rows)) + [whole((D, width)), whole((width, D))],
+        [shaped((D, width), FULLTYPE), shaped((width, D), FULLTYPE)],
+        [whole((D, width)), whole((width, D))],
+        [*rows, *dy, w_in, w_out],
+        10 * count * len(rows) * D * width,
+    )
+
+
+def flat_plan(experts):
+    shapes = [(PIX, D)] + [(D, 3 * D)] * 3 + [(D, D)] * 3 + [(D, FF)] * 2 + [(FF, D)] * 2
+    plan, start = [], 0
+    for height, width in shapes:
+        plan.append((start, height, width // 128))
+        start += height * width // 128
+    return (plan, start)
+
+
+def owner_rows(shard, parts):
+    return -(-((shard + 127 + 127) // 128) // (16 * parts)) * 16 * parts
+
+
+def chunk_of(rows, most=128):
+    return max(c for c in range(16, most + 1, 16) if rows % c == 0)
+
+
+def unpack_kernel(plan, shard, parts_ref, *refs):
+    outs, rest, flat = (refs[: len(plan)], refs[len(plan)], refs[len(plan) + 1])
+    owners, rows = parts_ref.shape[:2]
+    chunk = chunk_of(rows)
+    for owner in range(owners):
+        first = shard * owner // 128
+        if owner:
+            last = flat[pl.ds(first, 1), :]
+
+        def copy(i, carry, owner=owner, first=first):
+            flat[pl.ds(first + i * chunk, chunk), :] = parts_ref[
+                owner, pl.ds(pl.multiple_of(i * chunk, chunk), chunk), :
+            ].astype(FULLTYPE)
+            return carry
+
+        lax.fori_loop(0, rows // chunk, copy, 0)
+        if owner and shard * owner % 128:
+            flat[pl.ds(first, 1), :] += last
+    for (start, height, across), out in zip(plan, outs):
+
+        def place(i, carry, start=start, across=across, out=out):
+            for c in range(across):
+                taken = flat[pl.ds(start + i * 128 * across + c, 128, stride=across), :]
+                out[rows_of(i, 128), pl.ds(c * 128, 128)] = taken.astype(LOWTYPE)
+            return carry
+
+        lax.fori_loop(0, height // 128, place, 0)
+    start = plan[-1][0] + plan[-1][1] * plan[-1][2]
+    rest[...] = flat[pl.ds(start, rest.shape[0]), :]
+
+
+def unpack_weights(parts, shard, experts):
+    plan, start = flat_plan(experts)
+    owners, rows = parts.shape[:2]
+    rest = shard * owners // 128 - start
+    outs = [shaped((height, across * 128), LOWTYPE) for _, height, across in plan]
+    outs.append(shaped((rest, 128), FULLTYPE))
+    flat = pltpu.VMEM((-(-(shard * (owners - 1) // 128 + rows) // 8) * 8, 128), FULLTYPE)
+    return local_call(
+        functools.partial(unpack_kernel, plan, shard), outs, [parts], 0, [flat]
+    )
+
+
+def pack_kernel(plan, shard, select, place_ref, *refs):
+    count = len(plan)
+    mats, rest, norms = (refs[:count], refs[count], refs[count + 1 : count + 5])
+    outs, flat = (refs[count + 5 : -1], refs[-1])
+    for (start, height, across), mat in zip(plan, mats):
+
+        def place(i, carry, start=start, across=across, mat=mat):
+            for c in range(across):
+                flat[pl.ds(start + i * 128 * across + c, 128, stride=across), :] = mat[
+                    rows_of(i, 128), pl.ds(c * 128, 128)
+                ]
+            return carry
+
+        lax.fori_loop(0, height // 128, place, 0)
+    start = plan[-1][0] + plan[-1][1] * plan[-1][2]
+    flat[pl.ds(start, rest.shape[0]), :] = rest[...]
+    start += rest.shape[0]
+    for kind in (0, 1):
+        for layer, norm in enumerate(norms):
+            for k in range(2 if layer < 3 else 1):
+                for c in range(D // 128):
+                    row = start + ((7 * kind + 2 * layer + k) * D) // 128 + c
+                    flat[row : row + 1, :] = norm[2 * k + kind : 2 * k + kind + 1, c * 128 : c * 128 + 128]
+    for out, which in zip(outs, select):
+        groups, owners, rows = out.shape[:3]
+        chunk = chunk_of(rows)
+        for group in range(groups):
+            for owner in range(owners):
+                member = which(place_ref[0], group)
+                first = shard * owner // 128 + member * rows
+
+                def copy(i, carry, out=out, group=group, owner=owner, first=first):
+                    out[group, owner, pl.ds(pl.multiple_of(i * chunk, chunk), chunk), :] = flat[
+                        pl.ds(first + i * chunk, chunk), :
+                    ].astype(out.dtype)
+                    return carry
+
+                lax.fori_loop(0, rows // chunk, copy, 0)
+
+
+def pack_gradients(mats, rest, norms, shard, owners, groups, place, experts):
+    plan, _ = flat_plan(experts)
+    rows = owner_rows(shard, groups)
+    part = rows // groups
+    if groups == 2:
+        outs = [shaped((1, owners, part, 128), t) for t in (FULLTYPE, EXCHANGE)]
+        select = [lambda here, g: here, lambda here, g: 1 - here]
+    else:
+        outs = [shaped((groups, owners, part, 128), FULLTYPE)]
+        select = [lambda here, g: g]
+    flat = pltpu.VMEM((-(-(shard * (owners - 1) // 128 + rows) // 8) * 8, 128), FULLTYPE)
+    args = [place.reshape(1), *mats, rest, *norms]
+    moved = sum(math.prod(a.shape) * a.dtype.itemsize for a in (*args, *outs))
+    return pl.pallas_call(
+        functools.partial(pack_kernel, plan, shard, select),
+        out_shape=outs,
+        in_specs=[SCALARS] + in_vmem(len(args) - 1),
+        out_specs=in_vmem(len(outs)),
+        scratch_shapes=[flat],
+        compiler_params=pltpu.CompilerParams(vmem_limit_bytes=PACK_LIMIT),
+        cost_estimate=pl.CostEstimate(flops=0, bytes_accessed=moved, transcendentals=0),
+    )(*args)
+
+
+EXCHANGE = jnp.bfloat16
+PACK_LIMIT = 60 * 2**20
 
 
 def swap_dp(value):
@@ -549,12 +942,6 @@
 
 def to_experts(buffer):
     return lax.all_to_all(buffer, "ep", split_axis=0, concat_axis=0, tiled=True)
-
-
-def from_experts(buffer):
-    return lax.all_to_all(
-        buffer.astype(jnp.bfloat16), "ep", split_axis=0, concat_axis=0, tiled=True
-    ).astype(buffer.dtype)
 
 
 def per_device(
@@ -587,56 +974,59 @@
     seq = patches.shape[0]
     capacity = 3 * seq * TOP // (2 * experts)
     shard = dense_weight.shape[0]
-    part_rows = -(-shard // (groups * 1024)) * 8
-    padded = part_rows * 128 * groups
-    low_parts = jnp.pad(dense_weight.astype(LOWTYPE), (0, padded - shard)).reshape(
-        groups, part_rows, 128
-    )
-    own_part = lax.dynamic_index_in_dim(low_parts, dp_place, 0, keepdims=False)
-    parts = join_dp(lax.all_gather(own_part, "ep"), dp_place)
-    gathered = jnp.swapaxes(parts, 0, 1).reshape(ep_count, padded)[:, :shard].reshape(-1)
-    w_patch, w_qkv, w_attn, w_up, w_down, w_router, w_head, norms16 = unpack(gathered, experts)
-    norms = norms16.astype(FULLTYPE)
-    own_in, own_out = (
-        lax.all_gather(expert_in.astype(LOWTYPE), "dp", axis=2, tiled=True),
-        lax.all_gather(expert_out.astype(LOWTYPE), "dp", axis=1, tiled=True),
-    )
-    own_in = own_in[0]
-    own_out = own_out[0]
-    task = tasks[0]
-    router = lax.dynamic_index_in_dim(w_router, task, 0, keepdims=False)
-    slot, assign, used = make_slots(routes, experts, capacity)
-    route_hot = (routes[:, :, None] == jnp.arange(experts, dtype=jnp.int32)[None, None, :]).astype(
-        FULLTYPE
-    )
-
-    def dispatch(send):
-        buffer = jnp.repeat(send.reshape(experts, capacity, D), copies, axis=0)
-        return to_experts(buffer)
-
-    def combine(partial_value):
-        back = from_experts(partial_value).reshape(experts, copies, capacity, D)
-        summed = jnp.sum(back, 1).astype(LOWTYPE).reshape(experts * capacity, D)
-        return summed[slot].reshape(seq, TOP, D).astype(FULLTYPE)
-
-    def expert_backward(arrived, rows, hidden):
-        d_rows, (d_in, d_out) = feed_backward(rows, hidden, arrived.reshape(-1, D), own_in, own_out)
-        d_in_own, d_out_own = (
-            lax.psum_scatter(
-                d_in[None].astype(jnp.bfloat16), "dp", scatter_dimension=2, tiled=True
-            ).astype(jnp.float32),
-            lax.psum_scatter(
-                d_out[None].astype(jnp.bfloat16), "dp", scatter_dimension=1, tiled=True
-            ).astype(jnp.float32),
+    piece = shard // groups
+    edges = segment_edges(experts)
+    block_count = len(edges) + 1 + 2 * experts
+    span, firsts = owner_blocks(edges, shard, ep_count)
+    first_block = firsts[ep_place]
+    starts = [
+        jnp.take(jnp.array([0] + edges + [shard * ep_count] * span, jnp.int32), first_block + k)
+        - ep_place * shard
+        for k in range(span + 1)
+    ]
+
+    def placed(value, at, count):
+        return jnp.where(jnp.arange(count) == at, value, 0.0)
+
+    def block_sums(dense_vals, in_vals, out_vals):
+        part = lax.dynamic_slice_in_dim(dense_vals, dp_place * piece, piece)
+        square = part * part
+        index = dp_place * piece + jnp.arange(piece, dtype=jnp.int32)
+        listed = placed(jnp.sum(in_vals * in_vals), len(edges) + 1 + own_expert, block_count)
+        listed += placed(
+            jnp.sum(out_vals * out_vals), len(edges) + 1 + experts + own_expert, block_count
         )
-        return (d_rows.reshape(arrived.shape), d_in_own, d_out_own)
-
-    def norm_rows(layer):
-        rows = [norms[0, 2 * layer], norms[1, 2 * layer]]
-        if layer < 3:
-            rows += [norms[0, 2 * layer + 1], norms[1, 2 * layer + 1]]
-        return jnp.pad(jnp.stack(rows), ((0, 8 - len(rows)), (0, 0)))
-
+        for k in range(span):
+            inside = (index >= starts[k]) & (index < starts[k + 1])
+            listed += placed(jnp.sum(jnp.where(inside, square, 0.0)), first_block + k, block_count)
+        return listed
+
+    rows = owner_rows(shard, groups)
+    offset = lax.rem(ep_place * (shard % 128), 128)
+    spread = lax.dynamic_update_slice(
+        jnp.zeros((rows * 128,), LOWTYPE), dense_weight.astype(LOWTYPE), (offset,)
+    )
+    own_part = lax.dynamic_index_in_dim(
+        spread.reshape(groups, rows // groups, 128), dp_place, 0, keepdims=False
+    )
+    parts = lax.all_gather(own_part, ("ep", "dp")).reshape(ep_count, rows, 128)
+    low_in, low_out = (expert_in[0].astype(LOWTYPE), expert_out[0].astype(LOWTYPE))
+    all_in = lax.all_gather(low_in, ("ep", "dp"))
+    all_out = lax.all_gather(low_out, ("ep", "dp"))
+    width = low_in.shape[1]
+    w_in = all_in.reshape(experts, copies * groups, D, width)
+    if width % 128:
+        w_in = jnp.swapaxes(w_in, 1, 2).reshape(experts, 1, D, copies * groups * width)
+    w_out = all_out.reshape(experts, copies * groups * width, D)
+
+    named = jnp.sum(
+        (routes[:, :, None] == jnp.arange(experts, dtype=jnp.int32)[None, None, :]).astype(FULLTYPE),
+        1,
+    )
+    earlier = jnp.arange(seq)[:, None] > jnp.arange(seq)[None, :]
+    table = jnp.where(named > 0, plain(earlier.astype(LOWTYPE), named.astype(LOWTYPE)), -1.0)
+    place = table.T.reshape(experts, 1, seq)
+    loads = jnp.sum(named, 0).astype(jnp.int32)
     bias = jnp.where(patch_valid > 0, 0.0, NEG).astype(FULLTYPE)
     across, down = (bias.reshape(1, seq), bias.reshape(seq, 1))
     weight_pix = (pixel_mask * patch_valid[:, None]).astype(FULLTYPE)
@@ -645,96 +1035,141 @@
     counts = jnp.sum(jnp.where(class_hot, weight_pix[:, :, None], 0.0), 1)
     total = sum_all(jnp.sum(count_tok).reshape(1))[0]
 
+    together = lax.optimization_barrier
+    weight_sums = block_sums(dense_weight, expert_in, expert_out)
+    parts, counts, count_tok, total, table, place, loads, across, down, weight_sums = together(
+        (parts, counts, count_tok, total, table, place, loads, across, down, weight_sums)
+    )
+    *mats, rest = unpack_weights(parts, shard, experts)
+    w_patch, w_qkv, w_attn = (mats[0], mats[1:4], mats[4:7])
+    w_up, w_down = (mats[7:9], mats[9:11])
+    router_rows, head_rows = (TASKS * D * experts // 128, D * C // 128)
+    w_router = rest[:router_rows].reshape(TASKS, D, experts).astype(LOWTYPE)
+    w_head = rest[router_rows : router_rows + head_rows].reshape(D, C).astype(LOWTYPE)
+    norms = rest[router_rows + head_rows :].reshape(2, 7, D)
+    task = tasks[0]
+    router = lax.dynamic_index_in_dim(w_router, task, 0, keepdims=False)
+
+    def dispatch(send, block):
+        third = capacity // 3
+        taken = send.reshape(experts, capacity, D)[:, block * third : (block + 1) * third]
+        return to_experts(jnp.repeat(taken, copies, axis=0)).reshape(-1, D)
+
+    together = lax.optimization_barrier
+
+    def norm_rows(layer):
+        rows = [norms[0, 2 * layer], norms[1, 2 * layer]]
+        if layer < 3:
+            rows += [norms[0, 2 * layer + 1], norms[1, 2 * layer + 1]]
+        return jnp.pad(jnp.stack(rows), ((0, 8 - len(rows)), (0, 0)))
+
     x0, *kept0, x1, act0, slope0 = layer_forward(
         patches, w_patch, w_qkv[0], w_attn[0], norm_rows(0), across, w_up[0], w_down[0]
     )
     mid1, c16, *kept1 = layer_forward(
         x1, None, w_qkv[1], w_attn[1], norm_rows(1), across, None, None
     )
-    logits = plain(c16, router)
-    gates = jax.nn.softmax(jnp.sum(route_hot * logits[:, None, :], -1), -1)
-    send = jnp.where(used[:, None] > 0, c16[assign // TOP], jnp.zeros((), LOWTYPE))
-    arrived = dispatch(send)
-    rows = arrived.reshape(-1, D)
-    out, hidden = feed_forward(rows, own_in, own_out)
-    picks = combine(out.reshape(arrived.shape))
-    x2 = mid1 + jnp.sum(gates[:, :, None] * picks, 1)
+    gates, spread_place, spread_gate, sent, act1, slope1 = moe_up(
+        loads, c16, router, table, place, w_in, capacity
+    )
+    x2, y16 = moe_down(loads, mid1, spread_place, spread_gate, act1, w_out)
+    x2, sent = together((x2, sent))
+    rows_a = dispatch(sent, 0)
     *kept2, x3, act2, slope2 = layer_forward(
         x2, None, w_qkv[2], w_attn[2], norm_rows(2), across, w_up[1], w_down[1]
     )
+    x3, sent, rows_a = together((x3, sent, rows_a))
+    rows_b = dispatch(sent, 1)
     loss_lanes, d_head, d_normf, grad = head_call(
         x3, norm_rows(3), w_head, counts, count_tok, total
     )
     local = loss_lanes[0, 0]
+    grad, local = together((grad, local))
     d_qkv2, d_attn2, d_norm2, d_up1, d_down1, grad = layer_backward(
         grad, x2, (*kept2, act2, slope2), w_qkv[2], w_attn[2], norm_rows(2), down,
         (w_up[1], w_down[1]), None, None,
     )
-    d_gates = jnp.sum(grad[:, None, :] * picks, -1)
-    d_picked = gates * (d_gates - jnp.sum(gates * d_gates, -1, keepdims=True))
-    d_logits = jnp.sum(route_hot * d_picked[:, :, None], 1).astype(LOWTYPE)
+    grad, sent, rows_b = together((grad, sent, rows_b))
+    rows_c = dispatch(sent, 2)
+    d_own_router, d_c, dy16 = moe_gate_backward(
+        loads, grad, c16, router, gates, place, spread_place, spread_gate, y16
+    )
+    d_c, dy16, rows_c = together((d_c, dy16, rows_c))
+    dy_a = dispatch(dy16, 0)
+    d_c = moe_backward(loads, d_c, spread_place, w_in, w_out, dy16, slope1)
+    d_c, dy16, dy_a = together((d_c, dy16, dy_a))
+    dy_b = dispatch(dy16, 1)
     task_hot = (jnp.arange(TASKS, dtype=jnp.int32) == task)[:, None, None]
-    d_router = jnp.where(task_hot, left_t(c16, d_logits)[None], 0.0)
-    d_picks = (gates[:, :, None] * grad[:, None, :]).astype(LOWTYPE).reshape(seq * TOP, D)
-    send = jnp.where(used[:, None] > 0, d_picks[assign], jnp.zeros((), LOWTYPE))
-    d_rows, d_in, d_out = expert_backward(dispatch(send), rows, hidden)
-    d_c = right_t(d_logits, router) + jnp.sum(combine(d_rows), 1)
+    d_router = jnp.where(task_hot, d_own_router[None], 0.0)
     d_qkv1, d_attn1, d_norm1, grad = layer_backward(
         grad, x1, (mid1, c16, *kept1), w_qkv[1], w_attn[1], norm_rows(1), down, None, d_c, None
     )
+    grad, dy16, dy_b = together((grad, dy16, dy_b))
+    dy_c = dispatch(dy16, 2)
     d_qkv0, d_attn0, d_norm0, d_up0, d_down0, d_patch = layer_backward(
         grad, x0, (*kept0, act0, slope0), w_qkv[0], w_attn[0], norm_rows(0), down,
         (w_up[0], w_down[0]), None, patches,
     )
-    d_head = d_head[:, :C]
-    each = [d_norm0, d_norm1, d_norm2]
-    gain_list = [n[k] for n in each for k in (0, 2)] + [d_normf[0]]
-    bias_list = [n[k] for n in each for k in (1, 3)] + [d_normf[1]]
-    d_qkv_list = [d_qkv0, d_qkv1, d_qkv2]
-    d_attn_list = [d_attn0, d_attn1, d_attn2]
-    d_up_list = [d_up0, d_up1]
-    d_down_list = [d_down0, d_down1]
-    d_norms = jnp.stack([jnp.stack(gain_list), jnp.stack(bias_list)])
-    listed = [
-        d_patch,
-        jnp.stack(d_qkv_list),
-        jnp.stack(d_attn_list),
-        jnp.stack(d_up_list),
-        jnp.stack(d_down_list),
-        d_router,
-        d_head,
-        d_norms,
-    ]
-    flat_grad = jnp.concatenate([piece.reshape(-1) for piece in listed])
-    by_owner = jnp.pad(flat_grad.reshape(ep_count, shard), ((0, 0), (0, padded - shard)))
-    by_part = jnp.swapaxes(by_owner.reshape(ep_count, groups, part_rows, 128), 0, 1)
-    own_sum = lax.psum_scatter(
-        sum_scatter_dp(by_part, dp_place), "ep", scatter_dimension=0, tiled=True
-    )[0]
-    dense_grad = join_dp(own_sum, dp_place).reshape(padded)[:shard]
-    piece = shard // groups
-    part_hot = segment_onehot(ep_place * shard + dp_place * piece, piece, experts)
-    expert_hot = (jnp.arange(experts, dtype=jnp.int32) == own_expert).astype(FULLTYPE)
-
-    def block_sums(dense_vals, in_vals, out_vals):
-        part = lax.dynamic_slice_in_dim(dense_vals, dp_place * piece, piece)
-        dense_part = jnp.sum(jnp.where(part_hot, (part * part)[:, None], 0.0), 0)
-        return jnp.concatenate(
-            [
-                dense_part,
-                expert_hot * jnp.sum(in_vals * in_vals),
-                expert_hot * jnp.sum(out_vals * out_vals),
-            ]
+    d_patch, dy_c = together((d_patch, dy_c))
+    expert_rows, expert_dy = ([rows_a, rows_b, rows_c], [dy_a, dy_b, dy_c])
+    d_rest = jnp.concatenate(
+        [
+            d_router.reshape(router_rows, 128),
+            d_head[:, :C].reshape(head_rows, 128),
+        ]
+    )
+    packed = pack_gradients(
+        [d_patch, d_qkv0, d_qkv1, d_qkv2, d_attn0, d_attn1, d_attn2, d_up0, d_up1, d_down0, d_down1],
+        d_rest, [d_norm0, d_norm1, d_norm2, d_normf], shard, ep_count, groups, dp_place, experts,
+    )
+    if groups == 2:
+        summed = packed[0][0] + swap_dp(packed[1][0]).astype(FULLTYPE)
+    else:
+        summed = lax.psum_scatter(packed[0], "dp", scatter_dimension=0, tiled=True)[0]
+    arrived = to_experts(summed.astype(LOWTYPE))
+
+    own_in = lax.dynamic_index_in_dim(
+        all_in.reshape(ep_count, groups, D, width), ep_place, 0, keepdims=False
+    )
+    own_out = lax.dynamic_index_in_dim(
+        all_out.reshape(ep_count, groups, width, D), ep_place, 0, keepdims=False
+    )
+    if groups == 2:
+
+        def weight_grads(member):
+            return moe_weight_backward(
+                expert_rows,
+                expert_dy,
+                lax.dynamic_index_in_dim(own_in, member, 0, keepdims=False),
+                lax.dynamic_index_in_dim(own_out, member, 0, keepdims=False),
+            )
+
+        theirs = weight_grads(1 - dp_place)
+        away = [swap_dp(t.astype(jnp.bfloat16)) for t in theirs]
+        mine = weight_grads(dp_place)
+        mine, away, arrived = together((mine, away, arrived))
+        d_in, d_out = [(m + t.astype(FULLTYPE))[None] for m, t in zip(mine, away)]
+    else:
+        d_in, d_out = moe_weight_backward(
+            expert_rows,
+            expert_dy,
+            jnp.swapaxes(own_in, 0, 1).reshape(D, groups * width),
+            own_out.reshape(groups * width, D),
         )
-
+        d_in, d_out = (
+            lax.psum_scatter(
+                value[None].astype(jnp.bfloat16), "dp", scatter_dimension=axis, tiled=True
+            ).astype(FULLTYPE)
+            for value, axis in ((d_in, 2), (d_out, 1))
+        )
+    own_sum = jnp.sum(arrived.astype(FULLTYPE), 0)
+    dense_grad = lax.dynamic_slice_in_dim(
+        join_dp(own_sum, dp_place).reshape(-1), offset, shard
+    )
     sums = sum_all(
-        jnp.concatenate(
-            [
-                local.reshape(1),
-                jnp.sum(block_sums(dense_grad, d_in, d_out)).reshape(1),
-                block_sums(dense_weight, expert_in, expert_out),
-            ]
-        )
+        placed(local, 0, 2 + block_count)
+        + placed(jnp.sum(block_sums(dense_grad, d_in, d_out)), 1, 2 + block_count)
+        + jnp.pad(weight_sums, (2, 0))
     )
     loss, grad_total, weight_total = (sums[0] / total, sums[1], sums[2:])
     grad_norm = jnp.sqrt(grad_total)
@@ -757,8 +1192,10 @@
     weight_norm = jnp.sqrt(weight_total)
     update_norm = jnp.sqrt(update_total)
     ratio = weight_norm / (update_norm + EPS_NORM)
-    whole_hot = segment_onehot(ep_place * shard, shard, experts)
-    dense_ratio = jnp.sum(jnp.where(whole_hot, ratio[None, :14], 0.0), 1)
+    whole_index = jnp.arange(shard, dtype=jnp.int32)
+    dense_ratio = jnp.broadcast_to(jnp.take(ratio, first_block), (shard,))
+    for k in range(1, span):
+        dense_ratio = jnp.where(whole_index >= starts[k], jnp.take(ratio, jnp.minimum(first_block + k, block_count - 1)), dense_ratio)
     in_ratio = lax.dynamic_index_in_dim(ratio, 14 + own_expert, 0, keepdims=False)
     out_ratio = lax.dynamic_index_in_dim(ratio, 14 + experts + own_expert, 0, keepdims=False)
 

time: 1690 us -> 978 us (0.58)
  waiting for transfers between devices: 502 us -> 208 us
  local copies, waits for them, and re-layouts: 303 us -> 45.4 us
  Pallas kernels: 262 us -> 498 us
  matrix products: 189 us -> 0.47 us
  blocking collectives: 110 us -> 0 us
  other arithmetic: 183 us -> 85.4 us
    pallas_call x0 -> x7, Pallas kernels: none -> 229 us  [the longest x6 211 us: gridded(): pl.pallas_call(kernel, grid=(steps,), out_shape=outs, in_specs=in_specs,...]
    unnamed x7 -> x3, waiting for transfers between devices: 175 us -> 0.05 us
    all_to_all x1 -> x0, blocking collectives: 110 us -> none  [to_experts(): return lax.all_to_all(buffer, 'ep', split_axis=0, concat_axis=0, tiled=True)]
    dot_general x4 -> x1, matrix products: 106 us -> 0.47 us  [plain(): return jnp.dot(left, right, preferred_element_type=FULLTYPE)]
    gather x4 -> x0, local copies, waits for them, and re-layouts: 84.6 us -> none  [the longest x2 34.5 us: combine(): return summed[slot].reshape(seq, TOP, D).astype(FULLTYPE)]
    dot_general x6 -> x0, matrix products: 82.6 us -> none  [the longest x3 52.2 us: right_t(): lax.dot_general(left, right, (((1,), (1,)), ((), ())), preferred_element_...]
    all_to_all x2 -> x0, waiting for transfers between devices: 78.6 us -> none  [from_experts(): lax.all_to_all(buffer.astype(jnp.bfloat16), 'ep', split_axis=0, concat_ax...]
    all_gather x3, waiting for transfers between devices: 92.4 us -> 160 us  [the longest x1 84.1 us: per_device(): all_out = lax.all_gather(low_out, ('ep', 'dp'))]
  transfers between devices with their start and end apart: 27 -> 29, of which waited for: 21 -> 20; matrix products, arithmetic and copies ran while one was open for 10% -> 5% of each run, Pallas kernels for 0% -> 46%
where the time goes in v2:
time: 978 us; the launch traced here: 973 us
  Pallas kernels  498 us (51%)
  waiting for transfers between devices  208 us (21%)
  starting transfers between devices  97.6 us (10%)
  other arithmetic  85.4 us (9%)
  local copies, waits for them, and re-layouts  45.4 us (5%)
  between operations  38.8 us (4%)
    pallas_call x8, Pallas kernels, local_call(): pl.pallas_call(kernel, out_shape=outs, in_specs=in_vmem(len(args)), out_s...  269 us
    pallas_call x6, Pallas kernels, gridded(): pl.pallas_call(kernel, grid=(steps,), out_shape=outs, in_specs=in_specs,...  211 us
    all_gather x1, waiting for transfers between devices, per_device(): all_out = lax.all_gather(low_out, ('ep', 'dp'))  84.1 us
    all_gather x1, waiting for transfers between devices, per_device(): all_in = lax.all_gather(low_in, ('ep', 'dp'))  50.9 us
    ppermute x15, starting transfers between devices, sum_all(): lax.ppermute(value, axis, [(i, i ^ step) for i in range(count)])  48.9 us
    all_to_all x7, starting transfers between devices, to_experts(): return lax.all_to_all(buffer, 'ep', split_axis=0, concat_axis=0, tiled=True)  48 us
    all_to_all x7, waiting for transfers between devices, to_experts(): return lax.all_to_all(buffer, 'ep', split_axis=0, concat_axis=0, tiled=True)  25.2 us
    all_gather x1, waiting for transfers between devices, per_device(): parts = lax.all_gather(own_part, ('ep', 'dp')).reshape(ep_count, rows, 128)  25.1 us
  transfers between devices with their start and end apart: 29, of which 20 were waited for; matrix products, arithmetic and copies ran while one was open for 5% of the time, Pallas kernels for 46%

profile of v2, /device:TPU:0, one launch (start us, length us, event | category | flops | bytes accessed | tf_op | source)
XLA Modules:
  0.0 973.1 jit_solution(10639757253849769616)
XLA Ops:
  8.6 5.2 dynamic_update_slice.3
  34.9 5.1 select_add_fusion.1
  40.6 12.2 %select_reduce_fusion = f32[1024,40]{1,0:T(8,128)S(1)} fusion(f32[1024,256]{1,0:T(8,128)S(1)} %get-tuple-element.407, s32[1024,256]{1,0:T(8,128)S(1)} %copy-done.38), kind=kLoop, calls=%fused_computation | loop fusion | flops 31416320 | bytes 2260992 | tf_op jit(solution)/shard_map/reduce_sum | solution.py:1035
  54.1 3.9 collective-permute-start.1
  58.8 3.4 collective-permute-start.2
  63.0 3.4 collective-permute-start.3
  67.2 4.4 collective-permute-start.4
  72.5 25.1 %all-gather.4.cloned.1.call-done = bf16[32,1104,128]{2,1,0:T(8,128)(2,1)} async-done(((bf16[1,1104,128]{2,1,0:T(8,128)(2,1)}), bf16[32,1104,128]{2,1,0:T(8,128)(2,1)}) %all-gather.4.cloned.1.call-update) | async-done | bytes 9043984 | tf_op jit(solution)/shard_map/all_gather | solution.py:1012
  97.6 11.5 %shard_map.367 = (bf16[768,384]{1,0:T(8,128)(2,1)}, bf16[384,1152]{1,0:T(8,128)(2,1)}, bf16[384,1152]{1,0:T(8,128)(2,1)}, bf16[384,1152]{1,0:T(8,128)(2,1)}, bf1...) custom-call(bf16[16,2208,128]{2,1,0:T(8,128)(2,1)} %bitcast.138), custom_call_target="tpu_custom_call" | custom-call | bytes 18072576 | tf_op jit(solution)/shard_map/pallas_call | solution.py:197
  113.4 34.8 %shard_map.368 = (f32[1024,384]{1,0:T(8,128)}, f32[1024,384]{1,0:T(8,128)}, bf16[1024,384]{1,0:T(8,128)(2,1)}, bf16[1024,1152]{1,0:T(8,128)(2,1)}, bf16[1024,384...) custom-call(bf16[1024,768]{1,0:T(8,128)(2,1)} %refs_15_.1, ...), custom_call_target="tpu_custom_call" | custom-call | flops 6845104128 | bytes 23838720 | tf_op jit(solution)/shard_map/pallas_call | solution.py:197
  148.2 25.4 %shard_map.369 = (f32[1024,384]{1,0:T(8,128)}, bf16[1024,384]{1,0:T(8,128)(2,1)}, bf16[1024,1152]{1,0:T(8,128)(2,1)}, bf16[1024,384]{1,0:T(8,128)(2,1)}, f32[8,1024]{1,0:T(8,128)}) custom-call(f32[1024,384]{1,0:T(8,128)} %get-tuple-element.134.refs_0_.refs_1_, bf16[384,1152]{1,0:T(8,128)(2,1)} %get-tuple-element.135.refs_1_.refs_6_, ...), custom_call_target="tpu_custom_call" | custom-call | flops 4429185024 | bytes 8306688 | tf_op jit(solution)/shard_map/pallas_call | solution.py:197
  173.7 50.9 %all-gather.6.cloned.1.call-done = bf16[32,384,768]{2,1,0:T(8,128)(2,1)} async-done(((bf16[1,384,768]{2,1,0:T(8,128)(2,1)}), bf16[32,384,768]{2,1,0:T(8,128)(2,1)}) %all-gather.6.cloned.1.call-update) | async-done | bytes 18874384 | tf_op jit(solution)/shard_map/all_gather | solution.py:1014
  224.6 42.3 %shard_map.370 = (f32[1024,16]{1,0:T(8,128)}, f32[16,1024,128]{2,1,0:T(8,128)}, f32[16,1024,128]{2,1,0:T(8,128)}, bf16[6144,384]{1,0:T(8,128)(2,1)}, bf16[6144,1536]{1,0:T(8,128)(2,1)}, /*index=5*/f32[6144,1536]{1,0:T(8,128)}) custom-call(s32[16]{0:T(128)} %convert_element_type.81.loads, bf16[1024,384]{1,0:T(8,128)(2,1)} %get-tuple-element.138.c_ref, ...), custom_call_target="tpu_custom_call" | custom-call | flops 12079595520 | bytes 97988672 | tf_op jit(solution)/shard_map/pallas_call | solution.py:661
  266.9 84.1 %all-gather.8.cloned.1.call-done = bf16[32,768,384]{2,1,0:T(8,128)(2,1)} async-done(((bf16[1,768,384]{2,1,0:T(8,128)(2,1)}), bf16[32,768,384]{2,1,0:T(8,128)(2,1)}) %all-gather.8.cloned.1.call-update) | async-done | bytes 18874384 | tf_op jit(solution)/shard_map/all_gather | solution.py:1015
  351.0 34.7 %shard_map.371 = (f32[1024,384]{1,0:T(8,128)}, bf16[6144,384]{1,0:T(8,128)(2,1)}) custom-call(s32[16]{0:T(128)} %convert_element_type.81.loads, f32[1024,384]{1,0:T(8,128)} %get-tuple-element.137.mid_ref.refs_2_, f32[16,1024,128]{2,1,0:T(8,128)} %get-tuple-element.141.spread_place, f32[16,1024,128]{2,1,0:T(8,128)} %get-tuple-element.142.spread_gate, ...), custom_call_target="tpu_custom_call" | custom-call | flops 12079595520 | bytes 62390336 | tf_op jit(solution)/shard_map/pallas_call | solution.py:661
  388.5 3.8 all-to-all-start
  392.9 33.3 %shard_map.372 = (f32[1024,384]{1,0:T(8,128)}, bf16[1024,384]{1,0:T(8,128)(2,1)}, bf16[1024,1152]{1,0:T(8,128)(2,1)}, bf16[1024,384]{1,0:T(8,128)(2,1)}, f32[8,1...) custom-call(f32[1024,384]{1,0:T(8,128)} %get-tuple-element.146.refs_0_.refs_1_, ...), custom_call_target="tpu_custom_call" | custom-call | flops 6845104128 | bytes 21676032 | tf_op jit(solution)/shard_map/pallas_call | solution.py:197
  426.6 3.3 slice.188
  429.9 8.3 all-to-all-start.1
  442.0 6.9 shard_map.373
  448.9 55.9 %shard_map.374 = (f32[384,1152]{1,0:T(8,128)}, f32[384,384]{1,0:T(8,128)}, f32[8,384]{1,0:T(8,128)}, f32[384,1536]{1,0:T(8,128)}, f32[1536,384]{1,0:T(8,128)}, /*index=5*/f32[1024,384]{1,0:T(8,128)}) custom-call(f32[1024,384]{1,0:T(8,128)} %get-tuple-element.161.refs_0_, f32[1024,384]{1,0:T(8,128)} %get-tuple-element.146.refs_0_.refs_1_, ...), custom_call_target="tpu_custom_call" | custom-call | flops 15300820992 | bytes 30339072 | tf_op jit(solution)/shard_map/pallas_call | solution.py:197
  504.8 3.3 slice.189
  508.1 7.4 all-to-all-start.2
  515.6 35.0 %shard_map.375 = (f32[384,16]{1,0:T(8,128)}, f32[1024,384]{1,0:T(8,128)}, bf16[6144,384]{1,0:T(8,128)(2,1)}) custom-call(s32[16]{0:T(128)} %convert_element_type.81.loads, f32[1024,384]{1,0:T(8,128)} %get-tuple-element.173.grad_ref.refs_0_, bf16[1024,384]{1,0:T(8,128)(2,1)} %get-tuple-element.138.c_ref, bf16[384,16]{1,0:T(8,128)(2,1)} %dynamic-slice_bitcast_fusion.4.router, ...), custom_call_target="tpu_custom_call" | custom-call | flops 9663676416 | bytes 30314560 | tf_op jit(solution)/shard_map/pallas_call | solution.py:661
  550.6 3.3 slice.190
  554.0 7.2 all-to-all-start.3
  561.2 44.6 %shard_map.376.refs_10_ = f32[1024,384]{1,0:T(8,128)} custom-call(s32[16]{0:T(128)} %convert_element_type.81.loads, f32[1024,384]{1,0:T(8,128)} %get-tuple-element.180.start_ref, f32[16,1024,128]{2,1,0:T(8,128)} %get-tuple-element.141.spread_place, bf16[16,2,384,768]{3,2,1,0:T(8,128)(2,1)} %bitcast.133, bf16[16,1536,384]{2,1,0:T(8,128)(2,1)} %bitcast.130, ...), custom_call_target="tpu_custom_call" | custom-call | flops 19327352832 | bytes 91750464 | tf_op jit(solution)/shard_map/pallas_call | solution.py:661
  605.8 3.4 slice.191
  609.2 6.8 all-to-all-start.4
  616.0 42.1 %shard_map.377 = (f32[384,1152]{1,0:T(8,128)}, f32[384,384]{1,0:T(8,128)}, f32[8,384]{1,0:T(8,128)}, f32[1024,384]{1,0:T(8,128)}) custom-call(f32[1024,384]{1,0:T(8,128)} %get-tuple-element.173.grad_ref.refs_0_, f32[1024,384]{1,0:T(8,128)} %get-tuple-element.134.refs_0_.refs_1_, f32[1024,384]{1,0:T(8,128)} %get-tuple-element.137.mid_ref.refs_2_, ...), custom_call_target="tpu_custom_call" | custom-call | flops 10468982784 | bytes 14610432 | tf_op jit(solution)/shard_map/pallas_call | solution.py:197
  658.1 3.4 slice.192
  661.5 7.2 all-to-all-start.5
  670.0 58.7 %shard_map.378 = (f32[384,1152]{1,0:T(8,128)}, f32[384,384]{1,0:T(8,128)}, f32[8,384]{1,0:T(8,128)}, f32[384,1536]{1,0:T(8,128)}, f32[1536,384]{1,0:T(8,128)}, /*index=5*/f32[768,384]{1,0:T(8,128)}) custom-call(f32[1024,384]{1,0:T(8,128)} %get-tuple-element.191.refs_0_, f32[1024,384]{1,0:T(8,128)} %get-tuple-element.192.refs_1_, ...), custom_call_target="tpu_custom_call" | custom-call | flops 15904800768 | bytes 31518720 | tf_op jit(solution)/shard_map/pallas_call | solution.py:197
  728.7 17.5 %shard_map.381 = (f32[1,16,1104,128]{3,2,1,0:T(8,128)}, bf16[1,16,1104,128]{3,2,1,0:T(8,128)(2,1)}) custom-call(s32[1]{0:T(128)} %bitcast.56.place_ref, f32[768,384]{1,0:T(8,128)} %get-tuple-element.207.refs_0_, f32[384,1152]{1,0:T(8,128)} %get-tuple-element.208.refs_1_, f32[384,1152]{1,0:T(8,128)} %get-tuple-element.209.refs_2_, ...), custom_call_target="tpu_custom_call" | custom-call | bytes 31469572 | tf_op jit(solution)/shard_map/pallas_call | solution.py:896
  746.3 7.8 collective-permute-done.7
  754.2 6.8 fusion
  760.9 7.3 all-to-all-start.6
  772.9 27.2 %shard_map.380 = (f32[384,768]{1,0:T(8,128)}, f32[768,384]{1,0:T(8,128)}) custom-call(bf16[2048,384]{1,0:T(8,128)(2,1)} %bitcast.144, bf16[2048,384]{1,0:T(8,128)(2,1)} %bitcast.146, bf16[2048,384]{1,0:T(8,128)(2,1)} %bitcast.148, bf16[2048,384]{1,0:T(8,128)(2,1)} %bitcast.150, bf16[2048,384]{1,0:T(8,128)(2,1)} %bitcast.152, bf16[2048,384]{1,0:T(8,128)(2,1)} %bitcast.154, ...), custom_call_target="tpu_custom_call" | custom-call | flops 18119393280 | bytes 12976128 | tf_op jit(solution)/shard_map/pallas_call | solution.py:661
  802.2 27.4 %shard_map.379 = (f32[384,768]{1,0:T(8,128)}, f32[768,384]{1,0:T(8,128)}) custom-call(bf16[2048,384]{1,0:T(8,128)(2,1)} %bitcast.145, bf16[2048,384]{1,0:T(8,128)(2,1)} %bitcast.147, bf16[2048,384]{1,0:T(8,128)(2,1)} %bitcast.149, bf16[2048,384]{1,0:T(8,128)(2,1)} %bitcast.151, bf16[2048,384]{1,0:T(8,128)(2,1)} %bitcast.153, bf16[2048,384]{1,0:T(8,128)(2,1)} %bitcast.155, ...), custom_call_target="tpu_custom_call" | custom-call | flops 18119393280 | bytes 12976128 | tf_op jit(solution)/shard_map/pallas_call | solution.py:661
  829.7 24.8 %all-to-all-done.6 = bf16[16,1104,128]{2,1,0:T(8,128)(2,1)} async-done(((bf16[16,1104,128]{2,1,0:T(8,128)(2,1)}), bf16[16,1104,128]{2,1,0:T(8,128)(2,1)}, u32[]{:S(2)}, u32[]{:S(2)}) %all-to-all-start.6) | async-done | bytes 4522016 | tf_op jit(solution)/shard_map/all_to_all | solution.py:944
  854.5 3.9 convert_reduce_fusion
  865.2 5.1 add_reduce_fusion
  877.3 6.7 collective-permute-start.11
  885.6 11.7 %collective-permute-start.12 = (f32[48]{0:T(128)S(1)}, f32[48]{0:T(128)S(1)}, u32[]{:S(2)}, u32[]{:S(2)}) collective-permute-start(f32[48]{0:T(128)S(1)} %add.365), channel_id=1, source_target_pairs={{0,8},{2,10},{4,12},{6,14},{8,0},{10,2},{12,4},{14,6},{16,24},{18,... | collective-permute-start | bytes 584 | tf_op jit(solution)/shard_map/ppermute | solution.py:938
  904.6 4.3 multiply_add_fusion.6
  917.4 4.4 select_add_fusion
  923.0 4.4 fusion.41
  931.0 4.4 fusion.43
  (205 shorter events, 89.9 us)
Async XLA Ops:
  7.2 90.4 %all-gather.4.cloned.1.call-start = ((), (), s32[]{:S(2)}) async-start(), calls=%async_computation.7 | async-start | bytes 9326592 | tf_op jit(solution)/shard_map/all_gather | solution.py:1012
  8.6 6.1 copy-start.2
  14.6 210.0 %all-gather.6.cloned.1.call-start = ((), (), s32[]{:S(2)}) async-start(), calls=%async_computation.8 | async-start | bytes 19464192 | tf_op jit(solution)/shard_map/all_gather | solution.py:1014
  16.4 334.6 %all-gather.8.cloned.1.call-start = ((), (), s32[]{:S(2)}) async-start(), calls=%async_computation.9 | async-start | bytes 19464192 | tf_op jit(solution)/shard_map/all_gather | solution.py:1015
  18.1 9.2 copy-start.43
  18.2 22.4 %copy-start.38 = (s32[1024,256]{1,0:T(8,128)S(1)}, s32[1024,256]{1,0:T(8,128)}, u32[]{:S(2)}) copy-start(s32[1024,256]{1,0:T(8,128)} %param.25) | copy-start | bytes 3145732
  19.1 10.1 %copy-start.44 = (s32[18]{0:T(128)S(1)}, s32[18]{0:T(128)}, u32[]{:S(2)}) copy-start(s32[18]{0:T(128)} %constant.303.clone..sunk.10) | copy-start | bytes 220
  19.1 14.6 %copy-start = (f32[279312]{0:T(1024)S(1)}, f32[279312]{0:T(1024)}, u32[]{:S(2)}) copy-start(f32[279312]{0:T(1024)} %param.30) | copy-start | bytes 3351748
  19.1 33.7 %collective-permute-start = (f32[1]{0:T(128)}, f32[1]{0:T(128)}, u32[]{:S(2)}, u32[]{:S(2)}) collective-permute-start(f32[1]{0:T(128)} %bitcast.2), channel_id=1, source_target_pairs={{0,1},{1,0},{2,3},{3,2},{4,5},{5,4},{6,7},{7,6},{8,9},{9,8},{10,11... | collective-permute-start | bytes 20 | tf_op jit(solution)/shard_map/ppermute | solution.py:938
  54.1 4.0 collective-permute-start.1
  58.8 3.6 collective-permute-start.2
  63.0 3.6 collective-permute-start.3
  67.2 4.6 collective-permute-start.4
  388.5 38.1 %all-to-all-start = ((bf16[16,128,384]{2,1,0:T(8,128)(2,1)}), bf16[16,128,384]{2,1,0:T(8,128)(2,1)S(1)}, u32[]{:S(2)}, u32[]{:S(2)}) async-start(bf16[16,128,384]{2,1,0:T(8,128)(2,1)} %slice.184), calls=%async_computation | async-start | bytes 3145728 | tf_op jit(solution)/shard_map/all_to_all | solution.py:944
  429.9 10.2 %copy-start.42 = (f32[1024]{0:T(1024)S(1)}, f32[1024]{0:T(1024)}, u32[]{:S(2)}) copy-start(f32[1024]{0:T(1024)} %compare_select_fusion) | copy-start | bytes 12292
  429.9 74.9 %all-to-all-start.1 = ((bf16[16,128,384]{2,1,0:T(8,128)(2,1)}), bf16[16,128,384]{2,1,0:T(8,128)(2,1)S(1)}, u32[]{:S(2)}, u32[]{:S(2)}) async-start(bf16[16,128,384]{2,1,0:T(8,128)(2,1)} %slice.188), calls=%async_computation.1 | async-start | bytes 3145728 | tf_op jit(solution)/shard_map/all_to_all | solution.py:944
  508.1 42.5 %all-to-all-start.2 = ((bf16[16,128,384]{2,1,0:T(8,128)(2,1)}), bf16[16,128,384]{2,1,0:T(8,128)(2,1)S(1)}, u32[]{:S(2)}, u32[]{:S(2)}) async-start(bf16[16,128,384]{2,1,0:T(8,128)(2,1)} %slice.189), calls=%async_computation.2 | async-start | bytes 3145728 | tf_op jit(solution)/shard_map/all_to_all | solution.py:944
  554.0 51.8 %all-to-all-start.3 = ((bf16[16,128,384]{2,1,0:T(8,128)(2,1)}), bf16[16,128,384]{2,1,0:T(8,128)(2,1)S(1)}, u32[]{:S(2)}, u32[]{:S(2)}) async-start(bf16[16,128,384]{2,1,0:T(8,128)(2,1)} %slice.190), calls=%async_computation.3 | async-start | bytes 3145728 | tf_op jit(solution)/shard_map/all_to_all | solution.py:944
  609.2 49.0 %all-to-all-start.4 = ((bf16[16,128,384]{2,1,0:T(8,128)(2,1)}), bf16[16,128,384]{2,1,0:T(8,128)(2,1)S(1)}, u32[]{:S(2)}, u32[]{:S(2)}) async-start(bf16[16,128,384]{2,1,0:T(8,128)(2,1)} %slice.191), calls=%async_computation.4 | async-start | bytes 3145728 | tf_op jit(solution)/shard_map/all_to_all | solution.py:944
  661.5 7.2 copy-start.40
  661.5 7.4 copy-start.39
  661.5 67.2 %all-to-all-start.5 = ((bf16[16,128,384]{2,1,0:T(8,128)(2,1)}), bf16[16,128,384]{2,1,0:T(8,128)(2,1)S(1)}, u32[]{:S(2)}, u32[]{:S(2)}) async-start(bf16[16,128,384]{2,1,0:T(8,128)(2,1)} %slice.192), calls=%async_computation.5 | async-start | bytes 3145728 | tf_op jit(solution)/shard_map/all_to_all | solution.py:944
  728.7 17.6 %copy-start.28 = (bf16[16,128,384]{2,1,0:T(8,128)(2,1)}, bf16[16,128,384]{2,1,0:T(8,128)(2,1)S(1)}, u32[]{:S(2)}) copy-start(bf16[16,128,384]{2,1,0:T(8,128)(2,1)S(1)} %all-to-all-done.5) | copy-start | bytes 4718596
  746.3 7.9 collective-permute-start.7
  760.9 93.6 %all-to-all-start.6 = ((bf16[16,1104,128]{2,1,0:T(8,128)(2,1)}), bf16[16,1104,128]{2,1,0:T(8,128)(2,1)}, u32[]{:S(2)}, u32[]{:S(2)}) async-start(bf16[16,1104,128]{2,1,0:T(8,128)(2,1)} %fusion), calls=%async_computation.6 | async-start | bytes 9043968 | tf_op jit(solution)/shard_map/all_to_all | solution.py:944
  801.5 28.1 %collective-permute-start.5 = (bf16[384,768]{1,0:T(8,128)(2,1)S(1)}, bf16[384,768]{1,0:T(8,128)(2,1)S(1)}, u32[]{:S(2)}, u32[]{:S(2)}) collective-permute-start(bf16[384,768]{1,0:T(8,128)(2,1)S(1)} %convert_element_type.86), channel_id=1, source_target_pairs={{0,1},{1,0},{2,3},{3,2},{4,5},{5,4},{6,7},{7,6},{8,9},{9,8},{10,11... | collective-permute-start | bytes 1769480 | tf_op jit(solution)/shard_map/ppermute | solution.py:912
  801.8 27.9 %collective-permute-start.6 = (bf16[768,384]{1,0:T(8,128)(2,1)S(1)}, bf16[768,384]{1,0:T(8,128)(2,1)S(1)}, u32[]{:S(2)}, u32[]{:S(2)}) collective-permute-start(bf16[768,384]{1,0:T(8,128)(2,1)S(1)} %convert_element_type.87), channel_id=1, source_target_pairs={{0,1},{1,0},{2,3},{3,2},{4,5},{5,4},{6,7},{7,6},{8,9},{9,8},{10,11... | collective-permute-start | bytes 1769480 | tf_op jit(solution)/shard_map/ppermute | solution.py:912
  829.7 31.0 %copy-start.19 = (bf16[384,768]{1,0:T(8,128)(2,1)}, bf16[384,768]{1,0:T(8,128)(2,1)S(1)}, u32[]{:S(2)}) copy-start(bf16[384,768]{1,0:T(8,128)(2,1)S(1)} %collective-permute-done.5) | copy-start | bytes 1769476
  829.7 30.1 %copy-start.21 = (bf16[768,384]{1,0:T(8,128)(2,1)}, bf16[768,384]{1,0:T(8,128)(2,1)S(1)}, u32[]{:S(2)}) copy-start(bf16[768,384]{1,0:T(8,128)(2,1)S(1)} %collective-permute-done.6) | copy-start | bytes 1769476
  858.4 3.2 collective-permute-start.8
  862.9 7.4 copy-start.45
  862.9 7.4 copy-start.46
  862.9 41.6 %copy-start.1 = (f32[279312]{0:T(1024)S(1)}, f32[279312]{0:T(1024)}, u32[]{:S(2)}) copy-start(f32[279312]{0:T(1024)} %param.30) | copy-start | bytes 3351748
  871.0 1.2 collective-permute-start.9
  873.0 4.3 collective-permute-start.10
  877.3 8.3 collective-permute-start.11
  885.6 13.2 %collective-permute-start.12 = (f32[48]{0:T(128)S(1)}, f32[48]{0:T(128)S(1)}, u32[]{:S(2)}, u32[]{:S(2)}) collective-permute-start(f32[48]{0:T(128)S(1)} %add.365), channel_id=1, source_target_pairs={{0,8},{2,10},{4,12},{6,14},{8,0},{10,2},{12,4},{14,6},{16,24},{18,... | collective-permute-start | bytes 584 | tf_op jit(solution)/shard_map/ppermute | solution.py:938
  898.8 4.4 collective-permute-start.13
  904.5 6.6 copy-start.5
  904.6 6.5 copy-start.13
  904.6 6.5 copy-start.22
  904.6 6.5 copy-start.32
  904.6 6.5 copy-start.33
  921.8 1.2 collective-permute-start.14
  927.4 3.6 collective-permute-start.15
  935.4 3.6 collective-permute-start.16
  939.0 3.5 collective-permute-start.17
  942.6 4.4 collective-permute-start.18
  (29 other events, 68.4 us)
Sparse Core Ops, SparseCore 0:
  14.7 82.7 all-gather.3
  101.0 123.5 all-gather.5
  228.1 122.9 all-gather.7

commit v3 on v2

--- a/solution.py
+++ b/solution.py
@@ -71,6 +71,9 @@
 
 VMEM_LIMIT = 56 * 2**20
 ROWS = 256
+TILE = 32
+KEYS = 64
+QUERIES = 512
 NEG = -1e30
 
 
@@ -110,7 +113,21 @@
     return [jnp.where((lane < HD) == (h == 0), scale, 0.0).astype(LOWTYPE) for h in (0, 1)]
 
 
-def attend_rows(qkv_ref, bias_ref, o_ref, lse_ref):
+def beside_head(head, own, extras):
+    lane = lax.broadcasted_iota(jnp.int32, own.shape, 1)
+    value = own.astype(FULLTYPE) * half_masks(1.0)[head].astype(FULLTYPE)
+    for k, extra in enumerate(extras):
+        value = jnp.where(lane == HD * (1 - head) + k, extra, value)
+    return value.astype(LOWTYPE)
+
+
+def three_parts(column):
+    high = column.astype(LOWTYPE).astype(FULLTYPE)
+    middle = (column - high).astype(LOWTYPE).astype(FULLTYPE)
+    return [high, middle, column - high - middle]
+
+
+def attend_rows(qkv_ref, bias_ref, o_ref, aug_ref, keys_ref, s_ref, p_ref):
     seq = qkv_ref.shape[0]
     masks = half_masks(SCALE)
     lane = lax.broadcasted_iota(jnp.int32, (ROWS, 128), 1)
@@ -118,21 +135,37 @@
     for pair in range(HEADS // 2):
         cols = pl.ds(pair * 128, 128)
 
+        def prepare(i, carry, pair=pair):
+            rows = rows_of(i)
+            keys = qkv_ref[rows, pl.ds(D + pair * 128, 128)]
+            for h in (0, 1):
+                keys_ref[h, rows, :] = beside_head(h, keys, [bias_ref[rows, :]])
+            return carry
+
+        lax.fori_loop(0, seq // ROWS, prepare, 0)
+
         def body(i, carry, pair=pair, cols=cols):
             rows = rows_of(i)
             query = qkv_ref[rows, cols]
-            keys = qkv_ref[:, pl.ds(D + pair * 128, 128)]
             values = qkv_ref[:, pl.ds(2 * D + pair * 128, 128)]
             outs = []
             for h in (0, 1):
-                s = right_t(query * masks[h], keys) + bias_ref[...]
-                top = jnp.max(s, -1, keepdims=True)
-                e = jnp.exp(s - top)
-                total = jnp.sum(e, -1, keepdims=True)
-                probs = (e * (1.0 / total)).astype(LOWTYPE)
-                outs.append(plain(probs, values))
-                lse = jnp.broadcast_to(top + jnp.log(total), (ROWS, 128)).T
-                lse_ref[pl.ds(2 * pair + h, 1), rows] = lse[0:1, :]
+                s_ref[h] = right_t(beside_head(h, query * masks[h], [1.0]), keys_ref[h])
+            for h in (0, 1):
+                for first in range(0, ROWS, TILE):
+                    s = s_ref[h, first : first + TILE, :]
+                    top = jnp.max(s, -1, keepdims=True)
+                    e = jnp.exp(s - top)
+                    total = jnp.sum(e, -1, keepdims=True)
+                    p_ref[h, first : first + TILE, :] = (e * (1.0 / total)).astype(LOWTYPE)
+                    at = pl.ds(pl.multiple_of(i * ROWS + first, TILE), TILE)
+                    aug_ref[at, pl.ds((2 * pair + h) * 128, 128)] = beside_head(
+                        h,
+                        query[first : first + TILE] * masks[h],
+                        [1.0] + three_parts(-(top + jnp.log(total))),
+                    )
+            for h in (0, 1):
+                outs.append(plain(p_ref[h], values))
             o_ref[rows, cols] = jnp.where(lane < HD, outs[0], outs[1]).astype(LOWTYPE)
             return carry
 
@@ -153,10 +186,11 @@
         x_ref = refs.pop(0)
     else:
         x_ref = x_in
-    mid_ref, c_ref, qkv_ref, o_ref, lse_ref = refs[:5]
+    mid_ref, c_ref, qkv_ref, o_ref, aug_ref = refs[:5]
     refs = refs[5:]
     if has_ff:
-        next_ref, act_ref, slope_ref = refs
+        next_ref, act_ref, slope_ref = refs[:3]
+    keys_ref, s_ref, p_ref = refs[-3:]
     seq = x_ref.shape[0]
 
     def project(i, carry):
@@ -168,8 +202,7 @@
         return carry
 
     lax.fori_loop(0, seq // ROWS, project, 0)
-    lse_ref[...] = jnp.zeros_like(lse_ref)
-    attend_rows(qkv_ref, bias, o_ref, lse_ref)
+    attend_rows(qkv_ref, bias, o_ref, aug_ref, keys_ref, s_ref, p_ref)
 
     def finish(i, carry):
         rows = rows_of(i)
@@ -219,7 +252,7 @@
         shaped((seq, D), LOWTYPE),
         shaped((seq, 3 * D), LOWTYPE),
         shaped((seq, D), LOWTYPE),
-        shaped((8, seq), FULLTYPE),
+        shaped((seq, 128 * HEADS), LOWTYPE),
     ]
     if has_ff:
         outs += [
@@ -228,42 +261,68 @@
             shaped((seq, FF), FULLTYPE),
         ]
     flops = 2 * seq * D * (4 * D + 4 * seq + 2 * FF * has_ff)
-    return local_call(functools.partial(forward_kernel, has_patch, has_ff), outs, args, flops)
-
-
-def attend_pull(qkv_ref, do_ref, lse_ref, valid_ref, dqkv_ref, dk_ref, dv_ref):
+    kernel = functools.partial(forward_kernel, has_patch, has_ff)
+    scratch = [
+        pltpu.VMEM((2, seq, 128), LOWTYPE),
+        pltpu.VMEM((2, ROWS, seq), FULLTYPE),
+        pltpu.VMEM((2, ROWS, seq), LOWTYPE),
+    ]
+    return local_call(kernel, outs, args, flops, scratch)
+
+
+def attend_pull(qkv_ref, o_ref, do_ref, aug_ref, valid_ref, dqkv_ref, dk_ref, dv_ref, sides):
     seq = qkv_ref.shape[0]
-    scaled, ones = (half_masks(SCALE), half_masks(1.0))
-    lane = lax.broadcasted_iota(jnp.int32, (ROWS, 128), 1)
+    keys_ref, values_ref, across_ref, s_ref, dp_ref, p_ref, ds_ref = sides
+    ones = half_masks(1.0)
 
     for pair in range(HEADS // 2):
         cols = pl.ds(pair * 128, 128)
         dk_ref[...] = jnp.zeros_like(dk_ref)
         dv_ref[...] = jnp.zeros_like(dv_ref)
 
+        def prepare(i, carry, pair=pair):
+            rows = rows_of(i)
+            keys = qkv_ref[rows, pl.ds(D + pair * 128, 128)]
+            values = qkv_ref[rows, pl.ds(2 * D + pair * 128, 128)]
+            across_ref[:, rows] = keys.astype(FULLTYPE).T.astype(LOWTYPE)
+            for h in (0, 1):
+                keys_ref[h, rows, :] = beside_head(h, keys, [valid_ref[rows, :], 1.0, 1.0, 1.0])
+                values_ref[h, rows, :] = beside_head(h, values, [1.0, 1.0, 1.0])
+            return carry
+
+        lax.fori_loop(0, seq // ROWS, prepare, 0)
+
         def body(i, carry, pair=pair, cols=cols):
-            rows = rows_of(i)
-            query = qkv_ref[rows, cols]
-            keys = qkv_ref[:, pl.ds(D + pair * 128, 128)]
-            values = qkv_ref[:, pl.ds(2 * D + pair * 128, 128)]
+            rows = rows_of(i, QUERIES)
             d_out = do_ref[rows, cols]
+            both = d_out.astype(FULLTYPE) * o_ref[rows, cols].astype(FULLTYPE)
             d_query = []
             for h in (0, 1):
-                own_q = query * scaled[h]
-                own_d = d_out * ones[h]
-                s = right_t(keys, own_q) + valid_ref[...]
-                probs = jnp.exp(s - lse_ref[pl.ds(2 * pair + h, 1), rows])
-                dv_ref[...] += plain(probs.astype(LOWTYPE), own_d)
-                d_probs = right_t(values, own_d)
-                delta = jnp.sum(probs * d_probs, 0, keepdims=True)
-                d_s = (probs * (d_probs - delta)).astype(LOWTYPE)
-                dk_ref[...] += plain(d_s, own_q)
-                d_query.append(left_t(d_s, keys))
-            picked = jnp.where(lane < HD, d_query[0], d_query[1]) * SCALE
-            dqkv_ref[rows, cols] = picked.astype(LOWTYPE)
+                own_q = aug_ref[rows, pl.ds((2 * pair + h) * 128, 128)]
+                s_ref[h] = right_t(keys_ref[h], own_q)
+                delta = jnp.sum(both * ones[h].astype(FULLTYPE), -1, keepdims=True)
+                own_d = beside_head(h, d_out, three_parts(-delta))
+                dp_ref[h] = right_t(values_ref[h], own_d)
+            for h in (0, 1):
+                for first in range(0, seq, KEYS):
+                    at, side = (pl.ds(first, KEYS), pl.ds(h * QUERIES, QUERIES))
+                    probs = jnp.exp(s_ref[h, at, :])
+                    p_ref[at, side] = probs.astype(LOWTYPE)
+                    ds_ref[at, side] = (probs * dp_ref[h, at, :]).astype(LOWTYPE)
+            own = [
+                aug_ref[rows, pl.ds((2 * pair + h) * 128, 128)] * ones[h] for h in (0, 1)
+            ]
+            dv_ref[...] += plain(p_ref[...], jnp.concatenate([d_out * ones[h] for h in (0, 1)]))
+            dk_ref[...] += plain(ds_ref[...], jnp.concatenate(own))
+            for h in (0, 1):
+                d_query.append(
+                    plain(across_ref[pl.ds(h * HD, HD), :], ds_ref[:, pl.ds(h * QUERIES, QUERIES)])
+                )
+            turned = jnp.concatenate(d_query).T * SCALE
+            dqkv_ref[rows, cols] = turned.astype(LOWTYPE)
             return carry
 
-        lax.fori_loop(0, seq // ROWS, body, 0)
+        lax.fori_loop(0, seq // QUERIES, body, 0)
         dqkv_ref[:, pl.ds(D + pair * 128, 128)] = dk_ref[...].astype(LOWTYPE)
         dqkv_ref[:, pl.ds(2 * D + pair * 128, 128)] = dv_ref[...].astype(LOWTYPE)
 
@@ -279,7 +338,7 @@
 
 def backward_kernel(has_patch, has_ff, *refs):
     refs = list(refs)
-    grad, x_ref, mid_ref, qkv, o_ref, lse, w_qkv, w_attn, norms, valid = refs[:10]
+    grad, x_ref, mid_ref, qkv, o_ref, aug, w_qkv, w_attn, norms, valid = refs[:10]
     refs = refs[10:]
     if has_ff:
         c_ref, act, slope, w_up, w_down = refs[:5]
@@ -298,7 +357,7 @@
     else:
         dx_ref = refs.pop(0)
     gmid, low, do_ref, dqkv, dk, dv = refs[:6]
-    refs = refs[6:]
+    sides, refs = (refs[6:13], refs[13:])
     if has_ff:
         dh_ref = refs.pop(0)
     seq = grad.shape[0]
@@ -336,7 +395,7 @@
 
     lax.fori_loop(0, blocks_count, out_pull, 0)
     weight_pull(o_ref, low, d_attn)
-    attend_pull(qkv, do_ref, lse, valid, dqkv, dk, dv)
+    attend_pull(qkv, o_ref, do_ref, aug, valid, dqkv, dk, dv, sides)
 
     def in_pull(i, carry):
         rows = rows_of(i)
@@ -368,9 +427,9 @@
 
 def layer_backward(grad, x, kept, w_qkv, w_attn, norms, valid, ff, d_c, patches):
     seq = grad.shape[0]
-    mid, c16, qkv16, o16, lse = kept[:5]
+    mid, c16, qkv16, o16, aug = kept[:5]
     has_ff, has_patch = (ff is not None, patches is not None)
-    args = [grad, x, mid, qkv16, o16, lse, w_qkv, w_attn, norms, valid]
+    args = [grad, x, mid, qkv16, o16, aug, w_qkv, w_attn, norms, valid]
     args += [c16, *kept[5:], *ff] if has_ff else [d_c]
     args += [patches] * has_patch
     outs = [
@@ -388,6 +447,13 @@
         pltpu.VMEM((seq, 3 * D), LOWTYPE),
         pltpu.VMEM((seq, 128), FULLTYPE),
         pltpu.VMEM((seq, 128), FULLTYPE),
+        pltpu.VMEM((2, seq, 128), LOWTYPE),
+        pltpu.VMEM((2, seq, 128), LOWTYPE),
+        pltpu.VMEM((128, seq), LOWTYPE),
+        pltpu.VMEM((2, seq, QUERIES), FULLTYPE),
+        pltpu.VMEM((2, seq, QUERIES), FULLTYPE),
+        pltpu.VMEM((seq, 2 * QUERIES), LOWTYPE),
+        pltpu.VMEM((seq, 2 * QUERIES), LOWTYPE),
     ] + [pltpu.VMEM((seq, FF), LOWTYPE)] * has_ff
     flops = 2 * seq * D * (8 * D + 10 * seq + 4 * FF * has_ff + PIX * has_patch)
     return local_call(
@@ -463,6 +529,14 @@
     return jnp.where(place == row, 1.0, 0.0).astype(LOWTYPE)
 
 
+def put_blocks(refs, rows):
+    for block, ref in enumerate(refs):
+        if block * SLOTS < rows.shape[0]:
+            ref[0] = rows[block * SLOTS : (block + 1) * SLOTS]
+        else:
+            ref[0] = jnp.zeros(ref.shape[1:], ref.dtype)
+
+
 def column_of(table, expert):
     lane = lax.broadcasted_iota(jnp.int32, table.shape, 1)
     return jnp.sum(jnp.where(lane == expert, table, 0.0), -1, keepdims=True)
@@ -481,10 +555,10 @@
 
 def moe_up_kernel(
     loads, c_ref, router, table, place, w_in,
-    gates_ref, spread_place, spread_gate, rows_ref, act_ref, slope_ref,
+    gates_ref, spread_place, spread_gate, act_ref, slope_ref, *rows_refs,
 ):
     expert = pl.program_id(0)
-    seq, capacity, parts = (c_ref.shape[0], rows_ref.shape[0], w_in.shape[1])
+    seq, capacity, parts = (c_ref.shape[0], act_ref.shape[0], w_in.shape[1])
     width = w_in.shape[3]
 
     @pl.when(expert == 0)
@@ -511,7 +585,7 @@
     def work(count):
         at = pl.ds(0, count)
         rows = plain(slot_select(place[0], count), c_ref[...]).astype(LOWTYPE)
-        rows_ref[at, :] = rows
+        put_blocks(rows_refs, rows)
         for part in range(parts):
             step = width // 3 if width % 384 == 0 else width
             for first in range(0, width, step):
@@ -519,8 +593,6 @@
                 units = pl.ds(part * width + first, step)
                 slope_ref[at, units] = slope
                 act_ref[at, units] = act.astype(LOWTYPE)
-        if count < capacity:
-            rows_ref[pl.ds(count, capacity - count), :] = jnp.zeros((capacity - count, D), LOWTYPE)
 
     by_load(loads[expert], capacity, work)
 
@@ -554,8 +626,9 @@
 
 def moe_gate_kernel(
     loads, grad_ref, c_ref, router, gates, place, spread_place, spread_gate, y_ref,
-    d_router, d_c, dy_ref, low_ref, dz_ref, d_gates,
+    d_router, d_c, *refs,
 ):
+    dy_refs, (low_ref, dz_ref, d_gates) = (refs[:-3], refs[-3:])
     expert = pl.program_id(0)
     seq, capacity = (grad_ref.shape[0], y_ref.shape[0])
     lane = lax.broadcasted_iota(jnp.int32, (ROWS, d_gates.shape[1]), 1)
@@ -580,9 +653,7 @@
             return carry
 
         lax.fori_loop(0, seq // ROWS, one, 0)
-        dy_ref[at, :] = plain(slot_select(place[0], count), low_ref[...]).astype(LOWTYPE)
-        if count < capacity:
-            dy_ref[pl.ds(count, capacity - count), :] = jnp.zeros((capacity - count, D), LOWTYPE)
+        put_blocks(dy_refs, plain(slot_select(place[0], count), low_ref[...]).astype(LOWTYPE))
 
     by_load(loads[expert], capacity, work)
 
@@ -601,9 +672,10 @@
         d_router[...] = left_t(c_ref[...], dz_ref[...])
 
 
-def moe_backward_kernel(loads, start_ref, spread_place, w_in, w_out, dy_ref, slope_ref, d_c, back_ref):
+def moe_backward_kernel(loads, start_ref, spread_place, w_in, w_out, slope_ref, *refs):
+    dy_refs, (d_c, back_ref) = (refs[:-2], refs[-2:])
     expert = pl.program_id(0)
-    seq, capacity, parts = (d_c.shape[0], dy_ref.shape[0], w_in.shape[1])
+    seq, capacity, parts = (d_c.shape[0], slope_ref.shape[0], w_in.shape[1])
     width = w_in.shape[3]
 
     @pl.when(expert == 0)
@@ -612,7 +684,7 @@
 
     def work(count):
         at = pl.ds(0, count)
-        d_y = dy_ref[at, :]
+        d_y = jnp.concatenate([ref[0] for ref in dy_refs[: count // SLOTS]])
         back = jnp.zeros((count, D), FULLTYPE)
         for part in range(parts):
             units = pl.ds(part * width, width)
@@ -683,6 +755,14 @@
 
 def spread_spec(seq):
     return pl.BlockSpec((1, seq, 128), lambda e: (e, 0, 0))
+
+
+def block_shapes(experts, capacity):
+    return [shaped((experts, SLOTS, D), LOWTYPE)] * (capacity // SLOTS)
+
+
+def block_specs(capacity):
+    return [pl.BlockSpec((1, SLOTS, D), lambda e: (e, 0, 0))] * (capacity // SLOTS)
 
 
 def moe_up(loads, c16, router, table, place, w_in, capacity):
@@ -698,11 +778,12 @@
             shaped((seq, experts), FULLTYPE),
             shaped((experts, seq, 128), FULLTYPE),
             shaped((experts, seq, 128), FULLTYPE),
-            shaped((experts * capacity, D), LOWTYPE),
             shaped((experts * capacity, hidden), LOWTYPE),
             shaped((experts * capacity, hidden), FULLTYPE),
-        ],
-        [whole((seq, experts)), spread_spec(seq), spread_spec(seq), per(D), per(hidden), per(hidden)],
+        ]
+        + block_shapes(experts, capacity),
+        [whole((seq, experts)), spread_spec(seq), spread_spec(seq), per(hidden), per(hidden)]
+        + block_specs(capacity),
         [loads, c16, router, table, place, w_in],
         2 * experts * capacity * D * (hidden + seq),
     )
@@ -735,9 +816,9 @@
         [
             shaped((D, experts), FULLTYPE),
             shaped((seq, D), FULLTYPE),
-            shaped((experts * capacity, D), LOWTYPE),
-        ],
-        [whole((D, experts)), whole((seq, D)), per],
+        ]
+        + block_shapes(experts, capacity),
+        [whole((D, experts)), whole((seq, D))] + block_specs(capacity),
         [loads, grad, c16, router, gates, place, spread_place, spread_gate, y16],
         4 * experts * capacity * D * seq,
         [
@@ -748,18 +829,19 @@
     )
 
 
-def moe_backward(loads, start, spread_place, w_in, w_out, dy16, slope):
+def moe_backward(loads, start, spread_place, w_in, w_out, dy, slope):
     seq, experts = (start.shape[0], w_out.shape[0])
-    capacity, hidden = (dy16.shape[0] // experts, w_out.shape[1])
+    capacity, hidden = (slope.shape[0] // experts, w_out.shape[1])
     per = lambda width: pl.BlockSpec((capacity, width), lambda e: (e, 0))
     return gridded(
         moe_backward_kernel,
         experts,
         [SCALARS, whole((seq, D)), spread_spec(seq), in_spec(w_in), out_spec(w_out)]
-        + [per(D), per(hidden)],
+        + [per(hidden)]
+        + block_specs(capacity),
         [shaped((seq, D), FULLTYPE)],
         [whole((seq, D))],
-        [loads, start, spread_place, w_in, w_out, dy16, slope],
+        [loads, start, spread_place, w_in, w_out, slope, *dy],
         2 * experts * capacity * D * (2 * hidden + seq),
         [pltpu.VMEM((capacity, D), LOWTYPE)],
     )[0]
@@ -797,7 +879,42 @@
     return max(c for c in range(16, most + 1, 16) if rows % c == 0)
 
 
-def unpack_kernel(plan, shard, parts_ref, *refs):
+def unpack_kernel(plan, shard, owners, orders, place_ref, *refs):
+    chains = len(orders)
+    own, other = (refs[:chains], refs[chains : 2 * chains])
+    refs = refs[2 * chains :]
+    outs, rest, flat = (refs[: len(plan)], refs[len(plan)], refs[len(plan) + 1])
+    sizes = [ref.shape[0] // owners for ref in own]
+    mine, core = (place_ref[0], place_ref[1])
+
+    def collect(owner, carry):
+        first = shard * owner // 128
+        last = flat[pl.ds(jnp.maximum(first, 0), 1), :]
+        shared = jnp.where(lax.rem(shard * owner, 128) == 0, 0.0, 1.0)
+        for half in (0, 1):
+            for chain, order in enumerate(orders):
+                away = jnp.bitwise_xor(mine, owner)
+                slot = sum(
+                    jnp.bitwise_and(away // bit, 1) * 2**k for k, bit in enumerate(order)
+                )
+                size, before = (sizes[chain], half * sum(sizes) + sum(sizes[:chain]))
+                source = pl.ds(pl.multiple_of(slot * size, 16), size)
+                target = pl.ds(first + before, size)
+                for ref, wanted in ((own[chain], core == half), (other[chain], core != half)):
+
+                    @pl.when(wanted)
+                    def _(ref=ref, source=source, target=target):
+                        flat[target, :] = ref[source, :].astype(FULLTYPE)
+
+        flat[pl.ds(first, 1), :] += last * shared
+        return carry
+
+    flat[0:8, :] = jnp.zeros((8, 128), FULLTYPE)
+    lax.fori_loop(0, owners, collect, 0)
+    spread_flat(plan, flat, outs, rest)
+
+
+def unpack_parts_kernel(plan, shard, parts_ref, *refs):
     outs, rest, flat = (refs[: len(plan)], refs[len(plan)], refs[len(plan) + 1])
     owners, rows = parts_ref.shape[:2]
     chunk = chunk_of(rows)
@@ -815,6 +932,10 @@
         lax.fori_loop(0, rows // chunk, copy, 0)
         if owner and shard * owner % 128:
             flat[pl.ds(first, 1), :] += last
+    spread_flat(plan, flat, outs, rest)
+
+
+def spread_flat(plan, flat, outs, rest):
     for (start, height, across), out in zip(plan, outs):
 
         def place(i, carry, start=start, across=across, out=out):
@@ -828,16 +949,54 @@
     rest[...] = flat[pl.ds(start, rest.shape[0]), :]
 
 
-def unpack_weights(parts, shard, experts):
+ORDERS = ((1, 2, 4, 8), (2, 4, 8, 1), (4, 8, 1, 2))
+
+
+def chain_sizes(rows):
+    units = rows // 16
+    first = max(1, units * 2 // 9)
+    second = (units - first) // 2
+    return [16 * first, 16 * second, 16 * (units - first - second)]
+
+
+def gather_weights(part, shard, ep_place, dp_place, experts, beside):
     plan, start = flat_plan(experts)
-    owners, rows = parts.shape[:2]
-    rest = shard * owners // 128 - start
+    owners, groups = (lax.axis_size("ep"), lax.axis_size("dp"))
+    rows = owner_rows(shard, groups)
     outs = [shaped((height, across * 128), LOWTYPE) for _, height, across in plan]
-    outs.append(shaped((rest, 128), FULLTYPE))
+    outs.append(shaped((shard * owners // 128 - start, 128), FULLTYPE))
     flat = pltpu.VMEM((-(-(shard * (owners - 1) // 128 + rows) // 8) * 8, 128), FULLTYPE)
-    return local_call(
-        functools.partial(unpack_kernel, plan, shard), outs, [parts], 0, [flat]
-    )
+    if (owners, groups) != (16, 2) or part.shape[0] < 48:
+        parts = lax.all_gather(part, ("ep", "dp")).reshape(owners, rows, 128)
+        kernel, args = (functools.partial(unpack_parts_kernel, plan, shard), [parts])
+        return (local_call(kernel, outs, args, 0, [flat]), beside[0](*beside[1]))
+    sizes = chain_sizes(part.shape[0])
+    chains = [part[sum(sizes[:c]) : sum(sizes[: c + 1])] for c in range(len(ORDERS))]
+    work, inputs = beside
+    for step in range(len(ORDERS[0])):
+        got = [
+            lax.ppermute(v, "ep", [(i, i ^ order[step]) for i in range(owners)])
+            for v, order in zip(chains, ORDERS)
+        ]
+        if step == len(ORDERS[0]) - 2:
+            got, inputs = lax.optimization_barrier((got, inputs))
+        elif step == len(ORDERS[0]) - 1:
+            got, results = lax.optimization_barrier((got, work(*inputs)))
+        else:
+            got = lax.optimization_barrier(got)
+        chains = [jnp.concatenate([v, g]) for v, g in zip(chains, got)]
+    args = [jnp.stack([ep_place, dp_place]).astype(jnp.int32), *chains, *map(swap_dp, chains)]
+    moved = sum(math.prod(a.shape) * a.dtype.itemsize for a in (*args, *outs))
+    mats = pl.pallas_call(
+        functools.partial(unpack_kernel, plan, shard, owners, ORDERS),
+        out_shape=outs,
+        in_specs=[SCALARS] + in_vmem(len(args) - 1),
+        out_specs=in_vmem(len(outs)),
+        scratch_shapes=[flat],
+        compiler_params=pltpu.CompilerParams(vmem_limit_bytes=VMEM_LIMIT),
+        cost_estimate=pl.CostEstimate(flops=0, bytes_accessed=moved, transcendentals=0),
+    )(*args)
+    return (mats, results)
 
 
 def pack_kernel(plan, shard, select, place_ref, *refs):
@@ -1009,38 +1168,55 @@
     own_part = lax.dynamic_index_in_dim(
         spread.reshape(groups, rows // groups, 128), dp_place, 0, keepdims=False
     )
-    parts = lax.all_gather(own_part, ("ep", "dp")).reshape(ep_count, rows, 128)
     low_in, low_out = (expert_in[0].astype(LOWTYPE), expert_out[0].astype(LOWTYPE))
     all_in = lax.all_gather(low_in, ("ep", "dp"))
     all_out = lax.all_gather(low_out, ("ep", "dp"))
     width = low_in.shape[1]
-    w_in = all_in.reshape(experts, copies * groups, D, width)
-    if width % 128:
-        w_in = jnp.swapaxes(w_in, 1, 2).reshape(experts, 1, D, copies * groups * width)
     w_out = all_out.reshape(experts, copies * groups * width, D)
 
-    named = jnp.sum(
-        (routes[:, :, None] == jnp.arange(experts, dtype=jnp.int32)[None, None, :]).astype(FULLTYPE),
-        1,
-    )
-    earlier = jnp.arange(seq)[:, None] > jnp.arange(seq)[None, :]
-    table = jnp.where(named > 0, plain(earlier.astype(LOWTYPE), named.astype(LOWTYPE)), -1.0)
-    place = table.T.reshape(experts, 1, seq)
-    loads = jnp.sum(named, 0).astype(jnp.int32)
-    bias = jnp.where(patch_valid > 0, 0.0, NEG).astype(FULLTYPE)
-    across, down = (bias.reshape(1, seq), bias.reshape(seq, 1))
-    weight_pix = (pixel_mask * patch_valid[:, None]).astype(FULLTYPE)
-    count_tok = jnp.sum(weight_pix, 1)
-    class_hot = labels[:, :, None] == jnp.arange(C, dtype=jnp.int32)[None, None, :]
-    counts = jnp.sum(jnp.where(class_hot, weight_pix[:, :, None], 0.0), 1)
-    total = sum_all(jnp.sum(count_tok).reshape(1))[0]
-
     together = lax.optimization_barrier
-    weight_sums = block_sums(dense_weight, expert_in, expert_out)
-    parts, counts, count_tok, total, table, place, loads, across, down, weight_sums = together(
-        (parts, counts, count_tok, total, table, place, loads, across, down, weight_sums)
-    )
-    *mats, rest = unpack_weights(parts, shard, experts)
+
+    def prepare(labels, pixel_mask, patch_valid, routes, weights):
+        named = jnp.sum(
+            (routes[:, :, None] == jnp.arange(experts, dtype=jnp.int32)[None, None, :]).astype(FULLTYPE),
+            1,
+        )
+        earlier = jnp.arange(seq)[:, None] > jnp.arange(seq)[None, :]
+        table = jnp.where(named > 0, plain(earlier.astype(LOWTYPE), named.astype(LOWTYPE)), -1.0)
+        weight_pix = (pixel_mask * patch_valid[:, None]).astype(FULLTYPE)
+        class_hot = labels[:, :, None] == jnp.arange(C, dtype=jnp.int32)[None, None, :]
+        return (
+            table,
+            table.T.reshape(experts, 1, seq),
+            jnp.sum(named, 0).astype(jnp.int32),
+            jnp.where(patch_valid > 0, 0.0, NEG).astype(FULLTYPE).reshape(seq, 1),
+            jnp.sum(weight_pix, 1),
+            jnp.sum(jnp.where(class_hot, weight_pix[:, :, None], 0.0), 1),
+            block_sums(*weights),
+        )
+
+    (*mats, rest), prepared = gather_weights(
+        own_part,
+        shard,
+        ep_place,
+        dp_place,
+        experts,
+        (
+            prepare,
+            (labels, pixel_mask, patch_valid, routes, (dense_weight, expert_in, expert_out)),
+        ),
+    )
+    table, place, loads, down, count_tok, counts, weight_sums = prepared
+    steps = [(axis, 2**k) for axis in ("dp", "ep") for k in range(lax.axis_size(axis).bit_length() - 1)]
+    fourth = -(-len(steps) // 4)
+
+    def add_steps(value, turn):
+        for axis, step in steps[turn * fourth : (turn + 1) * fourth]:
+            count = lax.axis_size(axis)
+            value = value + lax.ppermute(value, axis, [(i, i ^ step) for i in range(count)])
+        return value
+
+    total = add_steps(jnp.sum(count_tok).reshape(1), 0)
     w_patch, w_qkv, w_attn = (mats[0], mats[1:4], mats[4:7])
     w_up, w_down = (mats[7:9], mats[9:11])
     router_rows, head_rows = (TASKS * D * experts // 128, D * C // 128)
@@ -1050,10 +1226,8 @@
     task = tasks[0]
     router = lax.dynamic_index_in_dim(w_router, task, 0, keepdims=False)
 
-    def dispatch(send, block):
-        third = capacity // 3
-        taken = send.reshape(experts, capacity, D)[:, block * third : (block + 1) * third]
-        return to_experts(jnp.repeat(taken, copies, axis=0)).reshape(-1, D)
+    def dispatch(send):
+        return to_experts(jnp.repeat(send, copies, axis=0)).reshape(-1, D)
 
     together = lax.optimization_barrier
 
@@ -1064,22 +1238,30 @@
         return jnp.pad(jnp.stack(rows), ((0, 8 - len(rows)), (0, 0)))
 
     x0, *kept0, x1, act0, slope0 = layer_forward(
-        patches, w_patch, w_qkv[0], w_attn[0], norm_rows(0), across, w_up[0], w_down[0]
-    )
+        patches, w_patch, w_qkv[0], w_attn[0], norm_rows(0), down, w_up[0], w_down[0]
+    )
+    x1, all_in, total = together((x1, all_in, total))
+    total = add_steps(total, 1)
     mid1, c16, *kept1 = layer_forward(
-        x1, None, w_qkv[1], w_attn[1], norm_rows(1), across, None, None
-    )
-    gates, spread_place, spread_gate, sent, act1, slope1 = moe_up(
+        x1, None, w_qkv[1], w_attn[1], norm_rows(1), down, None, None
+    )
+    c16, total = together((c16, total))
+    total = add_steps(total, 2)
+    w_in = all_in.reshape(experts, copies * groups, D, width)
+    if width % 128:
+        w_in = jnp.swapaxes(w_in, 1, 2).reshape(experts, 1, D, copies * groups * width)
+    gates, spread_place, spread_gate, act1, slope1, *sent = moe_up(
         loads, c16, router, table, place, w_in, capacity
     )
     x2, y16 = moe_down(loads, mid1, spread_place, spread_gate, act1, w_out)
-    x2, sent = together((x2, sent))
-    rows_a = dispatch(sent, 0)
+    x2, sent, total = together((x2, sent, total))
+    total = add_steps(total, 3)
+    rows_a = dispatch(sent[0])
     *kept2, x3, act2, slope2 = layer_forward(
-        x2, None, w_qkv[2], w_attn[2], norm_rows(2), across, w_up[1], w_down[1]
+        x2, None, w_qkv[2], w_attn[2], norm_rows(2), down, w_up[1], w_down[1]
     )
     x3, sent, rows_a = together((x3, sent, rows_a))
-    rows_b = dispatch(sent, 1)
+    rows_b = dispatch(sent[1])
     loss_lanes, d_head, d_normf, grad = head_call(
         x3, norm_rows(3), w_head, counts, count_tok, total
     )
@@ -1090,22 +1272,22 @@
         (w_up[1], w_down[1]), None, None,
     )
     grad, sent, rows_b = together((grad, sent, rows_b))
-    rows_c = dispatch(sent, 2)
-    d_own_router, d_c, dy16 = moe_gate_backward(
+    rows_c = dispatch(sent[2])
+    d_own_router, d_c, *dy16 = moe_gate_backward(
         loads, grad, c16, router, gates, place, spread_place, spread_gate, y16
     )
     d_c, dy16, rows_c = together((d_c, dy16, rows_c))
-    dy_a = dispatch(dy16, 0)
+    dy_a = dispatch(dy16[0])
     d_c = moe_backward(loads, d_c, spread_place, w_in, w_out, dy16, slope1)
     d_c, dy16, dy_a = together((d_c, dy16, dy_a))
-    dy_b = dispatch(dy16, 1)
+    dy_b = dispatch(dy16[1])
     task_hot = (jnp.arange(TASKS, dtype=jnp.int32) == task)[:, None, None]
     d_router = jnp.where(task_hot, d_own_router[None], 0.0)
     d_qkv1, d_attn1, d_norm1, grad = layer_backward(
         grad, x1, (mid1, c16, *kept1), w_qkv[1], w_attn[1], norm_rows(1), down, None, d_c, None
     )
     grad, dy16, dy_b = together((grad, dy16, dy_b))
-    dy_c = dispatch(dy16, 2)
+    dy_c = dispatch(dy16[2])
     d_qkv0, d_attn0, d_norm0, d_up0, d_down0, d_patch = layer_backward(
         grad, x0, (*kept0, act0, slope0), w_qkv[0], w_attn[0], norm_rows(0), down,
         (w_up[0], w_down[0]), None, patches,

time: 978 us -> 905 us (0.925)
  waiting for transfers between devices: 208 us -> 118 us
  starting transfers between devices: 97.6 us -> 142 us
  Pallas kernels: 498 us -> 467 us
    all_gather x1, waiting for transfers between devices: 84.1 us -> 24.7 us  [per_device(): all_out = lax.all_gather(low_out, ('ep', 'dp'))]
    all_gather x1, waiting for transfers between devices: 50.9 us -> 0.01 us  [per_device(): all_in = lax.all_gather(low_in, ('ep', 'dp'))]
    ppermute x0 -> x17, starting transfers between devices: none -> 50.3 us  [the longest x5 31.4 us: add_steps(): lax.ppermute(value, axis, [(i, i ^ step) for i in range(count)])]
    ppermute x0 -> x17, waiting for transfers between devices: none -> 45.4 us  [the longest x12 41.4 us: gather_weights(): lax.ppermute(v, 'ep', [(i, i ^ order[step]) for i in range(owners)])]
    pallas_call x8 -> x7, Pallas kernels: 269 us -> 227 us  [local_call(): pl.pallas_call(kernel, out_shape=outs, in_specs=in_vmem(len(args)), out_s...]
    all_gather x1 -> x0, waiting for transfers between devices: 25.1 us -> none  [per_device(): parts = lax.all_gather(own_part, ('ep', 'dp')).reshape(ep_count, rows, 128)]
    slice x6 -> x0, local copies, waits for them, and re-layouts: 19.5 us -> none  [dispatch(): send.reshape(experts, capacity, D)[:, block * third:(block + 1) * third]]
    ppermute x15 -> x10, starting transfers between devices: 48.9 us -> 33.3 us  [sum_all(): lax.ppermute(value, axis, [(i, i ^ step) for i in range(count)])]
  transfers between devices with their start and end apart: 29 -> 43, of which waited for: 20 -> 20; matrix products, arithmetic and copies ran while one was open for 5% -> 7% of each run, Pallas kernels for 46% -> 50%
where the time goes in v3:
time: 905 us; the launch traced here: 895 us
  Pallas kernels  467 us (52%)
  starting transfers between devices  142 us (16%)
  waiting for transfers between devices  118 us (13%)
  other arithmetic  89.4 us (10%)
  between operations  39.2 us (4%)
  local copies, waits for them, and re-layouts  38.9 us (4%)
    pallas_call x7, Pallas kernels, local_call(): pl.pallas_call(kernel, out_shape=outs, in_specs=in_vmem(len(args)), out_s...  227 us
    pallas_call x6, Pallas kernels, gridded(): pl.pallas_call(kernel, grid=(steps,), out_shape=outs, in_specs=in_specs,...  211 us
    all_to_all x7, starting transfers between devices, to_experts(): return lax.all_to_all(buffer, 'ep', split_axis=0, concat_axis=0, tiled=True)  57 us
    ppermute x12, waiting for transfers between devices, gather_weights(): lax.ppermute(v, 'ep', [(i, i ^ order[step]) for i in range(owners)])  41.4 us
    ppermute x10, starting transfers between devices, sum_all(): lax.ppermute(value, axis, [(i, i ^ step) for i in range(count)])  33.3 us
    ppermute x5, starting transfers between devices, add_steps(): lax.ppermute(value, axis, [(i, i ^ step) for i in range(count)])  31.4 us
    all_to_all x7, waiting for transfers between devices, to_experts(): return lax.all_to_all(buffer, 'ep', split_axis=0, concat_axis=0, tiled=True)  25.9 us
    all_gather x1, waiting for transfers between devices, per_device(): all_out = lax.all_gather(low_out, ('ep', 'dp'))  24.7 us
  transfers between devices with their start and end apart: 43, of which 20 were waited for; matrix products, arithmetic and copies ran while one was open for 7% of the time, Pallas kernels for 50%

profile of v3, /device:TPU:0, one launch (start us, length us, event | category | flops | bytes accessed | tf_op | source)
XLA Modules:
  0.0 894.7 jit_solution(5279425489177936744)
XLA Ops:
  11.1 5.2 dynamic_update_slice.3
  18.9 3.0 collective-permute-start.1
  26.4 4.0 collective-permute-done
  32.2 5.2 collective-permute-start.5
  56.5 22.2 %collective-permute-done.6 = bf16[960,128]{1,0:T(8,128)(2,1)S(1)} collective-permute-done((bf16[960,128]{1,0:T(8,128)(2,1)S(1)}, bf16[960,128]{1,0:T(8,128)(2,1)S(1)}, u32[]{:S(2)}, u32[]{:S(2)}) %collective-permute-start.6) | collective-permute-done | bytes 245792 | tf_op jit(solution)/shard_map/ppermute | solution.py:978
  78.7 15.2 %collective-permute-done.7 = bf16[1728,128]{1,0:T(8,128)(2,1)S(1)} collective-permute-done((bf16[1728,128]{1,0:T(8,128)(2,1)S(1)}, bf16[1728,128]{1,0:T(8,128)(2,1)S(1)}, u32[]{:S(2)}, u32[]{:S(2)}) %collective-permute-start.7) | collective-permute-done | bytes 442400 | tf_op jit(solution)/shard_map/ppermute | solution.py:978
  100.0 12.0 %select_reduce_fusion = f32[1024,40]{1,0:T(8,128)S(1)} fusion(f32[1024,256]{1,0:T(8,128)S(1)} %get-tuple-element.476, s32[1024,256]{1,0:T(8,128)S(1)} %copy-done.38), kind=kLoop, calls=%fused_computation | loop fusion | flops 31416320 | bytes 2260992 | tf_op jit(solution)/shard_map/reduce_sum | solution.py:1194
  113.7 5.1 select_add_fusion.1
  137.5 11.3 %shard_map.367 = (bf16[768,384]{1,0:T(8,128)(2,1)}, bf16[384,1152]{1,0:T(8,128)(2,1)}, bf16[384,1152]{1,0:T(8,128)(2,1)}, bf16[384,1152]{1,0:T(8,128)(2,1)}, bf1...) custom-call(s32[2]{0:T(128)} %pad_add_fusion.place_ref, ...), custom_call_target="tpu_custom_call" | custom-call | bytes 18072584 | tf_op jit(solution)/shard_map/pallas_call | solution.py:990
  152.7 34.3 %shard_map.368 = (f32[1024,384]{1,0:T(8,128)}, f32[1024,384]{1,0:T(8,128)}, bf16[1024,384]{1,0:T(8,128)(2,1)}, bf16[1024,1152]{1,0:T(8,128)(2,1)}, bf16[1024,384...) custom-call(bf16[1024,768]{1,0:T(8,128)(2,1)} %refs_15_.1, ...), custom_call_target="tpu_custom_call" | custom-call | flops 6845104128 | bytes 25378816 | tf_op jit(solution)/shard_map/pallas_call | solution.py:230
  189.5 24.4 %shard_map.369 = (f32[1024,384]{1,0:T(8,128)}, bf16[1024,384]{1,0:T(8,128)(2,1)}, bf16[1024,1152]{1,0:T(8,128)(2,1)}, bf16[1024,384]{1,0:T(8,128)(2,1)}, bf16[1024,768]{1,0:T(8,128)(2,1)}) custom-call(f32[1024,384]{1,0:T(8,128)} %get-tuple-element.186.refs_0_.refs_1_, bf16[384,1152]{1,0:T(8,128)(2,1)} %get-tuple-element.187.refs_1_.refs_6_, ...), custom_call_target="tpu_custom_call" | custom-call | flops 4429185024 | bytes 9846784 | tf_op jit(solution)/shard_map/pallas_call | solution.py:230
  214.5 25.0 %collective-permute-start.18 = (f32[1]{0:T(128)}, f32[1]{0:T(128)}, u32[]{:S(2)}, u32[]{:S(2)}) collective-permute-start(f32[1]{0:T(128)} %add.348), channel_id=1, source_target_pairs={{0,8},{2,10},{4,12},{6,14},{8,0},{10,2},{12,4},{14,6},{16,24},{18,... | collective-permute-start | bytes 20 | tf_op jit(solution)/shard_map/ppermute | solution.py:1216
  241.9 42.4 %shard_map.370 = (f32[1024,16]{1,0:T(8,128)}, f32[16,1024,128]{2,1,0:T(8,128)}, f32[16,1024,128]{2,1,0:T(8,128)}, bf16[6144,1536]{1,0:T(8,128)(2,1)}, f32[6144,1...) custom-call(s32[16]{0:T(128)} %convert_element_type.80.loads, ...), custom_call_target="tpu_custom_call" | custom-call | flops 12079595520 | bytes 97988672 | tf_op jit(solution)/shard_map/pallas_call | solution.py:733
  284.3 24.7 %all-gather.5.cloned.1.call-done = bf16[32,768,384]{2,1,0:T(8,128)(2,1)} async-done(((bf16[1,768,384]{2,1,0:T(8,128)(2,1)}), bf16[32,768,384]{2,1,0:T(8,128)(2,1)}) %all-gather.5.cloned.1.call-update) | async-done | bytes 18874384 | tf_op jit(solution)/shard_map/all_gather | solution.py:1173
  309.0 34.5 %shard_map.371 = (f32[1024,384]{1,0:T(8,128)}, bf16[6144,384]{1,0:T(8,128)(2,1)}) custom-call(s32[16]{0:T(128)} %convert_element_type.80.loads, f32[1024,384]{1,0:T(8,128)} %get-tuple-element.189.mid_ref.refs_2_, f32[16,1024,128]{2,1,0:T(8,128)} %get-tuple-element.196.spread_place, f32[16,1024,128]{2,1,0:T(8,128)} %get-tuple-element.197.spread_gate, ...), custom_call_target="tpu_custom_call" | custom-call | flops 12079595520 | bytes 62390336 | tf_op jit(solution)/shard_map/pallas_call | solution.py:733
  344.1 4.5 all-to-all-start
  349.2 32.5 %shard_map.372 = (f32[1024,384]{1,0:T(8,128)}, bf16[1024,384]{1,0:T(8,128)(2,1)}, bf16[1024,1152]{1,0:T(8,128)(2,1)}, bf16[1024,384]{1,0:T(8,128)(2,1)}, bf16[10...) custom-call(f32[1024,384]{1,0:T(8,128)} %get-tuple-element.204.refs_0_.refs_1_, ...), custom_call_target="tpu_custom_call" | custom-call | flops 6845104128 | bytes 23216128 | tf_op jit(solution)/shard_map/pallas_call | solution.py:230
  384.0 16.3 %all-to-all-start.1 = ((bf16[16,128,384]{2,1,0:T(8,128)(2,1)}), bf16[16,128,384]{2,1,0:T(8,128)(2,1)}, u32[]{:S(2)}, u32[]{:S(2)}) async-start(bf16[16,128,384]{2,1,0:T(8,128)(2,1)} %get-tuple-element.229), calls=%async_computation.1 | async-start | bytes 3145728 | tf_op jit(solution)/shard_map/all_to_all | solution.py:1103
  403.5 7.0 shard_map.373
  410.5 46.9 %shard_map.374 = (f32[384,1152]{1,0:T(8,128)}, f32[384,384]{1,0:T(8,128)}, f32[8,384]{1,0:T(8,128)}, f32[384,1536]{1,0:T(8,128)}, f32[1536,384]{1,0:T(8,128)}, /*index=5*/f32[1024,384]{1,0:T(8,128)}) custom-call(f32[1024,384]{1,0:T(8,128)} %get-tuple-element.220.refs_0_, f32[1024,384]{1,0:T(8,128)} %get-tuple-element.204.refs_0_.refs_1_, ...), custom_call_target="tpu_custom_call" | custom-call | flops 15300820992 | bytes 31879168 | tf_op jit(solution)/shard_map/pallas_call | solution.py:230
  457.4 7.0 all-to-all-start.2
  464.4 35.3 %shard_map.375 = (f32[384,16]{1,0:T(8,128)}, f32[1024,384]{1,0:T(8,128)}, bf16[16,128,384]{2,1,0:T(8,128)(2,1)}, bf16[16,128,384]{2,1,0:T(8,128)(2,1)}, bf16[16,128,384]{2,1,0:T(8,128)(2,1)}) custom-call(s32[16]{0:T(128)} %convert_element_type.80.loads, f32[1024,384]{1,0:T(8,128)} %get-tuple-element.232.grad_ref.refs_0_, ...), custom_call_target="tpu_custom_call" | custom-call | flops 9663676416 | bytes 30314560 | tf_op jit(solution)/shard_map/pallas_call | solution.py:733
  501.0 6.9 all-to-all-start.3
  507.9 44.7 %shard_map.376.refs_10_ = f32[1024,384]{1,0:T(8,128)} custom-call(s32[16]{0:T(128)} %convert_element_type.80.loads, f32[1024,384]{1,0:T(8,128)} %get-tuple-element.241.start_ref, f32[16,1024,128]{2,1,0:T(8,128)} %get-tuple-element.196.spread_place, bf16[16,2,384,768]{3,2,1,0:T(8,128)(2,1)} %bitcast.132, bf16[16,1536,384]{2,1,0:T(8,128)(2,1)} %bitcast.129, ...), custom_call_target="tpu_custom_call" | custom-call | flops 19327352832 | bytes 91750464 | tf_op jit(solution)/shard_map/pallas_call | solution.py:733
  552.6 7.8 all-to-all-start.4
  560.4 32.9 %shard_map.377 = (f32[384,1152]{1,0:T(8,128)}, f32[384,384]{1,0:T(8,128)}, f32[8,384]{1,0:T(8,128)}, f32[1024,384]{1,0:T(8,128)}) custom-call(f32[1024,384]{1,0:T(8,128)} %get-tuple-element.232.grad_ref.refs_0_, f32[1024,384]{1,0:T(8,128)} %get-tuple-element.186.refs_0_.refs_1_, f32[1024,384]{1,0:T(8,128)} %get-tuple-element.189.mid_ref.refs_2_, ...), custom_call_target="tpu_custom_call" | custom-call | flops 10468982784 | bytes 16150528 | tf_op jit(solution)/shard_map/pallas_call | solution.py:230
  594.4 7.2 all-to-all-start.5
  602.9 49.3 %shard_map.378 = (f32[384,1152]{1,0:T(8,128)}, f32[384,384]{1,0:T(8,128)}, f32[8,384]{1,0:T(8,128)}, f32[384,1536]{1,0:T(8,128)}, f32[1536,384]{1,0:T(8,128)}, /*index=5*/f32[768,384]{1,0:T(8,128)}) custom-call(f32[1024,384]{1,0:T(8,128)} %get-tuple-element.255.refs_0_, f32[1024,384]{1,0:T(8,128)} %get-tuple-element.256.refs_1_, ...), custom_call_target="tpu_custom_call" | custom-call | flops 15904800768 | bytes 33058816 | tf_op jit(solution)/shard_map/pallas_call | solution.py:230
  652.2 17.1 %shard_map.381 = (f32[1,16,1104,128]{3,2,1,0:T(8,128)}, bf16[1,16,1104,128]{3,2,1,0:T(8,128)(2,1)}) custom-call(s32[1]{0:T(128)} %bitcast.18.place_ref, f32[768,384]{1,0:T(8,128)} %get-tuple-element.271.refs_0_, f32[384,1152]{1,0:T(8,128)} %get-tuple-element.272.refs_1_, f32[384,1152]{1,0:T(8,128)} %get-tuple-element.273.refs_2_, ...), custom_call_target="tpu_custom_call" | custom-call | bytes 31469572 | tf_op jit(solution)/shard_map/pallas_call | solution.py:1055
  669.3 7.8 collective-permute-done.22
  677.2 6.7 fusion
  683.9 7.3 all-to-all-start.6
  695.9 27.2 %shard_map.380 = (f32[384,768]{1,0:T(8,128)}, f32[768,384]{1,0:T(8,128)}) custom-call(bf16[2048,384]{1,0:T(8,128)(2,1)} %bitcast.136, bf16[2048,384]{1,0:T(8,128)(2,1)} %bitcast.42.refs_1_, bf16[2048,384]{1,0:T(8,128)(2,1)} %bitcast.138, bf16[2048,384]{1,0:T(8,128)(2,1)} %bitcast.44.refs_3_, bf16[2048,384]{1,0:T(8,128)(2,1)} %bitcast.140, ...), custom_call_target="tpu_custom_call" | custom-call | flops 18119393280 | bytes 12976128 | tf_op jit(solution)/shard_map/pallas_call | solution.py:733
  725.2 27.4 %shard_map.379 = (f32[384,768]{1,0:T(8,128)}, f32[768,384]{1,0:T(8,128)}) custom-call(bf16[2048,384]{1,0:T(8,128)(2,1)} %bitcast.137, bf16[2048,384]{1,0:T(8,128)(2,1)} %bitcast.42.refs_1_, bf16[2048,384]{1,0:T(8,128)(2,1)} %bitcast.139, bf16[2048,384]{1,0:T(8,128)(2,1)} %bitcast.44.refs_3_, bf16[2048,384]{1,0:T(8,128)(2,1)} %bitcast.141, ...), custom_call_target="tpu_custom_call" | custom-call | flops 18119393280 | bytes 12976128 | tf_op jit(solution)/shard_map/pallas_call | solution.py:733
  752.7 24.8 %all-to-all-done.6 = bf16[16,1104,128]{2,1,0:T(8,128)(2,1)} async-done(((bf16[16,1104,128]{2,1,0:T(8,128)(2,1)}), bf16[16,1104,128]{2,1,0:T(8,128)(2,1)}, u32[]{:S(2)}, u32[]{:S(2)}) %all-to-all-start.6) | async-done | bytes 4522016 | tf_op jit(solution)/shard_map/all_to_all | solution.py:1103
  777.5 3.9 convert_reduce_fusion
  787.1 5.1 add_reduce_fusion
  795.0 2.8 collective-permute-start.25
  799.3 6.7 collective-permute-start.26
  807.5 11.7 %collective-permute-start.27 = (f32[48]{0:T(128)S(1)}, f32[48]{0:T(128)S(1)}, u32[]{:S(2)}, u32[]{:S(2)}) collective-permute-start(f32[48]{0:T(128)S(1)} %add.365), channel_id=1, source_target_pairs={{0,8},{2,10},{4,12},{6,14},{8,0},{10,2},{12,4},{14,6},{16,24},{18,... | collective-permute-start | bytes 584 | tf_op jit(solution)/shard_map/ppermute | solution.py:1097
  820.8 2.8 collective-permute-start.28
  826.6 4.0 multiply_add_fusion.6
  831.9 2.9 multiply_reduce_fusion
  835.2 2.9 multiply_reduce_fusion.1
  838.1 4.6 select_add_fusion
  843.9 4.6 fusion.39
  852.1 4.6 fusion.41
  863.9 2.8 collective-permute-start.33
  (251 shorter events, 111.1 us)
Async XLA Ops:
  7.2 179.8 %all-gather.3.cloned.1.call-start = ((), (), s32[]{:S(2)}) async-start(), calls=%async_computation.7 | async-start | bytes 19464192 | tf_op jit(solution)/shard_map/all_gather | solution.py:1172
  9.5 299.5 %all-gather.5.cloned.1.call-start = ((), (), s32[]{:S(2)}) async-start(), calls=%async_computation.8 | async-start | bytes 19464192 | tf_op jit(solution)/shard_map/all_gather | solution.py:1173
  17.1 21.0 %copy-start.46 = (s32[16]{0:T(128)S(1)}, s32[16]{0:T(128)}, u32[]{:S(2)}) copy-start(s32[16]{0:T(128)} %constant.302.clone) | copy-start | bytes 196
  17.1 28.7 %copy-start.43 = (s32[18]{0:T(128)S(1)}, s32[18]{0:T(128)}, u32[]{:S(2)}) copy-start(s32[18]{0:T(128)} %constant.303.clone..sunk.10) | copy-start | bytes 220
  18.9 11.5 %collective-permute-start.1 = (bf16[432,128]{1,0:T(8,128)(2,1)S(1)}, bf16[432,128]{1,0:T(8,128)(2,1)S(1)}, u32[]{:S(2)}, u32[]{:S(2)}) collective-permute-start(bf16[432,128]{1,0:T(8,128)(2,1)S(1)} %get-tuple-element.484), channel_id=1, source_target_pairs={{0,4},{2,6},{4,0},{6,2},{8,12},{10,14},{12,8},{14,10},{16,20},{18,... | collective-permute-start | bytes 331784 | tf_op jit(solution)/shard_map/ppermute | solution.py:978
  21.8 8.6 collective-permute-start.2
  24.9 5.5 collective-permute-start
  31.1 18.6 %collective-permute-start.4 = (bf16[864,128]{1,0:T(8,128)(2,1)}, bf16[864,128]{1,0:T(8,128)(2,1)S(1)}, u32[]{:S(2)}, u32[]{:S(2)}) collective-permute-start(bf16[864,128]{1,0:T(8,128)(2,1)} %pad_maximum_fusion.7), channel_id=1, source_target_pairs={{0,8},{2,10},{4,12},{6,14},{8,0},{10,2},{12,4},{14,6},{16,24},{18,... | collective-permute-start | bytes 663560 | tf_op jit(solution)/shard_map/ppermute | solution.py:978
  32.2 17.5 %collective-permute-start.5 = (bf16[864,128]{1,0:T(8,128)(2,1)}, bf16[864,128]{1,0:T(8,128)(2,1)S(1)}, u32[]{:S(2)}, u32[]{:S(2)}) collective-permute-start(bf16[864,128]{1,0:T(8,128)(2,1)} %pad_maximum_fusion.8), channel_id=1, source_target_pairs={{0,16},{2,18},{4,20},{6,22},{8,24},{10,26},{12,28},{14,30},{16,0},... | collective-permute-start | bytes 663560 | tf_op jit(solution)/shard_map/ppermute | solution.py:978
  38.1 11.6 %collective-permute-start.3 = (bf16[480,128]{1,0:T(8,128)(2,1)}, bf16[480,128]{1,0:T(8,128)(2,1)S(1)}, u32[]{:S(2)}, u32[]{:S(2)}) collective-permute-start(bf16[480,128]{1,0:T(8,128)(2,1)} %pad_maximum_fusion.10), channel_id=1, source_target_pairs={{0,4},{2,6},{4,0},{6,2},{8,12},{10,14},{12,8},{14,10},{16,20},{18,... | collective-permute-start | bytes 368648 | tf_op jit(solution)/shard_map/ppermute | solution.py:978
  49.8 44.1 %collective-permute-start.7 = (bf16[1728,128]{1,0:T(8,128)(2,1)S(1)}, bf16[1728,128]{1,0:T(8,128)(2,1)S(1)}, u32[]{:S(2)}, u32[]{:S(2)}) collective-permute-start(bf16[1728,128]{1,0:T(8,128)(2,1)S(1)} %pad_maximum_fusion.4), channel_id=1, source_target_pairs={{0,16},{2,18},{4,20},{6,22},{8,24},{10,26},{12,28},{14,30},{16,0},... | collective-permute-start | bytes 1327112 | tf_op jit(solution)/shard_map/ppermute | solution.py:978
  51.1 42.8 %collective-permute-start.8 = (bf16[1728,128]{1,0:T(8,128)(2,1)S(1)}, bf16[1728,128]{1,0:T(8,128)(2,1)S(1)}, u32[]{:S(2)}, u32[]{:S(2)}) collective-permute-start(bf16[1728,128]{1,0:T(8,128)(2,1)S(1)} %pad_maximum_fusion.5), channel_id=1, source_target_pairs={{0,2},{2,0},{4,6},{6,4},{8,10},{10,8},{12,14},{14,12},{16,18},{18,... | collective-permute-start | bytes 1327112 | tf_op jit(solution)/shard_map/ppermute | solution.py:978
  52.7 26.0 %collective-permute-start.6 = (bf16[960,128]{1,0:T(8,128)(2,1)S(1)}, bf16[960,128]{1,0:T(8,128)(2,1)S(1)}, u32[]{:S(2)}, u32[]{:S(2)}) collective-permute-start(bf16[960,128]{1,0:T(8,128)(2,1)S(1)} %pad_maximum_fusion.6), channel_id=1, source_target_pairs={{0,8},{2,10},{4,12},{6,14},{8,0},{10,2},{12,4},{14,6},{16,24},{18,... | collective-permute-start | bytes 737288 | tf_op jit(solution)/shard_map/ppermute | solution.py:978
  93.9 27.6 %collective-permute-start.9 = (bf16[1920,128]{1,0:T(8,128)(2,1)S(1)}, bf16[1920,128]{1,0:T(8,128)(2,1)S(1)}, u32[]{:S(2)}, u32[]{:S(2)}) collective-permute-start(bf16[1920,128]{1,0:T(8,128)(2,1)S(1)} %pad_maximum_fusion.3), channel_id=1, source_target_pairs={{0,16},{2,18},{4,20},{6,22},{8,24},{10,26},{12,28},{14,30},{16,0},... | collective-permute-start | bytes 1474568 | tf_op jit(solution)/shard_map/ppermute | solution.py:978
  94.1 27.5 %collective-permute-start.10 = (bf16[3456,128]{1,0:T(8,128)(2,1)S(1)}, bf16[3456,128]{1,0:T(8,128)(2,1)S(1)}, u32[]{:S(2)}, u32[]{:S(2)}) collective-permute-start(bf16[3456,128]{1,0:T(8,128)(2,1)S(1)} %pad_maximum_fusion.1), channel_id=1, source_target_pairs={{0,2},{2,0},{4,6},{6,4},{8,10},{10,8},{12,14},{14,12},{16,18},{18,... | collective-permute-start | bytes 2654216 | tf_op jit(solution)/shard_map/ppermute | solution.py:978
  95.9 25.7 %collective-permute-start.11 = (bf16[3456,128]{1,0:T(8,128)(2,1)S(1)}, bf16[3456,128]{1,0:T(8,128)(2,1)S(1)}, u32[]{:S(2)}, u32[]{:S(2)}) collective-permute-start(bf16[3456,128]{1,0:T(8,128)(2,1)S(1)} %pad_maximum_fusion.2), channel_id=1, source_target_pairs={{0,4},{2,6},{4,0},{6,2},{8,12},{10,14},{12,8},{14,10},{16,20},{18,... | collective-permute-start | bytes 2654216 | tf_op jit(solution)/shard_map/ppermute | solution.py:978
  122.5 13.7 %collective-permute-start.13 = (bf16[6912,128]{1,0:T(8,128)(2,1)}, bf16[6912,128]{1,0:T(8,128)(2,1)S(1)}, u32[]{:S(2)}, u32[]{:S(2)}) collective-permute-start(bf16[6912,128]{1,0:T(8,128)(2,1)} %constant_dynamic-update-slice_fusion.5.refs_1_), channel_id=1, source_target_pairs={{0,1},{1,0},{2,3},{3,2},{4,5},{5,4},{6,7},{7,6},{8,9},{9,8},{10,11... | collective-permute-start | bytes 5308424 | tf_op jit(solution)/shard_map/ppermute | solution.py:1071
  123.6 12.7 %collective-permute-start.14 = (bf16[6912,128]{1,0:T(8,128)(2,1)}, bf16[6912,128]{1,0:T(8,128)(2,1)}, u32[]{:S(2)}, u32[]{:S(2)}) collective-permute-start(bf16[6912,128]{1,0:T(8,128)(2,1)} %constant_dynamic-update-slice_fusion.10.refs_2_), channel_id=1, source_target_pairs={{0,1},{1,0},{2,3},{3,2},{4,5},{5,4},{6,7},{7,6},{8,9},{9,8},{10,11... | collective-permute-start | bytes 5308424 | tf_op jit(solution)/shard_map/ppermute | solution.py:1071
  124.2 12.0 %collective-permute-start.12 = (bf16[3840,128]{1,0:T(8,128)(2,1)S(1)}, bf16[3840,128]{1,0:T(8,128)(2,1)}, u32[]{:S(2)}, u32[]{:S(2)}) collective-permute-start(bf16[3840,128]{1,0:T(8,128)(2,1)S(1)} %constant_dynamic-update-slice_fusion.refs_0_), channel_id=1, source_target_pairs={{0,1},{1,0},{2,3},{3,2},{4,5},{5,4},{6,7},{7,6},{8,9},{9,8},{10,11... | collective-permute-start | bytes 2949128 | tf_op jit(solution)/shard_map/ppermute | solution.py:1071
  127.2 3.6 collective-permute-start.15
  132.1 3.6 collective-permute-start.16
  187.0 26.9 %collective-permute-start.17 = (f32[1]{0:T(128)}, f32[1]{0:T(128)}, u32[]{:S(2)}, u32[]{:S(2)}) collective-permute-start(f32[1]{0:T(128)} %add.347), channel_id=1, source_target_pairs={{0,4},{2,6},{4,0},{6,2},{8,12},{10,14},{12,8},{14,10},{16,20},{18,... | collective-permute-start | bytes 20 | tf_op jit(solution)/shard_map/ppermute | solution.py:1216
  214.5 25.4 %collective-permute-start.18 = (f32[1]{0:T(128)}, f32[1]{0:T(128)}, u32[]{:S(2)}, u32[]{:S(2)}) collective-permute-start(f32[1]{0:T(128)} %add.348), channel_id=1, source_target_pairs={{0,8},{2,10},{4,12},{6,14},{8,0},{10,2},{12,4},{14,6},{16,24},{18,... | collective-permute-start | bytes 20 | tf_op jit(solution)/shard_map/ppermute | solution.py:1216
  240.5 103.0 %collective-permute-start.19 = (f32[1]{0:T(128)}, f32[1]{0:T(128)}, u32[]{:S(2)}, u32[]{:S(2)}) collective-permute-start(f32[1]{0:T(128)} %add.349), channel_id=1, source_target_pairs={{0,16},{2,18},{4,20},{6,22},{8,24},{10,26},{12,28},{14,30},{16,0},... | collective-permute-start | bytes 20 | tf_op jit(solution)/shard_map/ppermute | solution.py:1216
  344.1 38.7 %all-to-all-start = ((bf16[16,128,384]{2,1,0:T(8,128)(2,1)}), bf16[16,128,384]{2,1,0:T(8,128)(2,1)S(1)}, u32[]{:S(2)}, u32[]{:S(2)}) async-start(bf16[16,128,384]{2,1,0:T(8,128)(2,1)} %get-tuple-element.210), calls=%async_computation | async-start | bytes 3145728 | tf_op jit(solution)/shard_map/all_to_all | solution.py:1103
  384.0 73.5 %all-to-all-start.1 = ((bf16[16,128,384]{2,1,0:T(8,128)(2,1)}), bf16[16,128,384]{2,1,0:T(8,128)(2,1)}, u32[]{:S(2)}, u32[]{:S(2)}) async-start(bf16[16,128,384]{2,1,0:T(8,128)(2,1)} %get-tuple-element.229), calls=%async_computation.1 | async-start | bytes 3145728 | tf_op jit(solution)/shard_map/all_to_all | solution.py:1103
  457.4 42.4 %all-to-all-start.2 = ((bf16[16,128,384]{2,1,0:T(8,128)(2,1)}), bf16[16,128,384]{2,1,0:T(8,128)(2,1)S(1)}, u32[]{:S(2)}, u32[]{:S(2)}) async-start(bf16[16,128,384]{2,1,0:T(8,128)(2,1)} %get-tuple-element.239), calls=%async_computation.2 | async-start | bytes 3145728 | tf_op jit(solution)/shard_map/all_to_all | solution.py:1103
  501.0 51.6 %all-to-all-start.3 = ((bf16[16,128,384]{2,1,0:T(8,128)(2,1)}), bf16[16,128,384]{2,1,0:T(8,128)(2,1)}, u32[]{:S(2)}, u32[]{:S(2)}) async-start(bf16[16,128,384]{2,1,0:T(8,128)(2,1)} %get-tuple-element.243.refs_0_), calls=%async_computation.3 | async-start | bytes 3145728 | tf_op jit(solution)/shard_map/all_to_all | solution.py:1103
  552.6 40.7 %all-to-all-start.4 = ((bf16[16,128,384]{2,1,0:T(8,128)(2,1)}), bf16[16,128,384]{2,1,0:T(8,128)(2,1)S(1)}, u32[]{:S(2)}, u32[]{:S(2)}) async-start(bf16[16,128,384]{2,1,0:T(8,128)(2,1)} %get-tuple-element.252.refs_1_), calls=%async_computation.4 | async-start | bytes 3145728 | tf_op jit(solution)/shard_map/all_to_all | solution.py:1103
  594.4 57.7 %all-to-all-start.5 = ((bf16[16,128,384]{2,1,0:T(8,128)(2,1)}), bf16[16,128,384]{2,1,0:T(8,128)(2,1)}, u32[]{:S(2)}, u32[]{:S(2)}) async-start(bf16[16,128,384]{2,1,0:T(8,128)(2,1)} %get-tuple-element.265.refs_2_), calls=%async_computation.5 | async-start | bytes 3145728 | tf_op jit(solution)/shard_map/all_to_all | solution.py:1103
  669.3 7.8 collective-permute-start.22
  683.9 93.6 %all-to-all-start.6 = ((bf16[16,1104,128]{2,1,0:T(8,128)(2,1)}), bf16[16,1104,128]{2,1,0:T(8,128)(2,1)}, u32[]{:S(2)}, u32[]{:S(2)}) async-start(bf16[16,1104,128]{2,1,0:T(8,128)(2,1)} %fusion), calls=%async_computation.6 | async-start | bytes 9043968 | tf_op jit(solution)/shard_map/all_to_all | solution.py:1103
  724.5 28.1 %collective-permute-start.20 = (bf16[384,768]{1,0:T(8,128)(2,1)S(1)}, bf16[384,768]{1,0:T(8,128)(2,1)S(1)}, u32[]{:S(2)}, u32[]{:S(2)}) collective-permute-start(bf16[384,768]{1,0:T(8,128)(2,1)S(1)} %convert_element_type.86), channel_id=1, source_target_pairs={{0,1},{1,0},{2,3},{3,2},{4,5},{5,4},{6,7},{7,6},{8,9},{9,8},{10,11... | collective-permute-start | bytes 1769480 | tf_op jit(solution)/shard_map/ppermute | solution.py:1071
  724.8 27.9 %collective-permute-start.21 = (bf16[768,384]{1,0:T(8,128)(2,1)S(1)}, bf16[768,384]{1,0:T(8,128)(2,1)S(1)}, u32[]{:S(2)}, u32[]{:S(2)}) collective-permute-start(bf16[768,384]{1,0:T(8,128)(2,1)S(1)} %convert_element_type.87), channel_id=1, source_target_pairs={{0,1},{1,0},{2,3},{3,2},{4,5},{5,4},{6,7},{7,6},{8,9},{9,8},{10,11... | collective-permute-start | bytes 1769480 | tf_op jit(solution)/shard_map/ppermute | solution.py:1071
  752.6 31.0 %copy-start.18 = (bf16[384,768]{1,0:T(8,128)(2,1)}, bf16[384,768]{1,0:T(8,128)(2,1)S(1)}, u32[]{:S(2)}) copy-start(bf16[384,768]{1,0:T(8,128)(2,1)S(1)} %collective-permute-done.20) | copy-start | bytes 1769476
  752.7 30.1 %copy-start.20 = (bf16[768,384]{1,0:T(8,128)(2,1)}, bf16[768,384]{1,0:T(8,128)(2,1)S(1)}, u32[]{:S(2)}) copy-start(bf16[768,384]{1,0:T(8,128)(2,1)S(1)} %collective-permute-done.21) | copy-start | bytes 1769476
  781.3 3.2 collective-permute-start.23
  785.9 40.6 %copy-start.5 = (f32[279312]{0:T(1024)S(1)}, f32[279312]{0:T(1024)}, u32[]{:S(2)}) copy-start(f32[279312]{0:T(1024)} %param.30) | copy-start | bytes 3351748
  793.0 1.2 collective-permute-start.24
  795.0 4.3 collective-permute-start.25
  799.3 8.3 collective-permute-start.26
  807.5 13.2 %collective-permute-start.27 = (f32[48]{0:T(128)S(1)}, f32[48]{0:T(128)S(1)}, u32[]{:S(2)}, u32[]{:S(2)}) collective-permute-start(f32[48]{0:T(128)S(1)} %add.365), channel_id=1, source_target_pairs={{0,8},{2,10},{4,12},{6,14},{8,0},{10,2},{12,4},{14,6},{16,24},{18,... | collective-permute-start | bytes 584 | tf_op jit(solution)/shard_map/ppermute | solution.py:1097
  820.8 4.4 collective-permute-start.28
  842.7 1.2 collective-permute-start.29
  848.5 3.6 collective-permute-start.30
  856.8 3.6 collective-permute-start.31
  860.4 3.5 collective-permute-start.32
  863.9 4.4 collective-permute-start.33
  (42 other events, 137.5 us)
Sparse Core Ops, SparseCore 0:
  11.5 164.6 all-gather.2
  179.7 129.2 all-gather.4

commit v4 on v3

--- a/solution.py
+++ b/solution.py
@@ -70,7 +70,7 @@
 
 
 VMEM_LIMIT = 56 * 2**20
-ROWS = 256
+ROWS = 512
 TILE = 32
 KEYS = 64
 QUERIES = 512
@@ -327,7 +327,7 @@
         dqkv_ref[:, pl.ds(2 * D + pair * 128, 128)] = dv_ref[...].astype(LOWTYPE)
 
 
-def weight_pull(left_ref, right_ref, out_ref, tile=128):
+def weight_pull(left_ref, right_ref, out_ref, tile=384):
     def body(j, carry):
         cols = rows_of(j, tile)
         out_ref[cols, :] = left_t(left_ref[:, cols], right_ref[...])
@@ -597,7 +597,7 @@
     by_load(loads[expert], capacity, work)
 
 
-def moe_down_kernel(loads, mid_ref, spread_place, spread_gate, act_ref, w_out, next_ref, y_ref):
+def moe_down_kernel(loads, mid_ref, spread_place, spread_gate, act_ref, w_out, next_ref, taken_ref, y_ref):
     expert = pl.program_id(0)
     seq, capacity = (mid_ref.shape[0], act_ref.shape[0])
 
@@ -608,12 +608,11 @@
     def work(count):
         at = pl.ds(0, count)
         y_ref[at, :] = plain(act_ref[at, :], w_out[0]).astype(LOWTYPE)
-        if count < capacity:
-            y_ref[pl.ds(count, capacity - count), :] = jnp.zeros((capacity - count, D), LOWTYPE)
 
         def add(i, carry):
             rows = rows_of(i)
             taken = plain(patch_select(spread_place[0, rows, :], count), y_ref[at, :])
+            taken_ref[0, rows, :] = taken.astype(LOWTYPE)
             for first in range(0, D, 128):
                 lanes = pl.ds(first, 128)
                 next_ref[rows, lanes] += spread_gate[0, rows, :] * taken[:, first : first + 128]
@@ -625,12 +624,12 @@
 
 
 def moe_gate_kernel(
-    loads, grad_ref, c_ref, router, gates, place, spread_place, spread_gate, y_ref,
+    loads, grad_ref, c_ref, router, gates, place, spread_gate, taken_ref,
     d_router, d_c, *refs,
 ):
     dy_refs, (low_ref, dz_ref, d_gates) = (refs[:-3], refs[-3:])
     expert = pl.program_id(0)
-    seq, capacity = (grad_ref.shape[0], y_ref.shape[0])
+    seq, capacity = (grad_ref.shape[0], SLOTS * len(dy_refs))
     lane = lax.broadcasted_iota(jnp.int32, (ROWS, d_gates.shape[1]), 1)
 
     @pl.when(expert == 0)
@@ -638,13 +637,11 @@
         d_gates[...] = jnp.zeros_like(d_gates)
 
     def work(count):
-        at = pl.ds(0, count)
-
         def one(i, carry):
             rows = rows_of(i)
             grad = grad_ref[rows, :]
             gate = spread_gate[0, rows, :]
-            taken = plain(patch_select(spread_place[0, rows, :], count), y_ref[at, :])
+            taken = taken_ref[0, rows, :].astype(FULLTYPE)
             d_gate = jnp.sum(grad * taken, -1, keepdims=True)
             d_gates[rows, :] += jnp.where(lane == expert, d_gate, 0.0)
             for first in range(0, D, 128):
@@ -755,6 +752,10 @@
 
 def spread_spec(seq):
     return pl.BlockSpec((1, seq, 128), lambda e: (e, 0, 0))
+
+
+def taken_spec(seq):
+    return pl.BlockSpec((1, seq, D), lambda e: (e, 0, 0))
 
 
 def block_shapes(experts, capacity):
@@ -797,29 +798,28 @@
         moe_down_kernel,
         experts,
         [SCALARS, whole((seq, D)), spread_spec(seq), spread_spec(seq), per(hidden), out_spec(w_out)],
-        [shaped((seq, D), FULLTYPE), shaped((experts * capacity, D), LOWTYPE)],
-        [whole((seq, D)), per(D)],
+        [shaped((seq, D), FULLTYPE), shaped((experts, seq, D), LOWTYPE)],
+        [whole((seq, D)), taken_spec(seq)],
         [loads, mid, spread_place, spread_gate, act, w_out],
         2 * experts * capacity * D * (hidden + seq),
-    )
-
-
-def moe_gate_backward(loads, grad, c16, router, gates, place, spread_place, spread_gate, y16):
+        [pltpu.VMEM((capacity, D), LOWTYPE)],
+    )
+
+
+def moe_gate_backward(loads, grad, c16, router, gates, place, spread_gate, taken, capacity):
     seq, experts = gates.shape
-    capacity = y16.shape[0] // experts
-    per = pl.BlockSpec((capacity, D), lambda e: (e, 0))
     return gridded(
         moe_gate_kernel,
         experts,
         [SCALARS, whole((seq, D)), whole((seq, D)), whole((D, experts)), whole((seq, experts))]
-        + [pl.BlockSpec((1, 1, seq), lambda e: (e, 0, 0)), spread_spec(seq), spread_spec(seq), per],
+        + [pl.BlockSpec((1, 1, seq), lambda e: (e, 0, 0)), spread_spec(seq), taken_spec(seq)],
         [
             shaped((D, experts), FULLTYPE),
             shaped((seq, D), FULLTYPE),
         ]
         + block_shapes(experts, capacity),
         [whole((D, experts)), whole((seq, D))] + block_specs(capacity),
-        [loads, grad, c16, router, gates, place, spread_place, spread_gate, y16],
+        [loads, grad, c16, router, gates, place, spread_gate, taken],
         4 * experts * capacity * D * seq,
         [
             pltpu.VMEM((seq, D), LOWTYPE),
@@ -949,14 +949,12 @@
     rest[...] = flat[pl.ds(start, rest.shape[0]), :]
 
 
-ORDERS = ((1, 2, 4, 8), (2, 4, 8, 1), (4, 8, 1, 2))
+ORDERS = ((4, 8, 1, 2), (4, 8, 2, 1))
 
 
 def chain_sizes(rows):
     units = rows // 16
-    first = max(1, units * 2 // 9)
-    second = (units - first) // 2
-    return [16 * first, 16 * second, 16 * (units - first - second)]
+    return [16 * (units // 2), 16 * (units - units // 2)]
 
 
 def gather_weights(part, shard, ep_place, dp_place, experts, beside):
@@ -966,7 +964,7 @@
     outs = [shaped((height, across * 128), LOWTYPE) for _, height, across in plan]
     outs.append(shaped((shard * owners // 128 - start, 128), FULLTYPE))
     flat = pltpu.VMEM((-(-(shard * (owners - 1) // 128 + rows) // 8) * 8, 128), FULLTYPE)
-    if (owners, groups) != (16, 2) or part.shape[0] < 48:
+    if (owners, groups) != (16, 2) or part.shape[0] < 32:
         parts = lax.all_gather(part, ("ep", "dp")).reshape(owners, rows, 128)
         kernel, args = (functools.partial(unpack_parts_kernel, plan, shard), [parts])
         return (local_call(kernel, outs, args, 0, [flat]), beside[0](*beside[1]))
@@ -1207,6 +1205,7 @@
         ),
     )
     table, place, loads, down, count_tok, counts, weight_sums = prepared
+    first_block, starts, table = together((first_block, starts, table))
     steps = [(axis, 2**k) for axis in ("dp", "ep") for k in range(lax.axis_size(axis).bit_length() - 1)]
     fourth = -(-len(steps) // 4)
 
@@ -1253,7 +1252,7 @@
     gates, spread_place, spread_gate, act1, slope1, *sent = moe_up(
         loads, c16, router, table, place, w_in, capacity
     )
-    x2, y16 = moe_down(loads, mid1, spread_place, spread_gate, act1, w_out)
+    x2, taken = moe_down(loads, mid1, spread_place, spread_gate, act1, w_out)
     x2, sent, total = together((x2, sent, total))
     total = add_steps(total, 3)
     rows_a = dispatch(sent[0])
@@ -1274,7 +1273,7 @@
     grad, sent, rows_b = together((grad, sent, rows_b))
     rows_c = dispatch(sent[2])
     d_own_router, d_c, *dy16 = moe_gate_backward(
-        loads, grad, c16, router, gates, place, spread_place, spread_gate, y16
+        loads, grad, c16, router, gates, place, spread_gate, taken, capacity
     )
     d_c, dy16, rows_c = together((d_c, dy16, rows_c))
     dy_a = dispatch(dy16[0])
@@ -1348,10 +1347,11 @@
     dense_grad = lax.dynamic_slice_in_dim(
         join_dp(own_sum, dp_place).reshape(-1), offset, shard
     )
+    own_grad = lax.dynamic_slice_in_dim(dense_grad, dp_place * piece, piece)
     sums = sum_all(
-        placed(local, 0, 2 + block_count)
-        + placed(jnp.sum(block_sums(dense_grad, d_in, d_out)), 1, 2 + block_count)
-        + jnp.pad(weight_sums, (2, 0))
+        together(placed(local, 0, 2 + block_count)
+        + placed(jnp.sum(own_grad * own_grad) + jnp.sum(d_in * d_in) + jnp.sum(d_out * d_out), 1, 2 + block_count)
+        + jnp.pad(weight_sums, (2, 0)))
     )
     loss, grad_total, weight_total = (sums[0] / total, sums[1], sums[2:])
     grad_norm = jnp.sqrt(grad_total)
@@ -1370,7 +1370,7 @@
     dense_m, dense_v, dense_step = moments(dense_weight, dense_first, dense_second, dense_grad)
     in_m, in_v, in_step = moments(expert_in, in_first, in_second, d_in)
     out_m, out_v, out_step = moments(expert_out, out_first, out_second, d_out)
-    update_total = sum_all(block_sums(dense_step, in_step, out_step))
+    update_total = sum_all(together(block_sums(dense_step, in_step, out_step)))
     weight_norm = jnp.sqrt(weight_total)
     update_norm = jnp.sqrt(update_total)
     ratio = weight_norm / (update_norm + EPS_NORM)

time: 905 us -> 860 us (0.950)
  waiting for transfers between devices: 118 us -> 166 us
  Pallas kernels: 467 us -> 421 us
  starting transfers between devices: 142 us -> 107 us
  other arithmetic: 89.4 us -> 71.5 us
    pallas_call x7, Pallas kernels: 227 us -> 199 us  [local_call(): pl.pallas_call(kernel, out_shape=outs, in_specs=in_vmem(len(args)), out_s...]
    ppermute x12 -> x8, waiting for transfers between devices: 41.4 us -> 63.8 us  [gather_weights(): lax.ppermute(v, 'ep', [(i, i ^ order[step]) for i in range(owners)])]
    ppermute x5, starting transfers between devices: 31.4 us -> 9.3 us  [add_steps(): lax.ppermute(value, axis, [(i, i ^ step) for i in range(count)])]
    pallas_call x6, Pallas kernels: 211 us -> 194 us  [gridded(): pl.pallas_call(kernel, grid=(steps,), out_shape=outs, in_specs=in_specs,...]
    all_to_all x7, waiting for transfers between devices: 25.9 us -> 41.3 us  [to_experts(): return lax.all_to_all(buffer, 'ep', split_axis=0, concat_axis=0, tiled=True)]
    add x9, other arithmetic: 9.98 us -> 0.03 us  [sum_all(): value + lax.ppermute(value, axis, [(i, i ^ step) for i in range(count)])]
    all_gather x1, waiting for transfers between devices: 24.7 us -> 34.6 us  [per_device(): all_out = lax.all_gather(low_out, ('ep', 'dp'))]
    ppermute x12 -> x8, starting transfers between devices: 19 us -> 13.7 us  [gather_weights(): lax.ppermute(v, 'ep', [(i, i ^ order[step]) for i in range(owners)])]
  transfers between devices with their start and end apart: 43 -> 38, of which waited for: 20 -> 23; matrix products, arithmetic and copies ran while one was open for 7% -> 7% of each run, Pallas kernels for 50% -> 48%
where the time goes in v4:
time: 860 us; the launch traced here: 849 us
  Pallas kernels  421 us (49%)
  waiting for transfers between devices  166 us (19%)
  starting transfers between devices  107 us (12%)
  other arithmetic  71.5 us (8%)
  between operations  43.6 us (5%)
  local copies, waits for them, and re-layouts  39.7 us (5%)
    pallas_call x7, Pallas kernels, local_call(): pl.pallas_call(kernel, out_shape=outs, in_specs=in_vmem(len(args)), out_s...  199 us
    pallas_call x6, Pallas kernels, gridded(): pl.pallas_call(kernel, grid=(steps,), out_shape=outs, in_specs=in_specs,...  194 us
    ppermute x8, waiting for transfers between devices, gather_weights(): lax.ppermute(v, 'ep', [(i, i ^ order[step]) for i in range(owners)])  63.8 us
    all_to_all x7, starting transfers between devices, to_experts(): return lax.all_to_all(buffer, 'ep', split_axis=0, concat_axis=0, tiled=True)  49.5 us
    all_to_all x7, waiting for transfers between devices, to_experts(): return lax.all_to_all(buffer, 'ep', split_axis=0, concat_axis=0, tiled=True)  41.3 us
    all_gather x1, waiting for transfers between devices, per_device(): all_out = lax.all_gather(low_out, ('ep', 'dp'))  34.6 us
    ppermute x10, starting transfers between devices, sum_all(): lax.ppermute(value, axis, [(i, i ^ step) for i in range(count)])  33.2 us
    unnamed x98, local copies, waits for them, and re-layouts  17.7 us
  transfers between devices with their start and end apart: 38, of which 23 were waited for; matrix products, arithmetic and copies ran while one was open for 7% of the time, Pallas kernels for 48%

profile of v4, /device:TPU:0, one launch (start us, length us, event | category | flops | bytes accessed | tf_op | source)
XLA Modules:
  0.0 848.5 jit_solution(5167637637619132585)
XLA Ops:
  11.1 5.2 dynamic_update_slice.3
  18.8 3.0 collective-permute-start.1
  23.4 11.6 %collective-permute-done = bf16[544,128]{1,0:T(8,128)(2,1)S(1)} collective-permute-done((bf16[544,128]{1,0:T(8,128)(2,1)S(1)}, bf16[544,128]{1,0:T(8,128)(2,1)S(1)}, u32[]{:S(2)}, u32[]{:S(2)}) %collective-permute-start) | collective-permute-done | bytes 139296 | tf_op jit(solution)/shard_map/ppermute | solution.py:976
  35.7 5.4 collective-permute-start.3
  54.1 22.9 %collective-permute-done.2 = bf16[1088,128]{1,0:T(8,128)(2,1)S(1)} collective-permute-done((bf16[1088,128]{1,0:T(8,128)(2,1)}, bf16[1088,128]{1,0:T(8,128)(2,1)S(1)}, u32[]{:S(2)}, u32[]{:S(2)}) %collective-permute-start.2) | collective-permute-done | bytes 278560 | tf_op jit(solution)/shard_map/ppermute | solution.py:976
  82.4 9.1 %collective-permute-done.4 = bf16[2176,128]{1,0:T(8,128)(2,1)S(1)} collective-permute-done((bf16[2176,128]{1,0:T(8,128)(2,1)S(1)}, bf16[2176,128]{1,0:T(8,128)(2,1)S(1)}, u32[]{:S(2)}, u32[]{:S(2)}) %collective-permute-start.4) | collective-permute-done | bytes 557088 | tf_op jit(solution)/shard_map/ppermute | solution.py:976
  98.7 5.1 fusion.45
  105.9 12.0 %select_reduce_fusion = f32[1024,40]{1,0:T(8,128)S(1)} fusion(f32[1024,256]{1,0:T(8,128)S(1)} %get-tuple-element.476, s32[1024,256]{1,0:T(8,128)S(1)} %copy-done.36), kind=kLoop, calls=%fused_computation | loop fusion | flops 31416320 | bytes 2260992 | tf_op jit(solution)/shard_map/reduce_sum | solution.py:1192
  117.9 16.0 %collective-permute-done.6 = bf16[4352,128]{1,0:T(8,128)(2,1)S(1)} collective-permute-done((bf16[4352,128]{1,0:T(8,128)(2,1)S(1)}, bf16[4352,128]{1,0:T(8,128)(2,1)S(1)}, u32[]{:S(2)}, u32[]{:S(2)}) %collective-permute-start.6) | collective-permute-done | bytes 1114144 | tf_op jit(solution)/shard_map/ppermute | solution.py:976
  133.9 4.2 collective-permute-done.7
  154.1 11.3 %shard_map.367 = (bf16[768,384]{1,0:T(8,128)(2,1)}, bf16[384,1152]{1,0:T(8,128)(2,1)}, bf16[384,1152]{1,0:T(8,128)(2,1)}, bf16[384,1152]{1,0:T(8,128)(2,1)}, bf1...) custom-call(s32[2]{0:T(128)} %pad_add_fusion.place_ref, ...), custom_call_target="tpu_custom_call" | custom-call | bytes 18072584 | tf_op jit(solution)/shard_map/pallas_call | solution.py:988
  168.7 29.1 %shard_map.368 = (f32[1024,384]{1,0:T(8,128)}, f32[1024,384]{1,0:T(8,128)}, bf16[1024,384]{1,0:T(8,128)(2,1)}, bf16[1024,1152]{1,0:T(8,128)(2,1)}, bf16[1024,384...) custom-call(bf16[1024,768]{1,0:T(8,128)(2,1)} %refs_15_.1, ...), custom_call_target="tpu_custom_call" | custom-call | flops 6845104128 | bytes 25378816 | tf_op jit(solution)/shard_map/pallas_call | solution.py:230
  199.1 20.2 %shard_map.369 = (f32[1024,384]{1,0:T(8,128)}, bf16[1024,384]{1,0:T(8,128)(2,1)}, bf16[1024,1152]{1,0:T(8,128)(2,1)}, bf16[1024,384]{1,0:T(8,128)(2,1)}, bf16[1024,768]{1,0:T(8,128)(2,1)}) custom-call(f32[1024,384]{1,0:T(8,128)} %get-tuple-element.185.refs_0_.refs_1_, bf16[384,1152]{1,0:T(8,128)(2,1)} %get-tuple-element.186.refs_1_.refs_6_, ...), custom_call_target="tpu_custom_call" | custom-call | flops 4429185024 | bytes 9846784 | tf_op jit(solution)/shard_map/pallas_call | solution.py:230
  224.1 3.3 collective-permute-start.14
  227.4 40.0 %shard_map.370 = (f32[1024,16]{1,0:T(8,128)}, f32[16,1024,128]{2,1,0:T(8,128)}, f32[16,1024,128]{2,1,0:T(8,128)}, bf16[6144,1536]{1,0:T(8,128)(2,1)}, f32[6144,1...) custom-call(s32[16]{0:T(128)} %convert_element_type.80.loads, ...), custom_call_target="tpu_custom_call" | custom-call | flops 12079595520 | bytes 97988672 | tf_op jit(solution)/shard_map/pallas_call | solution.py:730
  267.5 34.6 %all-gather.5.cloned.1.call-done = bf16[32,768,384]{2,1,0:T(8,128)(2,1)} async-done(((bf16[1,768,384]{2,1,0:T(8,128)(2,1)}), bf16[32,768,384]{2,1,0:T(8,128)(2,1)}) %all-gather.5.cloned.1.call-update) | async-done | bytes 18874384 | tf_op jit(solution)/shard_map/all_gather | solution.py:1171
  302.1 33.7 %shard_map.371 = (f32[1024,384]{1,0:T(8,128)}, bf16[16,1024,384]{2,1,0:T(8,128)(2,1)}) custom-call(s32[16]{0:T(128)} %convert_element_type.80.loads, f32[1024,384]{1,0:T(8,128)} %get-tuple-element.188.mid_ref.refs_2_, f32[16,1024,128]{2,1,0:T(8,128)} %get-tuple-element.196.spread_place, f32[16,1024,128]{2,1,0:T(8,128)} %get-tuple-element.197.spread_gate, ...), custom_call_target="tpu_custom_call" | custom-call | flops 12079595520 | bytes 70254656 | tf_op jit(solution)/shard_map/pallas_call | solution.py:730
  336.5 4.4 all-to-all-start
  341.5 27.4 %shard_map.372 = (f32[1024,384]{1,0:T(8,128)}, bf16[1024,384]{1,0:T(8,128)(2,1)}, bf16[1024,1152]{1,0:T(8,128)(2,1)}, bf16[1024,384]{1,0:T(8,128)(2,1)}, bf16[10...) custom-call(f32[1024,384]{1,0:T(8,128)} %get-tuple-element.204.refs_0_.refs_1_, ...), custom_call_target="tpu_custom_call" | custom-call | flops 6845104128 | bytes 23216128 | tf_op jit(solution)/shard_map/pallas_call | solution.py:230
  368.8 6.2 all-to-all-done
  376.2 8.7 %all-to-all-start.1 = ((bf16[16,128,384]{2,1,0:T(8,128)(2,1)}), bf16[16,128,384]{2,1,0:T(8,128)(2,1)}, u32[]{:S(2)}, u32[]{:S(2)}) async-start(bf16[16,128,384]{2,1,0:T(8,128)(2,1)} %get-tuple-element.229), calls=%async_computation.1 | async-start | bytes 3145728 | tf_op jit(solution)/shard_map/all_to_all | solution.py:1101
  387.6 5.0 shard_map.373
  392.6 41.2 %shard_map.374 = (f32[384,1152]{1,0:T(8,128)}, f32[384,384]{1,0:T(8,128)}, f32[8,384]{1,0:T(8,128)}, f32[384,1536]{1,0:T(8,128)}, f32[1536,384]{1,0:T(8,128)}, /*index=5*/f32[1024,384]{1,0:T(8,128)}) custom-call(f32[1024,384]{1,0:T(8,128)} %get-tuple-element.220.refs_0_, f32[1024,384]{1,0:T(8,128)} %get-tuple-element.204.refs_0_.refs_1_, ...), custom_call_target="tpu_custom_call" | custom-call | flops 15300820992 | bytes 31879168 | tf_op jit(solution)/shard_map/pallas_call | solution.py:230
  433.9 7.0 all-to-all-start.2
  440.9 23.8 %shard_map.375 = (f32[384,16]{1,0:T(8,128)}, f32[1024,384]{1,0:T(8,128)}, bf16[16,128,384]{2,1,0:T(8,128)(2,1)}, bf16[16,128,384]{2,1,0:T(8,128)(2,1)}, bf16[16,128,384]{2,1,0:T(8,128)(2,1)}) custom-call(s32[16]{0:T(128)} %convert_element_type.80.loads, f32[1024,384]{1,0:T(8,128)} %get-tuple-element.232.grad_ref.refs_0_, ...), custom_call_target="tpu_custom_call" | custom-call | flops 9663676416 | bytes 29790272 | tf_op jit(solution)/shard_map/pallas_call | solution.py:730
  464.7 9.4 %all-to-all-done.2 = bf16[16,128,384]{2,1,0:T(8,128)(2,1)S(1)} async-done(((bf16[16,128,384]{2,1,0:T(8,128)(2,1)}), bf16[16,128,384]{2,1,0:T(8,128)(2,1)S(1)}, u32[]{:S(2)}, u32[]{:S(2)}) %all-to-all-start.2) | async-done | bytes 1572896 | tf_op jit(solution)/shard_map/all_to_all | solution.py:1101
  475.3 7.3 all-to-all-start.3
  482.6 41.5 %shard_map.376.refs_10_ = f32[1024,384]{1,0:T(8,128)} custom-call(s32[16]{0:T(128)} %convert_element_type.80.loads, f32[1024,384]{1,0:T(8,128)} %get-tuple-element.241.start_ref, f32[16,1024,128]{2,1,0:T(8,128)} %get-tuple-element.196.spread_place, bf16[16,2,384,768]{3,2,1,0:T(8,128)(2,1)} %bitcast.129, bf16[16,1536,384]{2,1,0:T(8,128)(2,1)} %bitcast.126, ...), custom_call_target="tpu_custom_call" | custom-call | flops 19327352832 | bytes 91750464 | tf_op jit(solution)/shard_map/pallas_call | solution.py:730
  524.2 7.5 all-to-all-start.4
  531.7 31.5 %shard_map.377 = (f32[384,1152]{1,0:T(8,128)}, f32[384,384]{1,0:T(8,128)}, f32[8,384]{1,0:T(8,128)}, f32[1024,384]{1,0:T(8,128)}) custom-call(f32[1024,384]{1,0:T(8,128)} %get-tuple-element.232.grad_ref.refs_0_, f32[1024,384]{1,0:T(8,128)} %get-tuple-element.185.refs_0_.refs_1_, f32[1024,384]{1,0:T(8,128)} %get-tuple-element.188.mid_ref.refs_2_, ...), custom_call_target="tpu_custom_call" | custom-call | flops 10468982784 | bytes 16150528 | tf_op jit(solution)/shard_map/pallas_call | solution.py:230
  565.3 7.3 all-to-all-start.5
  573.9 44.5 %shard_map.378 = (f32[384,1152]{1,0:T(8,128)}, f32[384,384]{1,0:T(8,128)}, f32[8,384]{1,0:T(8,128)}, f32[384,1536]{1,0:T(8,128)}, f32[1536,384]{1,0:T(8,128)}, /*index=5*/f32[768,384]{1,0:T(8,128)}) custom-call(f32[1024,384]{1,0:T(8,128)} %get-tuple-element.255.refs_0_, f32[1024,384]{1,0:T(8,128)} %get-tuple-element.256.refs_1_, ...), custom_call_target="tpu_custom_call" | custom-call | flops 15904800768 | bytes 33058816 | tf_op jit(solution)/shard_map/pallas_call | solution.py:230
  618.4 17.0 %shard_map.381 = (f32[1,16,1104,128]{3,2,1,0:T(8,128)}, bf16[1,16,1104,128]{3,2,1,0:T(8,128)(2,1)}) custom-call(s32[1]{0:T(128)} %bitcast.17.place_ref, f32[768,384]{1,0:T(8,128)} %get-tuple-element.271.refs_0_, f32[384,1152]{1,0:T(8,128)} %get-tuple-element.272.refs_1_, f32[384,1152]{1,0:T(8,128)} %get-tuple-element.273.refs_2_, ...), custom_call_target="tpu_custom_call" | custom-call | bytes 31469572 | tf_op jit(solution)/shard_map/pallas_call | solution.py:1053
  635.4 7.8 collective-permute-done.17
  643.2 6.8 fusion
  650.0 7.1 all-to-all-start.6
  661.8 27.2 %shard_map.380 = (f32[384,768]{1,0:T(8,128)}, f32[768,384]{1,0:T(8,128)}) custom-call(bf16[2048,384]{1,0:T(8,128)(2,1)} %bitcast.133, bf16[2048,384]{1,0:T(8,128)(2,1)} %bitcast.41.refs_1_, bf16[2048,384]{1,0:T(8,128)(2,1)} %bitcast.135, bf16[2048,384]{1,0:T(8,128)(2,1)} %bitcast.43.refs_3_, bf16[2048,384]{1,0:T(8,128)(2,1)} %bitcast.137, ...), custom_call_target="tpu_custom_call" | custom-call | flops 18119393280 | bytes 12976128 | tf_op jit(solution)/shard_map/pallas_call | solution.py:730
  691.2 27.4 %shard_map.379 = (f32[384,768]{1,0:T(8,128)}, f32[768,384]{1,0:T(8,128)}) custom-call(bf16[2048,384]{1,0:T(8,128)(2,1)} %bitcast.134, bf16[2048,384]{1,0:T(8,128)(2,1)} %bitcast.41.refs_1_, bf16[2048,384]{1,0:T(8,128)(2,1)} %bitcast.136, bf16[2048,384]{1,0:T(8,128)(2,1)} %bitcast.43.refs_3_, bf16[2048,384]{1,0:T(8,128)(2,1)} %bitcast.138, ...), custom_call_target="tpu_custom_call" | custom-call | flops 18119393280 | bytes 12976128 | tf_op jit(solution)/shard_map/pallas_call | solution.py:730
  718.6 24.8 %all-to-all-done.6 = bf16[16,1104,128]{2,1,0:T(8,128)(2,1)} async-done(((bf16[16,1104,128]{2,1,0:T(8,128)(2,1)}), bf16[16,1104,128]{2,1,0:T(8,128)(2,1)}, u32[]{:S(2)}, u32[]{:S(2)}) %all-to-all-start.6) | async-done | bytes 4522016 | tf_op jit(solution)/shard_map/all_to_all | solution.py:1101
  743.4 3.9 convert_reduce_fusion
  757.9 2.9 collective-permute-start.20
  762.3 6.7 collective-permute-start.21
  770.5 11.7 %collective-permute-start.22 = (f32[48]{0:T(128)S(1)}, f32[48]{0:T(128)S(1)}, u32[]{:S(2)}, u32[]{:S(2)}) collective-permute-start(f32[48]{0:T(128)S(1)} %add.352), channel_id=1, source_target_pairs={{0,8},{2,10},{4,12},{6,14},{8,0},{10,2},{12,4},{14,6},{16,24},{18,... | collective-permute-start | bytes 584 | tf_op jit(solution)/shard_map/ppermute | solution.py:1095
  789.6 4.0 multiply_add_fusion.6
  793.7 2.9 multiply_reduce_fusion
  797.4 2.9 multiply_reduce_fusion.1
  801.4 4.5 fusion.46
  817.7 2.8 collective-permute-start.28
  (228 shorter events, 105.0 us)
Async XLA Ops:
  7.2 190.5 %all-gather.3.cloned.1.call-start = ((), (), s32[]{:S(2)}) async-start(), calls=%async_computation.7 | async-start | bytes 19464192 | tf_op jit(solution)/shard_map/all_gather | solution.py:1170
  9.5 292.6 %all-gather.5.cloned.1.call-start = ((), (), s32[]{:S(2)}) async-start(), calls=%async_computation.8 | async-start | bytes 19464192 | tf_op jit(solution)/shard_map/all_gather | solution.py:1171
  17.1 24.7 %copy-start.44 = (s32[16]{0:T(128)S(1)}, s32[16]{0:T(128)}, u32[]{:S(2)}) copy-start(s32[16]{0:T(128)} %constant.302.clone) | copy-start | bytes 196
  17.1 32.5 %copy-start.41 = (s32[18]{0:T(128)S(1)}, s32[18]{0:T(128)}, u32[]{:S(2)}) copy-start(s32[18]{0:T(128)} %constant.303.clone..sunk.10) | copy-start | bytes 220
  18.8 16.2 %collective-permute-start.1 = (bf16[560,128]{1,0:T(8,128)(2,1)S(1)}, bf16[560,128]{1,0:T(8,128)(2,1)S(1)}, u32[]{:S(2)}, u32[]{:S(2)}) collective-permute-start(bf16[560,128]{1,0:T(8,128)(2,1)S(1)} %get-tuple-element.472), channel_id=1, source_target_pairs={{0,8},{2,10},{4,12},{6,14},{8,0},{10,2},{12,4},{14,6},{16,24},{18,... | collective-permute-start | bytes 430088 | tf_op jit(solution)/shard_map/ppermute | solution.py:976
  23.4 11.6 %collective-permute-start = (bf16[544,128]{1,0:T(8,128)(2,1)S(1)}, bf16[544,128]{1,0:T(8,128)(2,1)S(1)}, u32[]{:S(2)}, u32[]{:S(2)}) collective-permute-start(bf16[544,128]{1,0:T(8,128)(2,1)S(1)} %get-tuple-element.474), channel_id=1, source_target_pairs={{0,8},{2,10},{4,12},{6,14},{8,0},{10,2},{12,4},{14,6},{16,24},{18,... | collective-permute-start | bytes 417800 | tf_op jit(solution)/shard_map/ppermute | solution.py:976
  35.7 41.3 %collective-permute-start.3 = (bf16[1120,128]{1,0:T(8,128)(2,1)}, bf16[1120,128]{1,0:T(8,128)(2,1)S(1)}, u32[]{:S(2)}, u32[]{:S(2)}) collective-permute-start(bf16[1120,128]{1,0:T(8,128)(2,1)} %pad_maximum_fusion.5), channel_id=1, source_target_pairs={{0,16},{2,18},{4,20},{6,22},{8,24},{10,26},{12,28},{14,30},{16,0},... | collective-permute-start | bytes 860168 | tf_op jit(solution)/shard_map/ppermute | solution.py:976
  41.8 35.2 %collective-permute-start.2 = (bf16[1088,128]{1,0:T(8,128)(2,1)}, bf16[1088,128]{1,0:T(8,128)(2,1)S(1)}, u32[]{:S(2)}, u32[]{:S(2)}) collective-permute-start(bf16[1088,128]{1,0:T(8,128)(2,1)} %pad_maximum_fusion.6), channel_id=1, source_target_pairs={{0,16},{2,18},{4,20},{6,22},{8,24},{10,26},{12,28},{14,30},{16,0},... | collective-permute-start | bytes 835592 | tf_op jit(solution)/shard_map/ppermute | solution.py:976
  77.1 14.5 %collective-permute-start.4 = (bf16[2176,128]{1,0:T(8,128)(2,1)S(1)}, bf16[2176,128]{1,0:T(8,128)(2,1)S(1)}, u32[]{:S(2)}, u32[]{:S(2)}) collective-permute-start(bf16[2176,128]{1,0:T(8,128)(2,1)S(1)} %pad_maximum_fusion.4), channel_id=1, source_target_pairs={{0,2},{2,0},{4,6},{6,4},{8,10},{10,8},{12,14},{14,12},{16,18},{18,... | collective-permute-start | bytes 1671176 | tf_op jit(solution)/shard_map/ppermute | solution.py:976
  78.6 13.0 %collective-permute-start.5 = (bf16[2240,128]{1,0:T(8,128)(2,1)S(1)}, bf16[2240,128]{1,0:T(8,128)(2,1)S(1)}, u32[]{:S(2)}, u32[]{:S(2)}) collective-permute-start(bf16[2240,128]{1,0:T(8,128)(2,1)S(1)} %pad_maximum_fusion.3), channel_id=1, source_target_pairs={{0,4},{2,6},{4,0},{6,2},{8,12},{10,14},{12,8},{14,10},{16,20},{18,... | collective-permute-start | bytes 1720328 | tf_op jit(solution)/shard_map/ppermute | solution.py:976
  91.6 42.3 %collective-permute-start.6 = (bf16[4352,128]{1,0:T(8,128)(2,1)S(1)}, bf16[4352,128]{1,0:T(8,128)(2,1)S(1)}, u32[]{:S(2)}, u32[]{:S(2)}) collective-permute-start(bf16[4352,128]{1,0:T(8,128)(2,1)S(1)} %pad_maximum_fusion.2), channel_id=1, source_target_pairs={{0,4},{2,6},{4,0},{6,2},{8,12},{10,14},{12,8},{14,10},{16,20},{18,... | collective-permute-start | bytes 3342344 | tf_op jit(solution)/shard_map/ppermute | solution.py:976
  93.2 44.9 %collective-permute-start.7 = (bf16[4480,128]{1,0:T(8,128)(2,1)S(1)}, bf16[4480,128]{1,0:T(8,128)(2,1)S(1)}, u32[]{:S(2)}, u32[]{:S(2)}) collective-permute-start(bf16[4480,128]{1,0:T(8,128)(2,1)S(1)} %pad_maximum_fusion), channel_id=1, source_target_pairs={{0,2},{2,0},{4,6},{6,4},{8,10},{10,8},{12,14},{14,12},{16,18},{18,... | collective-permute-start | bytes 3440648 | tf_op jit(solution)/shard_map/ppermute | solution.py:976
  96.9 6.9 copy-start.39
  96.9 6.9 copy-start.35
  139.2 13.5 %collective-permute-start.9 = (bf16[8960,128]{1,0:T(8,128)(2,1)}, bf16[8960,128]{1,0:T(8,128)(2,1)S(1)}, u32[]{:S(2)}, u32[]{:S(2)}) collective-permute-start(bf16[8960,128]{1,0:T(8,128)(2,1)} %constant_dynamic-update-slice_fusion.5.refs_1_), channel_id=1, source_target_pairs={{0,1},{1,0},{2,3},{3,2},{4,5},{5,4},{6,7},{7,6},{8,9},{9,8},{10,11... | collective-permute-start | bytes 6881288 | tf_op jit(solution)/shard_map/ppermute | solution.py:1069
  140.3 12.4 %collective-permute-start.8 = (bf16[8704,128]{1,0:T(8,128)(2,1)}, bf16[8704,128]{1,0:T(8,128)(2,1)}, u32[]{:S(2)}, u32[]{:S(2)}) collective-permute-start(bf16[8704,128]{1,0:T(8,128)(2,1)} %constant_dynamic-update-slice_fusion.refs_0_), channel_id=1, source_target_pairs={{0,1},{1,0},{2,3},{3,2},{4,5},{5,4},{6,7},{7,6},{8,9},{9,8},{10,11... | collective-permute-start | bytes 6684680 | tf_op jit(solution)/shard_map/ppermute | solution.py:1069
  143.7 3.5 collective-permute-start.10
  148.5 3.6 collective-permute-start.11
  197.7 21.5 %collective-permute-start.12 = (f32[1]{0:T(128)}, f32[1]{0:T(128)}, u32[]{:S(2)}, u32[]{:S(2)}) collective-permute-start(f32[1]{0:T(128)} %add.337), channel_id=1, source_target_pairs={{0,4},{2,6},{4,0},{6,2},{8,12},{10,14},{12,8},{14,10},{16,20},{18,... | collective-permute-start | bytes 20 | tf_op jit(solution)/shard_map/ppermute | solution.py:1215
  219.9 3.6 collective-permute-start.13
  224.1 111.7 %collective-permute-start.14 = (f32[1]{0:T(128)}, f32[1]{0:T(128)}, u32[]{:S(2)}, u32[]{:S(2)}) collective-permute-start(f32[1]{0:T(128)} %add.339), channel_id=1, source_target_pairs={{0,16},{2,18},{4,20},{6,22},{8,24},{10,26},{12,28},{14,30},{16,0},... | collective-permute-start | bytes 20 | tf_op jit(solution)/shard_map/ppermute | solution.py:1215
  336.5 38.6 %all-to-all-start = ((bf16[16,128,384]{2,1,0:T(8,128)(2,1)}), bf16[16,128,384]{2,1,0:T(8,128)(2,1)S(1)}, u32[]{:S(2)}, u32[]{:S(2)}) async-start(bf16[16,128,384]{2,1,0:T(8,128)(2,1)} %get-tuple-element.210), calls=%async_computation | async-start | bytes 3145728 | tf_op jit(solution)/shard_map/all_to_all | solution.py:1101
  376.2 57.7 %all-to-all-start.1 = ((bf16[16,128,384]{2,1,0:T(8,128)(2,1)}), bf16[16,128,384]{2,1,0:T(8,128)(2,1)}, u32[]{:S(2)}, u32[]{:S(2)}) async-start(bf16[16,128,384]{2,1,0:T(8,128)(2,1)} %get-tuple-element.229), calls=%async_computation.1 | async-start | bytes 3145728 | tf_op jit(solution)/shard_map/all_to_all | solution.py:1101
  433.9 40.3 %all-to-all-start.2 = ((bf16[16,128,384]{2,1,0:T(8,128)(2,1)}), bf16[16,128,384]{2,1,0:T(8,128)(2,1)S(1)}, u32[]{:S(2)}, u32[]{:S(2)}) async-start(bf16[16,128,384]{2,1,0:T(8,128)(2,1)} %get-tuple-element.239), calls=%async_computation.2 | async-start | bytes 3145728 | tf_op jit(solution)/shard_map/all_to_all | solution.py:1101
  475.3 48.9 %all-to-all-start.3 = ((bf16[16,128,384]{2,1,0:T(8,128)(2,1)}), bf16[16,128,384]{2,1,0:T(8,128)(2,1)}, u32[]{:S(2)}, u32[]{:S(2)}) async-start(bf16[16,128,384]{2,1,0:T(8,128)(2,1)} %get-tuple-element.243.refs_0_), calls=%async_computation.3 | async-start | bytes 3145728 | tf_op jit(solution)/shard_map/all_to_all | solution.py:1101
  524.2 39.9 %all-to-all-start.4 = ((bf16[16,128,384]{2,1,0:T(8,128)(2,1)}), bf16[16,128,384]{2,1,0:T(8,128)(2,1)S(1)}, u32[]{:S(2)}, u32[]{:S(2)}) async-start(bf16[16,128,384]{2,1,0:T(8,128)(2,1)} %get-tuple-element.252.refs_1_), calls=%async_computation.4 | async-start | bytes 3145728 | tf_op jit(solution)/shard_map/all_to_all | solution.py:1101
  564.1 8.6 %copy-start.38 = (f32[384,128]{1,0:T(8,128)S(1)}, f32[384,128]{1,0:T(8,128)}, u32[]{:S(2)}) copy-start(f32[384,128]{1,0:T(8,128)} %get-tuple-element.283) | copy-start | bytes 589828
  564.1 8.7 %copy-start.37 = (f32[384,16]{1,0:T(8,128)S(1)}, f32[384,16]{1,0:T(8,128)}, u32[]{:S(2)}) copy-start(f32[384,16]{1,0:T(8,128)} %get-tuple-element.282) | copy-start | bytes 73732
  565.3 53.1 %all-to-all-start.5 = ((bf16[16,128,384]{2,1,0:T(8,128)(2,1)}), bf16[16,128,384]{2,1,0:T(8,128)(2,1)}, u32[]{:S(2)}, u32[]{:S(2)}) async-start(bf16[16,128,384]{2,1,0:T(8,128)(2,1)} %get-tuple-element.265.refs_2_), calls=%async_computation.5 | async-start | bytes 3145728 | tf_op jit(solution)/shard_map/all_to_all | solution.py:1101
  635.4 7.8 collective-permute-start.17
  650.0 93.5 %all-to-all-start.6 = ((bf16[16,1104,128]{2,1,0:T(8,128)(2,1)}), bf16[16,1104,128]{2,1,0:T(8,128)(2,1)}, u32[]{:S(2)}, u32[]{:S(2)}) async-start(bf16[16,1104,128]{2,1,0:T(8,128)(2,1)} %fusion), calls=%async_computation.6 | async-start | bytes 9043968 | tf_op jit(solution)/shard_map/all_to_all | solution.py:1101
  690.4 28.1 %collective-permute-start.15 = (bf16[384,768]{1,0:T(8,128)(2,1)S(1)}, bf16[384,768]{1,0:T(8,128)(2,1)S(1)}, u32[]{:S(2)}, u32[]{:S(2)}) collective-permute-start(bf16[384,768]{1,0:T(8,128)(2,1)S(1)} %convert_element_type.86), channel_id=1, source_target_pairs={{0,1},{1,0},{2,3},{3,2},{4,5},{5,4},{6,7},{7,6},{8,9},{9,8},{10,11... | collective-permute-start | bytes 1769480 | tf_op jit(solution)/shard_map/ppermute | solution.py:1069
  690.7 27.9 %collective-permute-start.16 = (bf16[768,384]{1,0:T(8,128)(2,1)S(1)}, bf16[768,384]{1,0:T(8,128)(2,1)S(1)}, u32[]{:S(2)}, u32[]{:S(2)}) collective-permute-start(bf16[768,384]{1,0:T(8,128)(2,1)S(1)} %convert_element_type.87), channel_id=1, source_target_pairs={{0,1},{1,0},{2,3},{3,2},{4,5},{5,4},{6,7},{7,6},{8,9},{9,8},{10,11... | collective-permute-start | bytes 1769480 | tf_op jit(solution)/shard_map/ppermute | solution.py:1069
  718.6 31.4 %copy-start.18 = (bf16[384,768]{1,0:T(8,128)(2,1)}, bf16[384,768]{1,0:T(8,128)(2,1)S(1)}, u32[]{:S(2)}) copy-start(bf16[384,768]{1,0:T(8,128)(2,1)S(1)} %collective-permute-done.15) | copy-start | bytes 1769476
  718.6 32.3 %copy-start.20 = (bf16[768,384]{1,0:T(8,128)(2,1)}, bf16[768,384]{1,0:T(8,128)(2,1)S(1)}, u32[]{:S(2)}) copy-start(bf16[768,384]{1,0:T(8,128)(2,1)S(1)} %collective-permute-done.16) | copy-start | bytes 1769476
  747.3 4.5 collective-permute-start.18
  753.1 36.4 %copy-start.5 = (f32[279312]{0:T(1024)S(1)}, f32[279312]{0:T(1024)}, u32[]{:S(2)}) copy-start(f32[279312]{0:T(1024)} %param.30) | copy-start | bytes 3351748
  756.1 1.7 collective-permute-start.19
  757.9 4.4 collective-permute-start.20
  762.3 8.3 collective-permute-start.21
  770.5 13.2 %collective-permute-start.22 = (f32[48]{0:T(128)S(1)}, f32[48]{0:T(128)S(1)}, u32[]{:S(2)}, u32[]{:S(2)}) collective-permute-start(f32[48]{0:T(128)S(1)} %add.352), channel_id=1, source_target_pairs={{0,8},{2,10},{4,12},{6,14},{8,0},{10,2},{12,4},{14,6},{16,24},{18,... | collective-permute-start | bytes 584 | tf_op jit(solution)/shard_map/ppermute | solution.py:1095
  783.7 4.4 collective-permute-start.23
  793.6 6.7 copy-start.6
  805.9 1.2 collective-permute-start.24
  807.1 3.5 collective-permute-start.25
  810.7 3.5 collective-permute-start.26
  814.2 3.5 collective-permute-start.27
  817.7 4.4 collective-permute-start.28
  (35 other events, 89.3 us)
Sparse Core Ops, SparseCore 0:
  11.5 164.5 all-gather.2
  179.6 122.4 all-gather.4

commit v5 on v4

--- a/solution.py
+++ b/solution.py
@@ -1259,13 +1259,12 @@
     *kept2, x3, act2, slope2 = layer_forward(
         x2, None, w_qkv[2], w_attn[2], norm_rows(2), down, w_up[1], w_down[1]
     )
-    x3, sent, rows_a = together((x3, sent, rows_a))
-    rows_b = dispatch(sent[1])
     loss_lanes, d_head, d_normf, grad = head_call(
         x3, norm_rows(3), w_head, counts, count_tok, total
     )
     local = loss_lanes[0, 0]
-    grad, local = together((grad, local))
+    grad, local, sent, rows_a = together((grad, local, sent, rows_a))
+    rows_b = dispatch(sent[1])
     d_qkv2, d_attn2, d_norm2, d_up1, d_down1, grad = layer_backward(
         grad, x2, (*kept2, act2, slope2), w_qkv[2], w_attn[2], norm_rows(2), down,
         (w_up[1], w_down[1]), None, None,

time: 860 us -> 856 us (level)
  waiting for transfers between devices: 166 us -> 150 us
  Pallas kernels: 421 us -> 433 us
    pallas_call x7, Pallas kernels: 199 us -> 211 us  [local_call(): pl.pallas_call(kernel, out_shape=outs, in_specs=in_vmem(len(args)), out_s...]
    all_gather x1, waiting for transfers between devices: 34.6 us -> 23.2 us  [per_device(): all_out = lax.all_gather(low_out, ('ep', 'dp'))]
    unnamed x98 -> x104, local copies, waits for them, and re-layouts: 17.7 us -> 20 us
  transfers between devices with their start and end apart: 38 -> 38, of which waited for: 23 -> 22; matrix products, arithmetic and copies ran while one was open for 7% -> 7% of each run, Pallas kernels for 48% -> 49%
where the time goes in v5:
time: 856 us; the launch traced here: 845 us
  Pallas kernels  433 us (51%)
  waiting for transfers between devices  150 us (18%)
  starting transfers between devices  104 us (12%)
  other arithmetic  71.5 us (8%)
  between operations  43.6 us (5%)
  local copies, waits for them, and re-layouts  42 us (5%)
    pallas_call x7, Pallas kernels, local_call(): pl.pallas_call(kernel, out_shape=outs, in_specs=in_vmem(len(args)), out_s...  211 us
    pallas_call x6, Pallas kernels, gridded(): pl.pallas_call(kernel, grid=(steps,), out_shape=outs, in_specs=in_specs,...  193 us
    ppermute x8, waiting for transfers between devices, gather_weights(): lax.ppermute(v, 'ep', [(i, i ^ order[step]) for i in range(owners)])  63.7 us
    all_to_all x7, starting transfers between devices, to_experts(): return lax.all_to_all(buffer, 'ep', split_axis=0, concat_axis=0, tiled=True)  46.7 us
    all_to_all x7, waiting for transfers between devices, to_experts(): return lax.all_to_all(buffer, 'ep', split_axis=0, concat_axis=0, tiled=True)  37.3 us
    ppermute x10, starting transfers between devices, sum_all(): lax.ppermute(value, axis, [(i, i ^ step) for i in range(count)])  33.2 us
    all_gather x1, waiting for transfers between devices, per_device(): all_out = lax.all_gather(low_out, ('ep', 'dp'))  23.2 us
    unnamed x104, local copies, waits for them, and re-layouts  20 us
  transfers between devices with their start and end apart: 38, of which 22 were waited for; matrix products, arithmetic and copies ran while one was open for 7% of the time, Pallas kernels for 49%

profile of v5, /device:TPU:0, one launch (start us, length us, event | category | flops | bytes accessed | tf_op | source)
XLA Modules:
  0.0 845.2 jit_solution(16449326672684048913)
XLA Ops:
  11.1 5.2 dynamic_update_slice.3
  18.8 3.0 collective-permute-start.1
  23.4 11.6 %collective-permute-done = bf16[544,128]{1,0:T(8,128)(2,1)S(1)} collective-permute-done((bf16[544,128]{1,0:T(8,128)(2,1)S(1)}, bf16[544,128]{1,0:T(8,128)(2,1)S(1)}, u32[]{:S(2)}, u32[]{:S(2)}) %collective-permute-start) | collective-permute-done | bytes 139296 | tf_op jit(solution)/shard_map/ppermute | solution.py:976
  35.7 5.4 collective-permute-start.3
  54.2 22.9 %collective-permute-done.2 = bf16[1088,128]{1,0:T(8,128)(2,1)S(1)} collective-permute-done((bf16[1088,128]{1,0:T(8,128)(2,1)}, bf16[1088,128]{1,0:T(8,128)(2,1)S(1)}, u32[]{:S(2)}, u32[]{:S(2)}) %collective-permute-start.2) | collective-permute-done | bytes 278560 | tf_op jit(solution)/shard_map/ppermute | solution.py:976
  82.3 9.2 %collective-permute-done.4 = bf16[2176,128]{1,0:T(8,128)(2,1)S(1)} collective-permute-done((bf16[2176,128]{1,0:T(8,128)(2,1)S(1)}, bf16[2176,128]{1,0:T(8,128)(2,1)S(1)}, u32[]{:S(2)}, u32[]{:S(2)}) %collective-permute-start.4) | collective-permute-done | bytes 557088 | tf_op jit(solution)/shard_map/ppermute | solution.py:976
  98.7 5.2 fusion.45
  106.0 12.0 %select_reduce_fusion = f32[1024,40]{1,0:T(8,128)S(1)} fusion(f32[1024,256]{1,0:T(8,128)S(1)} %get-tuple-element.474, s32[1024,256]{1,0:T(8,128)S(1)} %copy-done.39), kind=kLoop, calls=%fused_computation | loop fusion | flops 31416320 | bytes 2260992 | tf_op jit(solution)/shard_map/reduce_sum | solution.py:1192
  118.0 15.8 %collective-permute-done.6 = bf16[4352,128]{1,0:T(8,128)(2,1)S(1)} collective-permute-done((bf16[4352,128]{1,0:T(8,128)(2,1)S(1)}, bf16[4352,128]{1,0:T(8,128)(2,1)S(1)}, u32[]{:S(2)}, u32[]{:S(2)}) %collective-permute-start.6) | collective-permute-done | bytes 1114144 | tf_op jit(solution)/shard_map/ppermute | solution.py:976
  133.8 4.2 collective-permute-done.7
  154.1 11.3 %shard_map.367 = (bf16[768,384]{1,0:T(8,128)(2,1)}, bf16[384,1152]{1,0:T(8,128)(2,1)}, bf16[384,1152]{1,0:T(8,128)(2,1)}, bf16[384,1152]{1,0:T(8,128)(2,1)}, bf1...) custom-call(s32[2]{0:T(128)} %pad_add_fusion.place_ref, ...), custom_call_target="tpu_custom_call" | custom-call | bytes 18072584 | tf_op jit(solution)/shard_map/pallas_call | solution.py:988
  168.7 28.9 %shard_map.368 = (f32[1024,384]{1,0:T(8,128)}, f32[1024,384]{1,0:T(8,128)}, bf16[1024,384]{1,0:T(8,128)(2,1)}, bf16[1024,1152]{1,0:T(8,128)(2,1)}, bf16[1024,384...) custom-call(bf16[1024,768]{1,0:T(8,128)(2,1)} %refs_15_.1, ...), custom_call_target="tpu_custom_call" | custom-call | flops 6845104128 | bytes 25378816 | tf_op jit(solution)/shard_map/pallas_call | solution.py:230
  198.9 32.3 %shard_map.369 = (f32[1024,384]{1,0:T(8,128)}, bf16[1024,384]{1,0:T(8,128)(2,1)}, bf16[1024,1152]{1,0:T(8,128)(2,1)}, bf16[1024,384]{1,0:T(8,128)(2,1)}, bf16[1024,768]{1,0:T(8,128)(2,1)}) custom-call(f32[1024,384]{1,0:T(8,128)} %get-tuple-element.184.refs_0_.refs_1_, bf16[384,1152]{1,0:T(8,128)(2,1)} %get-tuple-element.185.refs_1_.refs_6_, ...), custom_call_target="tpu_custom_call" | custom-call | flops 4429185024 | bytes 9846784 | tf_op jit(solution)/shard_map/pallas_call | solution.py:230
  236.2 3.3 collective-permute-start.14
  239.4 39.4 %shard_map.370 = (f32[1024,16]{1,0:T(8,128)}, f32[16,1024,128]{2,1,0:T(8,128)}, f32[16,1024,128]{2,1,0:T(8,128)}, bf16[6144,1536]{1,0:T(8,128)(2,1)}, f32[6144,1...) custom-call(s32[16]{0:T(128)} %convert_element_type.80.loads, ...), custom_call_target="tpu_custom_call" | custom-call | flops 12079595520 | bytes 97988672 | tf_op jit(solution)/shard_map/pallas_call | solution.py:730
  278.9 23.2 %all-gather.5.cloned.1.call-done = bf16[32,768,384]{2,1,0:T(8,128)(2,1)} async-done(((bf16[1,768,384]{2,1,0:T(8,128)(2,1)}), bf16[32,768,384]{2,1,0:T(8,128)(2,1)}) %all-gather.5.cloned.1.call-update) | async-done | bytes 18874384 | tf_op jit(solution)/shard_map/all_gather | solution.py:1171
  302.1 33.8 %shard_map.371 = (f32[1024,384]{1,0:T(8,128)}, bf16[16,1024,384]{2,1,0:T(8,128)(2,1)}) custom-call(s32[16]{0:T(128)} %convert_element_type.80.loads, f32[1024,384]{1,0:T(8,128)} %get-tuple-element.187.mid_ref.refs_2_, f32[16,1024,128]{2,1,0:T(8,128)} %get-tuple-element.195.spread_place, f32[16,1024,128]{2,1,0:T(8,128)} %get-tuple-element.196.spread_gate, ...), custom_call_target="tpu_custom_call" | custom-call | flops 12079595520 | bytes 70254656 | tf_op jit(solution)/shard_map/pallas_call | solution.py:730
  336.6 3.9 all-to-all-start
  343.8 27.4 %shard_map.372 = (f32[1024,384]{1,0:T(8,128)}, bf16[1024,384]{1,0:T(8,128)(2,1)}, bf16[1024,1152]{1,0:T(8,128)(2,1)}, bf16[1024,384]{1,0:T(8,128)(2,1)}, bf16[10...) custom-call(f32[1024,384]{1,0:T(8,128)} %get-tuple-element.203.refs_0_.refs_1_, ...), custom_call_target="tpu_custom_call" | custom-call | flops 6845104128 | bytes 23216128 | tf_op jit(solution)/shard_map/pallas_call | solution.py:230
  371.2 5.1 shard_map.373
  377.4 7.3 all-to-all-start.1
  384.7 41.4 %shard_map.374 = (f32[384,1152]{1,0:T(8,128)}, f32[384,384]{1,0:T(8,128)}, f32[8,384]{1,0:T(8,128)}, f32[384,1536]{1,0:T(8,128)}, f32[1536,384]{1,0:T(8,128)}, /*index=5*/f32[1024,384]{1,0:T(8,128)}) custom-call(f32[1024,384]{1,0:T(8,128)} %get-tuple-element.218.refs_0_, f32[1024,384]{1,0:T(8,128)} %get-tuple-element.203.refs_0_.refs_1_, ...), custom_call_target="tpu_custom_call" | custom-call | flops 15300820992 | bytes 31879168 | tf_op jit(solution)/shard_map/pallas_call | solution.py:230
  427.3 7.0 all-to-all-start.2
  434.3 23.8 %shard_map.375 = (f32[384,16]{1,0:T(8,128)}, f32[1024,384]{1,0:T(8,128)}, bf16[16,128,384]{2,1,0:T(8,128)(2,1)}, bf16[16,128,384]{2,1,0:T(8,128)(2,1)}, bf16[16,128,384]{2,1,0:T(8,128)(2,1)}) custom-call(s32[16]{0:T(128)} %convert_element_type.80.loads, f32[1024,384]{1,0:T(8,128)} %get-tuple-element.230.grad_ref.refs_0_, ...), custom_call_target="tpu_custom_call" | custom-call | flops 9663676416 | bytes 29790272 | tf_op jit(solution)/shard_map/pallas_call | solution.py:730
  458.1 10.1 %all-to-all-done.2 = bf16[16,128,384]{2,1,0:T(8,128)(2,1)S(1)} async-done(((bf16[16,128,384]{2,1,0:T(8,128)(2,1)}), bf16[16,128,384]{2,1,0:T(8,128)(2,1)S(1)}, u32[]{:S(2)}, u32[]{:S(2)}) %all-to-all-start.2) | async-done | bytes 1572896 | tf_op jit(solution)/shard_map/all_to_all | solution.py:1101
  469.4 7.3 all-to-all-start.3
  476.7 41.7 %shard_map.376.refs_10_ = f32[1024,384]{1,0:T(8,128)} custom-call(s32[16]{0:T(128)} %convert_element_type.80.loads, f32[1024,384]{1,0:T(8,128)} %get-tuple-element.239.start_ref, f32[16,1024,128]{2,1,0:T(8,128)} %get-tuple-element.195.spread_place, bf16[16,2,384,768]{3,2,1,0:T(8,128)(2,1)} %bitcast.129, bf16[16,1536,384]{2,1,0:T(8,128)(2,1)} %bitcast.126, ...), custom_call_target="tpu_custom_call" | custom-call | flops 19327352832 | bytes 91750464 | tf_op jit(solution)/shard_map/pallas_call | solution.py:730
  519.6 6.7 all-to-all-start.4
  526.3 31.6 %shard_map.377 = (f32[384,1152]{1,0:T(8,128)}, f32[384,384]{1,0:T(8,128)}, f32[8,384]{1,0:T(8,128)}, f32[1024,384]{1,0:T(8,128)}) custom-call(f32[1024,384]{1,0:T(8,128)} %get-tuple-element.230.grad_ref.refs_0_, f32[1024,384]{1,0:T(8,128)} %get-tuple-element.184.refs_0_.refs_1_, f32[1024,384]{1,0:T(8,128)} %get-tuple-element.187.mid_ref.refs_2_, ...), custom_call_target="tpu_custom_call" | custom-call | flops 10468982784 | bytes 16150528 | tf_op jit(solution)/shard_map/pallas_call | solution.py:230
  561.3 7.3 all-to-all-start.5
  569.9 44.5 %shard_map.378 = (f32[384,1152]{1,0:T(8,128)}, f32[384,384]{1,0:T(8,128)}, f32[8,384]{1,0:T(8,128)}, f32[384,1536]{1,0:T(8,128)}, f32[1536,384]{1,0:T(8,128)}, /*index=5*/f32[768,384]{1,0:T(8,128)}) custom-call(f32[1024,384]{1,0:T(8,128)} %get-tuple-element.253.refs_0_, f32[1024,384]{1,0:T(8,128)} %get-tuple-element.254.refs_1_, ...), custom_call_target="tpu_custom_call" | custom-call | flops 15904800768 | bytes 33058816 | tf_op jit(solution)/shard_map/pallas_call | solution.py:230
  614.4 17.5 %shard_map.381 = (f32[1,16,1104,128]{3,2,1,0:T(8,128)}, bf16[1,16,1104,128]{3,2,1,0:T(8,128)(2,1)}) custom-call(s32[1]{0:T(128)} %bitcast.17.place_ref, f32[768,384]{1,0:T(8,128)} %get-tuple-element.269.refs_0_, f32[384,1152]{1,0:T(8,128)} %get-tuple-element.270.refs_1_, f32[384,1152]{1,0:T(8,128)} %get-tuple-element.271.refs_2_, ...), custom_call_target="tpu_custom_call" | custom-call | bytes 31469572 | tf_op jit(solution)/shard_map/pallas_call | solution.py:1053
  632.0 7.8 collective-permute-done.17
  639.8 6.8 fusion
  646.6 7.2 all-to-all-start.6
  658.5 27.2 %shard_map.380 = (f32[384,768]{1,0:T(8,128)}, f32[768,384]{1,0:T(8,128)}) custom-call(bf16[2048,384]{1,0:T(8,128)(2,1)} %bitcast.133, bf16[2048,384]{1,0:T(8,128)(2,1)} %bitcast.135, bf16[2048,384]{1,0:T(8,128)(2,1)} %bitcast.137, bf16[2048,384]{1,0:T(8,128)(2,1)} %bitcast.139, bf16[2048,384]{1,0:T(8,128)(2,1)} %bitcast.141, bf16[2048,384]{1,0:T(8,128)(2,1)} %bitcast.143, ...), custom_call_target="tpu_custom_call" | custom-call | flops 18119393280 | bytes 12976128 | tf_op jit(solution)/shard_map/pallas_call | solution.py:730
  687.8 27.4 %shard_map.379 = (f32[384,768]{1,0:T(8,128)}, f32[768,384]{1,0:T(8,128)}) custom-call(bf16[2048,384]{1,0:T(8,128)(2,1)} %bitcast.134, bf16[2048,384]{1,0:T(8,128)(2,1)} %bitcast.136, bf16[2048,384]{1,0:T(8,128)(2,1)} %bitcast.138, bf16[2048,384]{1,0:T(8,128)(2,1)} %bitcast.140, bf16[2048,384]{1,0:T(8,128)(2,1)} %bitcast.142, bf16[2048,384]{1,0:T(8,128)(2,1)} %bitcast.144, ...), custom_call_target="tpu_custom_call" | custom-call | flops 18119393280 | bytes 12976128 | tf_op jit(solution)/shard_map/pallas_call | solution.py:730
  715.2 24.8 %all-to-all-done.6 = bf16[16,1104,128]{2,1,0:T(8,128)(2,1)} async-done(((bf16[16,1104,128]{2,1,0:T(8,128)(2,1)}), bf16[16,1104,128]{2,1,0:T(8,128)(2,1)}, u32[]{:S(2)}, u32[]{:S(2)}) %all-to-all-start.6) | async-done | bytes 4522016 | tf_op jit(solution)/shard_map/all_to_all | solution.py:1101
  740.1 3.9 convert_reduce_fusion
  754.5 2.9 collective-permute-start.20
  758.9 6.7 collective-permute-start.21
  767.2 11.7 %collective-permute-start.22 = (f32[48]{0:T(128)S(1)}, f32[48]{0:T(128)S(1)}, u32[]{:S(2)}, u32[]{:S(2)}) collective-permute-start(f32[48]{0:T(128)S(1)} %add.352), channel_id=1, source_target_pairs={{0,8},{2,10},{4,12},{6,14},{8,0},{10,2},{12,4},{14,6},{16,24},{18,... | collective-permute-start | bytes 584 | tf_op jit(solution)/shard_map/ppermute | solution.py:1095
  780.4 2.8 collective-permute-start.23
  786.2 4.0 multiply_add_fusion.6
  790.3 2.9 multiply_reduce_fusion
  794.0 2.9 multiply_reduce_fusion.1
  798.0 4.5 fusion.46
  814.4 2.8 collective-permute-start.28
  (234 shorter events, 106.3 us)
Async XLA Ops:
  7.2 190.3 %all-gather.3.cloned.1.call-start = ((), (), s32[]{:S(2)}) async-start(), calls=%async_computation.7 | async-start | bytes 19464192 | tf_op jit(solution)/shard_map/all_gather | solution.py:1170
  9.5 292.6 %all-gather.5.cloned.1.call-start = ((), (), s32[]{:S(2)}) async-start(), calls=%async_computation.8 | async-start | bytes 19464192 | tf_op jit(solution)/shard_map/all_gather | solution.py:1171
  17.1 24.7 %copy-start.47 = (s32[16]{0:T(128)S(1)}, s32[16]{0:T(128)}, u32[]{:S(2)}) copy-start(s32[16]{0:T(128)} %constant.302.clone) | copy-start | bytes 196
  17.1 32.5 %copy-start.44 = (s32[18]{0:T(128)S(1)}, s32[18]{0:T(128)}, u32[]{:S(2)}) copy-start(s32[18]{0:T(128)} %constant.303.clone..sunk.10) | copy-start | bytes 220
  18.8 16.2 %collective-permute-start.1 = (bf16[560,128]{1,0:T(8,128)(2,1)S(1)}, bf16[560,128]{1,0:T(8,128)(2,1)S(1)}, u32[]{:S(2)}, u32[]{:S(2)}) collective-permute-start(bf16[560,128]{1,0:T(8,128)(2,1)S(1)} %get-tuple-element.470), channel_id=1, source_target_pairs={{0,8},{2,10},{4,12},{6,14},{8,0},{10,2},{12,4},{14,6},{16,24},{18,... | collective-permute-start | bytes 430088 | tf_op jit(solution)/shard_map/ppermute | solution.py:976
  23.4 11.6 %collective-permute-start = (bf16[544,128]{1,0:T(8,128)(2,1)S(1)}, bf16[544,128]{1,0:T(8,128)(2,1)S(1)}, u32[]{:S(2)}, u32[]{:S(2)}) collective-permute-start(bf16[544,128]{1,0:T(8,128)(2,1)S(1)} %get-tuple-element.472), channel_id=1, source_target_pairs={{0,8},{2,10},{4,12},{6,14},{8,0},{10,2},{12,4},{14,6},{16,24},{18,... | collective-permute-start | bytes 417800 | tf_op jit(solution)/shard_map/ppermute | solution.py:976
  35.7 41.3 %collective-permute-start.3 = (bf16[1120,128]{1,0:T(8,128)(2,1)}, bf16[1120,128]{1,0:T(8,128)(2,1)S(1)}, u32[]{:S(2)}, u32[]{:S(2)}) collective-permute-start(bf16[1120,128]{1,0:T(8,128)(2,1)} %pad_maximum_fusion.5), channel_id=1, source_target_pairs={{0,16},{2,18},{4,20},{6,22},{8,24},{10,26},{12,28},{14,30},{16,0},... | collective-permute-start | bytes 860168 | tf_op jit(solution)/shard_map/ppermute | solution.py:976
  41.9 35.2 %collective-permute-start.2 = (bf16[1088,128]{1,0:T(8,128)(2,1)}, bf16[1088,128]{1,0:T(8,128)(2,1)S(1)}, u32[]{:S(2)}, u32[]{:S(2)}) collective-permute-start(bf16[1088,128]{1,0:T(8,128)(2,1)} %pad_maximum_fusion.6), channel_id=1, source_target_pairs={{0,16},{2,18},{4,20},{6,22},{8,24},{10,26},{12,28},{14,30},{16,0},... | collective-permute-start | bytes 835592 | tf_op jit(solution)/shard_map/ppermute | solution.py:976
  77.1 14.5 %collective-permute-start.4 = (bf16[2176,128]{1,0:T(8,128)(2,1)S(1)}, bf16[2176,128]{1,0:T(8,128)(2,1)S(1)}, u32[]{:S(2)}, u32[]{:S(2)}) collective-permute-start(bf16[2176,128]{1,0:T(8,128)(2,1)S(1)} %pad_maximum_fusion.4), channel_id=1, source_target_pairs={{0,2},{2,0},{4,6},{6,4},{8,10},{10,8},{12,14},{14,12},{16,18},{18,... | collective-permute-start | bytes 1671176 | tf_op jit(solution)/shard_map/ppermute | solution.py:976
  78.6 12.9 %collective-permute-start.5 = (bf16[2240,128]{1,0:T(8,128)(2,1)S(1)}, bf16[2240,128]{1,0:T(8,128)(2,1)S(1)}, u32[]{:S(2)}, u32[]{:S(2)}) collective-permute-start(bf16[2240,128]{1,0:T(8,128)(2,1)S(1)} %pad_maximum_fusion.3), channel_id=1, source_target_pairs={{0,4},{2,6},{4,0},{6,2},{8,12},{10,14},{12,8},{14,10},{16,20},{18,... | collective-permute-start | bytes 1720328 | tf_op jit(solution)/shard_map/ppermute | solution.py:976
  91.6 42.2 %collective-permute-start.6 = (bf16[4352,128]{1,0:T(8,128)(2,1)S(1)}, bf16[4352,128]{1,0:T(8,128)(2,1)S(1)}, u32[]{:S(2)}, u32[]{:S(2)}) collective-permute-start(bf16[4352,128]{1,0:T(8,128)(2,1)S(1)} %pad_maximum_fusion.2), channel_id=1, source_target_pairs={{0,4},{2,6},{4,0},{6,2},{8,12},{10,14},{12,8},{14,10},{16,20},{18,... | collective-permute-start | bytes 3342344 | tf_op jit(solution)/shard_map/ppermute | solution.py:976
  93.2 44.8 %collective-permute-start.7 = (bf16[4480,128]{1,0:T(8,128)(2,1)S(1)}, bf16[4480,128]{1,0:T(8,128)(2,1)S(1)}, u32[]{:S(2)}, u32[]{:S(2)}) collective-permute-start(bf16[4480,128]{1,0:T(8,128)(2,1)S(1)} %pad_maximum_fusion), channel_id=1, source_target_pairs={{0,2},{2,0},{4,6},{6,4},{8,10},{10,8},{12,14},{14,12},{16,18},{18,... | collective-permute-start | bytes 3440648 | tf_op jit(solution)/shard_map/ppermute | solution.py:976
  96.9 7.0 copy-start.42
  96.9 7.0 copy-start.38
  139.2 13.5 %collective-permute-start.9 = (bf16[8960,128]{1,0:T(8,128)(2,1)}, bf16[8960,128]{1,0:T(8,128)(2,1)S(1)}, u32[]{:S(2)}, u32[]{:S(2)}) collective-permute-start(bf16[8960,128]{1,0:T(8,128)(2,1)} %constant_dynamic-update-slice_fusion.5.refs_1_), channel_id=1, source_target_pairs={{0,1},{1,0},{2,3},{3,2},{4,5},{5,4},{6,7},{7,6},{8,9},{9,8},{10,11... | collective-permute-start | bytes 6881288 | tf_op jit(solution)/shard_map/ppermute | solution.py:1069
  140.3 12.4 %collective-permute-start.8 = (bf16[8704,128]{1,0:T(8,128)(2,1)}, bf16[8704,128]{1,0:T(8,128)(2,1)}, u32[]{:S(2)}, u32[]{:S(2)}) collective-permute-start(bf16[8704,128]{1,0:T(8,128)(2,1)} %constant_dynamic-update-slice_fusion.refs_0_), channel_id=1, source_target_pairs={{0,1},{1,0},{2,3},{3,2},{4,5},{5,4},{6,7},{7,6},{8,9},{9,8},{10,11... | collective-permute-start | bytes 6684680 | tf_op jit(solution)/shard_map/ppermute | solution.py:1069
  143.6 3.5 collective-permute-start.10
  148.4 3.7 collective-permute-start.11
  197.5 33.7 %collective-permute-start.12 = (f32[1]{0:T(128)}, f32[1]{0:T(128)}, u32[]{:S(2)}, u32[]{:S(2)}) collective-permute-start(f32[1]{0:T(128)} %add.337), channel_id=1, source_target_pairs={{0,4},{2,6},{4,0},{6,2},{8,12},{10,14},{12,8},{14,10},{16,20},{18,... | collective-permute-start | bytes 20 | tf_op jit(solution)/shard_map/ppermute | solution.py:1215
  231.9 3.7 collective-permute-start.13
  236.2 99.7 %collective-permute-start.14 = (f32[1]{0:T(128)}, f32[1]{0:T(128)}, u32[]{:S(2)}, u32[]{:S(2)}) collective-permute-start(f32[1]{0:T(128)} %add.339), channel_id=1, source_target_pairs={{0,16},{2,18},{4,20},{6,22},{8,24},{10,26},{12,28},{14,30},{16,0},... | collective-permute-start | bytes 20 | tf_op jit(solution)/shard_map/ppermute | solution.py:1215
  336.6 39.7 %all-to-all-start = ((bf16[16,128,384]{2,1,0:T(8,128)(2,1)}), bf16[16,128,384]{2,1,0:T(8,128)(2,1)S(1)}, u32[]{:S(2)}, u32[]{:S(2)}) async-start(bf16[16,128,384]{2,1,0:T(8,128)(2,1)} %get-tuple-element.213), calls=%async_computation | async-start | bytes 3145728 | tf_op jit(solution)/shard_map/all_to_all | solution.py:1101
  377.4 48.7 %all-to-all-start.1 = ((bf16[16,128,384]{2,1,0:T(8,128)(2,1)}), bf16[16,128,384]{2,1,0:T(8,128)(2,1)S(1)}, u32[]{:S(2)}, u32[]{:S(2)}) async-start(bf16[16,128,384]{2,1,0:T(8,128)(2,1)} %get-tuple-element.227), calls=%async_computation.1 | async-start | bytes 3145728 | tf_op jit(solution)/shard_map/all_to_all | solution.py:1101
  427.3 40.9 %all-to-all-start.2 = ((bf16[16,128,384]{2,1,0:T(8,128)(2,1)}), bf16[16,128,384]{2,1,0:T(8,128)(2,1)S(1)}, u32[]{:S(2)}, u32[]{:S(2)}) async-start(bf16[16,128,384]{2,1,0:T(8,128)(2,1)} %get-tuple-element.237), calls=%async_computation.2 | async-start | bytes 3145728 | tf_op jit(solution)/shard_map/all_to_all | solution.py:1101
  469.4 49.0 %all-to-all-start.3 = ((bf16[16,128,384]{2,1,0:T(8,128)(2,1)}), bf16[16,128,384]{2,1,0:T(8,128)(2,1)S(1)}, u32[]{:S(2)}, u32[]{:S(2)}) async-start(bf16[16,128,384]{2,1,0:T(8,128)(2,1)} %get-tuple-element.241.refs_0_), calls=%async_computation.3 | async-start | bytes 3145728 | tf_op jit(solution)/shard_map/all_to_all | solution.py:1101
  519.6 40.6 %all-to-all-start.4 = ((bf16[16,128,384]{2,1,0:T(8,128)(2,1)}), bf16[16,128,384]{2,1,0:T(8,128)(2,1)S(1)}, u32[]{:S(2)}, u32[]{:S(2)}) async-start(bf16[16,128,384]{2,1,0:T(8,128)(2,1)} %get-tuple-element.250.refs_1_), calls=%async_computation.4 | async-start | bytes 3145728 | tf_op jit(solution)/shard_map/all_to_all | solution.py:1101
  560.2 8.5 %copy-start.41 = (f32[384,128]{1,0:T(8,128)S(1)}, f32[384,128]{1,0:T(8,128)}, u32[]{:S(2)}) copy-start(f32[384,128]{1,0:T(8,128)} %get-tuple-element.281) | copy-start | bytes 589828
  560.2 8.6 %copy-start.40 = (f32[384,16]{1,0:T(8,128)S(1)}, f32[384,16]{1,0:T(8,128)}, u32[]{:S(2)}) copy-start(f32[384,16]{1,0:T(8,128)} %get-tuple-element.280) | copy-start | bytes 73732
  561.3 53.1 %all-to-all-start.5 = ((bf16[16,128,384]{2,1,0:T(8,128)(2,1)}), bf16[16,128,384]{2,1,0:T(8,128)(2,1)S(1)}, u32[]{:S(2)}, u32[]{:S(2)}) async-start(bf16[16,128,384]{2,1,0:T(8,128)(2,1)} %get-tuple-element.263.refs_2_), calls=%async_computation.5 | async-start | bytes 3145728 | tf_op jit(solution)/shard_map/all_to_all | solution.py:1101
  614.4 17.5 %copy-start.28 = (bf16[16,128,384]{2,1,0:T(8,128)(2,1)}, bf16[16,128,384]{2,1,0:T(8,128)(2,1)S(1)}, u32[]{:S(2)}) copy-start(bf16[16,128,384]{2,1,0:T(8,128)(2,1)S(1)} %all-to-all-done.5) | copy-start | bytes 4718596
  631.9 7.9 collective-permute-start.17
  646.6 93.5 %all-to-all-start.6 = ((bf16[16,1104,128]{2,1,0:T(8,128)(2,1)}), bf16[16,1104,128]{2,1,0:T(8,128)(2,1)}, u32[]{:S(2)}, u32[]{:S(2)}) async-start(bf16[16,1104,128]{2,1,0:T(8,128)(2,1)} %fusion), calls=%async_computation.6 | async-start | bytes 9043968 | tf_op jit(solution)/shard_map/all_to_all | solution.py:1101
  687.1 28.1 %collective-permute-start.15 = (bf16[384,768]{1,0:T(8,128)(2,1)S(1)}, bf16[384,768]{1,0:T(8,128)(2,1)S(1)}, u32[]{:S(2)}, u32[]{:S(2)}) collective-permute-start(bf16[384,768]{1,0:T(8,128)(2,1)S(1)} %convert_element_type.86), channel_id=1, source_target_pairs={{0,1},{1,0},{2,3},{3,2},{4,5},{5,4},{6,7},{7,6},{8,9},{9,8},{10,11... | collective-permute-start | bytes 1769480 | tf_op jit(solution)/shard_map/ppermute | solution.py:1069
  687.3 27.9 %collective-permute-start.16 = (bf16[768,384]{1,0:T(8,128)(2,1)S(1)}, bf16[768,384]{1,0:T(8,128)(2,1)S(1)}, u32[]{:S(2)}, u32[]{:S(2)}) collective-permute-start(bf16[768,384]{1,0:T(8,128)(2,1)S(1)} %convert_element_type.87), channel_id=1, source_target_pairs={{0,1},{1,0},{2,3},{3,2},{4,5},{5,4},{6,7},{7,6},{8,9},{9,8},{10,11... | collective-permute-start | bytes 1769480 | tf_op jit(solution)/shard_map/ppermute | solution.py:1069
  715.2 31.4 %copy-start.18 = (bf16[384,768]{1,0:T(8,128)(2,1)}, bf16[384,768]{1,0:T(8,128)(2,1)S(1)}, u32[]{:S(2)}) copy-start(bf16[384,768]{1,0:T(8,128)(2,1)S(1)} %collective-permute-done.15) | copy-start | bytes 1769476
  715.2 32.3 %copy-start.20 = (bf16[768,384]{1,0:T(8,128)(2,1)}, bf16[768,384]{1,0:T(8,128)(2,1)S(1)}, u32[]{:S(2)}) copy-start(bf16[768,384]{1,0:T(8,128)(2,1)S(1)} %collective-permute-done.16) | copy-start | bytes 1769476
  743.9 4.5 collective-permute-start.18
  749.8 36.4 %copy-start.5 = (f32[279312]{0:T(1024)S(1)}, f32[279312]{0:T(1024)}, u32[]{:S(2)}) copy-start(f32[279312]{0:T(1024)} %param.30) | copy-start | bytes 3351748
  752.8 1.7 collective-permute-start.19
  754.5 4.4 collective-permute-start.20
  758.9 8.3 collective-permute-start.21
  767.2 13.2 %collective-permute-start.22 = (f32[48]{0:T(128)S(1)}, f32[48]{0:T(128)S(1)}, u32[]{:S(2)}, u32[]{:S(2)}) collective-permute-start(f32[48]{0:T(128)S(1)} %add.352), channel_id=1, source_target_pairs={{0,8},{2,10},{4,12},{6,14},{8,0},{10,2},{12,4},{14,6},{16,24},{18,... | collective-permute-start | bytes 584 | tf_op jit(solution)/shard_map/ppermute | solution.py:1095
  780.4 4.4 collective-permute-start.23
  802.6 1.2 collective-permute-start.24
  803.7 3.5 collective-permute-start.25
  807.3 3.5 collective-permute-start.26
  810.8 3.5 collective-permute-start.27
  814.4 4.4 collective-permute-start.28
  (38 other events, 98.2 us)
Sparse Core Ops, SparseCore 0:
  11.5 164.5 all-gather.2
  179.6 122.4 all-gather.4

commit v6 on v5

--- a/solution.py
+++ b/solution.py
@@ -514,6 +514,7 @@
 
 
 SLOTS = 128
+WIDE = 1024
 
 
 def by_load(load, capacity, work):
@@ -564,7 +565,7 @@
     @pl.when(expert == 0)
     def _():
         def start(i, carry):
-            rows = rows_of(i)
+            rows = rows_of(i, WIDE)
             z = plain(c_ref[rows, :], router[...])
             named = table[rows, :] >= 0
             shown = jnp.where(named, z, NEG)
@@ -572,15 +573,15 @@
             gates_ref[rows, :] = e / jnp.sum(e, -1, keepdims=True)
             return carry
 
-        lax.fori_loop(0, seq // ROWS, start, 0)
+        lax.fori_loop(0, seq // WIDE, start, 0)
 
     def fan(i, carry):
-        rows = rows_of(i)
+        rows = rows_of(i, WIDE)
         for source, out in ((table, spread_place), (gates_ref, spread_gate)):
-            out[0, rows, :] = jnp.broadcast_to(column_of(source[rows, :], expert), (ROWS, 128))
+            out[0, rows, :] = jnp.broadcast_to(column_of(source[rows, :], expert), (WIDE, 128))
         return carry
 
-    lax.fori_loop(0, seq // ROWS, fan, 0)
+    lax.fori_loop(0, seq // WIDE, fan, 0)
 
     def work(count):
         at = pl.ds(0, count)
@@ -610,7 +611,7 @@
         y_ref[at, :] = plain(act_ref[at, :], w_out[0]).astype(LOWTYPE)
 
         def add(i, carry):
-            rows = rows_of(i)
+            rows = rows_of(i, WIDE)
             taken = plain(patch_select(spread_place[0, rows, :], count), y_ref[at, :])
             taken_ref[0, rows, :] = taken.astype(LOWTYPE)
             for first in range(0, D, 128):
@@ -618,7 +619,7 @@
                 next_ref[rows, lanes] += spread_gate[0, rows, :] * taken[:, first : first + 128]
             return carry
 
-        lax.fori_loop(0, seq // ROWS, add, 0)
+        lax.fori_loop(0, seq // WIDE, add, 0)
 
     by_load(loads[expert], capacity, work)
 
@@ -630,7 +631,7 @@
     dy_refs, (low_ref, dz_ref, d_gates) = (refs[:-3], refs[-3:])
     expert = pl.program_id(0)
     seq, capacity = (grad_ref.shape[0], SLOTS * len(dy_refs))
-    lane = lax.broadcasted_iota(jnp.int32, (ROWS, d_gates.shape[1]), 1)
+    lane = lax.broadcasted_iota(jnp.int32, (WIDE, d_gates.shape[1]), 1)
 
     @pl.when(expert == 0)
     def _():
@@ -638,7 +639,7 @@
 
     def work(count):
         def one(i, carry):
-            rows = rows_of(i)
+            rows = rows_of(i, WIDE)
             grad = grad_ref[rows, :]
             gate = spread_gate[0, rows, :]
             taken = taken_ref[0, rows, :].astype(FULLTYPE)
@@ -649,7 +650,7 @@
                 low_ref[rows, lanes] = (gate * grad[:, first : first + 128]).astype(LOWTYPE)
             return carry
 
-        lax.fori_loop(0, seq // ROWS, one, 0)
+        lax.fori_loop(0, seq // WIDE, one, 0)
         put_blocks(dy_refs, plain(slot_select(place[0], count), low_ref[...]).astype(LOWTYPE))
 
     by_load(loads[expert], capacity, work)
@@ -657,7 +658,7 @@
     @pl.when(expert == pl.num_programs(0) - 1)
     def _():
         def last(i, carry):
-            rows = rows_of(i)
+            rows = rows_of(i, WIDE)
             gate = gates[rows, :]
             d_gate = d_gates[rows, :]
             d_z = gate * (d_gate - jnp.sum(gate * d_gate, -1, keepdims=True))
@@ -665,7 +666,7 @@
             d_c[rows, :] = right_t(dz_ref[rows, :], router[...])
             return carry
 
-        lax.fori_loop(0, seq // ROWS, last, 0)
+        lax.fori_loop(0, seq // WIDE, last, 0)
         d_router[...] = left_t(c_ref[...], dz_ref[...])
 
 
@@ -691,11 +692,11 @@
         back_ref[at, :] = back.astype(LOWTYPE)
 
         def add(i, carry):
-            rows = rows_of(i)
+            rows = rows_of(i, WIDE)
             d_c[rows, :] += plain(patch_select(spread_place[0, rows, :], count), back_ref[at, :])
             return carry
 
-        lax.fori_loop(0, seq // ROWS, add, 0)
+        lax.fori_loop(0, seq // WIDE, add, 0)
 
     by_load(loads[expert], capacity, work)
 

time: 856 us -> 853 us (level)
  Pallas kernels: 433 us -> 414 us
  waiting for transfers between devices: 150 us -> 164 us
    all_gather x1, waiting for transfers between devices: 23.2 us -> 35.2 us  [per_device(): all_out = lax.all_gather(low_out, ('ep', 'dp'))]
    pallas_call x7, Pallas kernels: 211 us -> 199 us  [local_call(): pl.pallas_call(kernel, out_shape=outs, in_specs=in_vmem(len(args)), out_s...]
  transfers between devices with their start and end apart: 38 -> 38, of which waited for: 22 -> 22; matrix products, arithmetic and copies ran while one was open for 7% -> 7% of each run, Pallas kernels for 49% -> 47%
where the time goes in v6:
time: 853 us; the launch traced here: 841 us
  Pallas kernels  414 us (49%)
  waiting for transfers between devices  164 us (19%)
  starting transfers between devices  106 us (12%)
  other arithmetic  71.5 us (8%)
  between operations  43.6 us (5%)
  local copies, waits for them, and re-layouts  42 us (5%)
    pallas_call x7, Pallas kernels, local_call(): pl.pallas_call(kernel, out_shape=outs, in_specs=in_vmem(len(args)), out_s...  199 us
    pallas_call x6, Pallas kernels, gridded(): pl.pallas_call(kernel, grid=(steps,), out_shape=outs, in_specs=in_specs,...  186 us
    ppermute x8, waiting for transfers between devices, gather_weights(): lax.ppermute(v, 'ep', [(i, i ^ order[step]) for i in range(owners)])  63.7 us
    all_to_all x7, starting transfers between devices, to_experts(): return lax.all_to_all(buffer, 'ep', split_axis=0, concat_axis=0, tiled=True)  48.3 us
    all_to_all x7, waiting for transfers between devices, to_experts(): return lax.all_to_all(buffer, 'ep', split_axis=0, concat_axis=0, tiled=True)  39.1 us
    all_gather x1, waiting for transfers between devices, per_device(): all_out = lax.all_gather(low_out, ('ep', 'dp'))  35.2 us
    ppermute x10, starting transfers between devices, sum_all(): lax.ppermute(value, axis, [(i, i ^ step) for i in range(count)])  33.2 us
    unnamed x104, local copies, waits for them, and re-layouts  20 us
  transfers between devices with their start and end apart: 38, of which 22 were waited for; matrix products, arithmetic and copies ran while one was open for 7% of the time, Pallas kernels for 47%

profile of v6, /device:TPU:0, one launch (start us, length us, event | category | flops | bytes accessed | tf_op | source)
XLA Modules:
  0.0 841.4 jit_solution(6986973787051990197)
XLA Ops:
  11.1 5.2 dynamic_update_slice.3
  18.8 3.0 collective-permute-start.1
  23.4 11.6 %collective-permute-done = bf16[544,128]{1,0:T(8,128)(2,1)S(1)} collective-permute-done((bf16[544,128]{1,0:T(8,128)(2,1)S(1)}, bf16[544,128]{1,0:T(8,128)(2,1)S(1)}, u32[]{:S(2)}, u32[]{:S(2)}) %collective-permute-start) | collective-permute-done | bytes 139296 | tf_op jit(solution)/shard_map/ppermute | solution.py:977
  35.7 5.4 collective-permute-start.3
  54.2 22.9 %collective-permute-done.2 = bf16[1088,128]{1,0:T(8,128)(2,1)S(1)} collective-permute-done((bf16[1088,128]{1,0:T(8,128)(2,1)}, bf16[1088,128]{1,0:T(8,128)(2,1)S(1)}, u32[]{:S(2)}, u32[]{:S(2)}) %collective-permute-start.2) | collective-permute-done | bytes 278560 | tf_op jit(solution)/shard_map/ppermute | solution.py:977
  82.3 9.2 %collective-permute-done.4 = bf16[2176,128]{1,0:T(8,128)(2,1)S(1)} collective-permute-done((bf16[2176,128]{1,0:T(8,128)(2,1)S(1)}, bf16[2176,128]{1,0:T(8,128)(2,1)S(1)}, u32[]{:S(2)}, u32[]{:S(2)}) %collective-permute-start.4) | collective-permute-done | bytes 557088 | tf_op jit(solution)/shard_map/ppermute | solution.py:977
  98.7 5.2 fusion.45
  106.0 12.0 %select_reduce_fusion = f32[1024,40]{1,0:T(8,128)S(1)} fusion(f32[1024,256]{1,0:T(8,128)S(1)} %get-tuple-element.474, s32[1024,256]{1,0:T(8,128)S(1)} %copy-done.39), kind=kLoop, calls=%fused_computation | loop fusion | flops 31416320 | bytes 2260992 | tf_op jit(solution)/shard_map/reduce_sum | solution.py:1193
  118.0 15.8 %collective-permute-done.6 = bf16[4352,128]{1,0:T(8,128)(2,1)S(1)} collective-permute-done((bf16[4352,128]{1,0:T(8,128)(2,1)S(1)}, bf16[4352,128]{1,0:T(8,128)(2,1)S(1)}, u32[]{:S(2)}, u32[]{:S(2)}) %collective-permute-start.6) | collective-permute-done | bytes 1114144 | tf_op jit(solution)/shard_map/ppermute | solution.py:977
  133.8 4.2 collective-permute-done.7
  154.1 11.3 %shard_map.367 = (bf16[768,384]{1,0:T(8,128)(2,1)}, bf16[384,1152]{1,0:T(8,128)(2,1)}, bf16[384,1152]{1,0:T(8,128)(2,1)}, bf16[384,1152]{1,0:T(8,128)(2,1)}, bf1...) custom-call(s32[2]{0:T(128)} %pad_add_fusion.place_ref, ...), custom_call_target="tpu_custom_call" | custom-call | bytes 18072584 | tf_op jit(solution)/shard_map/pallas_call | solution.py:989
  168.7 29.1 %shard_map.368 = (f32[1024,384]{1,0:T(8,128)}, f32[1024,384]{1,0:T(8,128)}, bf16[1024,384]{1,0:T(8,128)(2,1)}, bf16[1024,1152]{1,0:T(8,128)(2,1)}, bf16[1024,384...) custom-call(bf16[1024,768]{1,0:T(8,128)(2,1)} %refs_15_.1, ...), custom_call_target="tpu_custom_call" | custom-call | flops 6845104128 | bytes 25378816 | tf_op jit(solution)/shard_map/pallas_call | solution.py:230
  199.1 20.2 %shard_map.369 = (f32[1024,384]{1,0:T(8,128)}, bf16[1024,384]{1,0:T(8,128)(2,1)}, bf16[1024,1152]{1,0:T(8,128)(2,1)}, bf16[1024,384]{1,0:T(8,128)(2,1)}, bf16[1024,768]{1,0:T(8,128)(2,1)}) custom-call(f32[1024,384]{1,0:T(8,128)} %get-tuple-element.184.refs_0_.refs_1_, bf16[384,1152]{1,0:T(8,128)(2,1)} %get-tuple-element.185.refs_1_.refs_6_, ...), custom_call_target="tpu_custom_call" | custom-call | flops 4429185024 | bytes 9846784 | tf_op jit(solution)/shard_map/pallas_call | solution.py:230
  224.3 3.2 collective-permute-start.14
  227.6 39.2 %shard_map.370 = (f32[1024,16]{1,0:T(8,128)}, f32[16,1024,128]{2,1,0:T(8,128)}, f32[16,1024,128]{2,1,0:T(8,128)}, bf16[6144,1536]{1,0:T(8,128)(2,1)}, f32[6144,1...) custom-call(s32[16]{0:T(128)} %convert_element_type.80.loads, ...), custom_call_target="tpu_custom_call" | custom-call | flops 12079595520 | bytes 97988672 | tf_op jit(solution)/shard_map/pallas_call | solution.py:731
  266.8 35.2 %all-gather.5.cloned.1.call-done = bf16[32,768,384]{2,1,0:T(8,128)(2,1)} async-done(((bf16[1,768,384]{2,1,0:T(8,128)(2,1)}), bf16[32,768,384]{2,1,0:T(8,128)(2,1)}) %all-gather.5.cloned.1.call-update) | async-done | bytes 18874384 | tf_op jit(solution)/shard_map/all_gather | solution.py:1172
  302.0 32.3 %shard_map.371 = (f32[1024,384]{1,0:T(8,128)}, bf16[16,1024,384]{2,1,0:T(8,128)(2,1)}) custom-call(s32[16]{0:T(128)} %convert_element_type.80.loads, f32[1024,384]{1,0:T(8,128)} %get-tuple-element.187.mid_ref.refs_2_, f32[16,1024,128]{2,1,0:T(8,128)} %get-tuple-element.195.spread_place, f32[16,1024,128]{2,1,0:T(8,128)} %get-tuple-element.196.spread_gate, ...), custom_call_target="tpu_custom_call" | custom-call | flops 12079595520 | bytes 70254656 | tf_op jit(solution)/shard_map/pallas_call | solution.py:731
  335.1 4.3 all-to-all-start
  342.7 27.4 %shard_map.372 = (f32[1024,384]{1,0:T(8,128)}, bf16[1024,384]{1,0:T(8,128)(2,1)}, bf16[1024,1152]{1,0:T(8,128)(2,1)}, bf16[1024,384]{1,0:T(8,128)(2,1)}, bf16[10...) custom-call(f32[1024,384]{1,0:T(8,128)} %get-tuple-element.203.refs_0_.refs_1_, ...), custom_call_target="tpu_custom_call" | custom-call | flops 6845104128 | bytes 23216128 | tf_op jit(solution)/shard_map/pallas_call | solution.py:230
  370.1 5.1 shard_map.373
  376.3 7.4 all-to-all-start.1
  383.7 41.4 %shard_map.374 = (f32[384,1152]{1,0:T(8,128)}, f32[384,384]{1,0:T(8,128)}, f32[8,384]{1,0:T(8,128)}, f32[384,1536]{1,0:T(8,128)}, f32[1536,384]{1,0:T(8,128)}, /*index=5*/f32[1024,384]{1,0:T(8,128)}) custom-call(f32[1024,384]{1,0:T(8,128)} %get-tuple-element.218.refs_0_, f32[1024,384]{1,0:T(8,128)} %get-tuple-element.203.refs_0_.refs_1_, ...), custom_call_target="tpu_custom_call" | custom-call | flops 15300820992 | bytes 31879168 | tf_op jit(solution)/shard_map/pallas_call | solution.py:230
  426.3 7.0 all-to-all-start.2
  433.3 20.4 %shard_map.375 = (f32[384,16]{1,0:T(8,128)}, f32[1024,384]{1,0:T(8,128)}, bf16[16,128,384]{2,1,0:T(8,128)(2,1)}, bf16[16,128,384]{2,1,0:T(8,128)(2,1)}, bf16[16,128,384]{2,1,0:T(8,128)(2,1)}) custom-call(s32[16]{0:T(128)} %convert_element_type.80.loads, f32[1024,384]{1,0:T(8,128)} %get-tuple-element.230.grad_ref.refs_0_, ...), custom_call_target="tpu_custom_call" | custom-call | flops 9663676416 | bytes 29790272 | tf_op jit(solution)/shard_map/pallas_call | solution.py:731
  453.7 13.1 %all-to-all-done.2 = bf16[16,128,384]{2,1,0:T(8,128)(2,1)S(1)} async-done(((bf16[16,128,384]{2,1,0:T(8,128)(2,1)}), bf16[16,128,384]{2,1,0:T(8,128)(2,1)S(1)}, u32[]{:S(2)}, u32[]{:S(2)}) %all-to-all-start.2) | async-done | bytes 1572896 | tf_op jit(solution)/shard_map/all_to_all | solution.py:1102
  467.9 7.3 all-to-all-start.3
  475.3 39.4 %shard_map.376.refs_10_ = f32[1024,384]{1,0:T(8,128)} custom-call(s32[16]{0:T(128)} %convert_element_type.80.loads, f32[1024,384]{1,0:T(8,128)} %get-tuple-element.239.start_ref, f32[16,1024,128]{2,1,0:T(8,128)} %get-tuple-element.195.spread_place, bf16[16,2,384,768]{3,2,1,0:T(8,128)(2,1)} %bitcast.129, bf16[16,1536,384]{2,1,0:T(8,128)(2,1)} %bitcast.126, ...), custom_call_target="tpu_custom_call" | custom-call | flops 19327352832 | bytes 91750464 | tf_op jit(solution)/shard_map/pallas_call | solution.py:731
  515.9 7.8 all-to-all-start.4
  523.7 31.5 %shard_map.377 = (f32[384,1152]{1,0:T(8,128)}, f32[384,384]{1,0:T(8,128)}, f32[8,384]{1,0:T(8,128)}, f32[1024,384]{1,0:T(8,128)}) custom-call(f32[1024,384]{1,0:T(8,128)} %get-tuple-element.230.grad_ref.refs_0_, f32[1024,384]{1,0:T(8,128)} %get-tuple-element.184.refs_0_.refs_1_, f32[1024,384]{1,0:T(8,128)} %get-tuple-element.187.mid_ref.refs_2_, ...), custom_call_target="tpu_custom_call" | custom-call | flops 10468982784 | bytes 16150528 | tf_op jit(solution)/shard_map/pallas_call | solution.py:230
  557.6 7.3 all-to-all-start.5
  566.1 44.5 %shard_map.378 = (f32[384,1152]{1,0:T(8,128)}, f32[384,384]{1,0:T(8,128)}, f32[8,384]{1,0:T(8,128)}, f32[384,1536]{1,0:T(8,128)}, f32[1536,384]{1,0:T(8,128)}, /*index=5*/f32[768,384]{1,0:T(8,128)}) custom-call(f32[1024,384]{1,0:T(8,128)} %get-tuple-element.253.refs_0_, f32[1024,384]{1,0:T(8,128)} %get-tuple-element.254.refs_1_, ...), custom_call_target="tpu_custom_call" | custom-call | flops 15904800768 | bytes 33058816 | tf_op jit(solution)/shard_map/pallas_call | solution.py:230
  610.6 17.5 %shard_map.381 = (f32[1,16,1104,128]{3,2,1,0:T(8,128)}, bf16[1,16,1104,128]{3,2,1,0:T(8,128)(2,1)}) custom-call(s32[1]{0:T(128)} %bitcast.17.place_ref, f32[768,384]{1,0:T(8,128)} %get-tuple-element.269.refs_0_, f32[384,1152]{1,0:T(8,128)} %get-tuple-element.270.refs_1_, f32[384,1152]{1,0:T(8,128)} %get-tuple-element.271.refs_2_, ...), custom_call_target="tpu_custom_call" | custom-call | bytes 31469572 | tf_op jit(solution)/shard_map/pallas_call | solution.py:1054
  628.2 7.8 collective-permute-done.17
  636.0 6.8 fusion
  642.8 7.2 all-to-all-start.6
  654.7 27.2 %shard_map.380 = (f32[384,768]{1,0:T(8,128)}, f32[768,384]{1,0:T(8,128)}) custom-call(bf16[2048,384]{1,0:T(8,128)(2,1)} %bitcast.133, bf16[2048,384]{1,0:T(8,128)(2,1)} %bitcast.135, bf16[2048,384]{1,0:T(8,128)(2,1)} %bitcast.137, bf16[2048,384]{1,0:T(8,128)(2,1)} %bitcast.139, bf16[2048,384]{1,0:T(8,128)(2,1)} %bitcast.141, bf16[2048,384]{1,0:T(8,128)(2,1)} %bitcast.143, ...), custom_call_target="tpu_custom_call" | custom-call | flops 18119393280 | bytes 12976128 | tf_op jit(solution)/shard_map/pallas_call | solution.py:731
  684.0 27.4 %shard_map.379 = (f32[384,768]{1,0:T(8,128)}, f32[768,384]{1,0:T(8,128)}) custom-call(bf16[2048,384]{1,0:T(8,128)(2,1)} %bitcast.134, bf16[2048,384]{1,0:T(8,128)(2,1)} %bitcast.136, bf16[2048,384]{1,0:T(8,128)(2,1)} %bitcast.138, bf16[2048,384]{1,0:T(8,128)(2,1)} %bitcast.140, bf16[2048,384]{1,0:T(8,128)(2,1)} %bitcast.142, bf16[2048,384]{1,0:T(8,128)(2,1)} %bitcast.144, ...), custom_call_target="tpu_custom_call" | custom-call | flops 18119393280 | bytes 12976128 | tf_op jit(solution)/shard_map/pallas_call | solution.py:731
  711.5 24.8 %all-to-all-done.6 = bf16[16,1104,128]{2,1,0:T(8,128)(2,1)} async-done(((bf16[16,1104,128]{2,1,0:T(8,128)(2,1)}), bf16[16,1104,128]{2,1,0:T(8,128)(2,1)}, u32[]{:S(2)}, u32[]{:S(2)}) %all-to-all-start.6) | async-done | bytes 4522016 | tf_op jit(solution)/shard_map/all_to_all | solution.py:1102
  736.3 3.9 convert_reduce_fusion
  750.7 2.9 collective-permute-start.20
  755.1 6.7 collective-permute-start.21
  763.4 11.7 %collective-permute-start.22 = (f32[48]{0:T(128)S(1)}, f32[48]{0:T(128)S(1)}, u32[]{:S(2)}, u32[]{:S(2)}) collective-permute-start(f32[48]{0:T(128)S(1)} %add.352), channel_id=1, source_target_pairs={{0,8},{2,10},{4,12},{6,14},{8,0},{10,2},{12,4},{14,6},{16,24},{18,... | collective-permute-start | bytes 584 | tf_op jit(solution)/shard_map/ppermute | solution.py:1096
  776.6 2.8 collective-permute-start.23
  782.4 4.0 multiply_add_fusion.6
  786.5 2.9 multiply_reduce_fusion
  790.2 2.9 multiply_reduce_fusion.1
  794.2 4.5 fusion.46
  810.6 2.8 collective-permute-start.28
  (234 shorter events, 105.2 us)
Async XLA Ops:
  7.2 190.6 %all-gather.3.cloned.1.call-start = ((), (), s32[]{:S(2)}) async-start(), calls=%async_computation.7 | async-start | bytes 19464192 | tf_op jit(solution)/shard_map/all_gather | solution.py:1171
  9.5 292.5 %all-gather.5.cloned.1.call-start = ((), (), s32[]{:S(2)}) async-start(), calls=%async_computation.8 | async-start | bytes 19464192 | tf_op jit(solution)/shard_map/all_gather | solution.py:1172
  17.1 24.7 %copy-start.47 = (s32[16]{0:T(128)S(1)}, s32[16]{0:T(128)}, u32[]{:S(2)}) copy-start(s32[16]{0:T(128)} %constant.302.clone) | copy-start | bytes 196
  17.1 32.5 %copy-start.44 = (s32[18]{0:T(128)S(1)}, s32[18]{0:T(128)}, u32[]{:S(2)}) copy-start(s32[18]{0:T(128)} %constant.303.clone..sunk.10) | copy-start | bytes 220
  18.8 16.2 %collective-permute-start.1 = (bf16[560,128]{1,0:T(8,128)(2,1)S(1)}, bf16[560,128]{1,0:T(8,128)(2,1)S(1)}, u32[]{:S(2)}, u32[]{:S(2)}) collective-permute-start(bf16[560,128]{1,0:T(8,128)(2,1)S(1)} %get-tuple-element.470), channel_id=1, source_target_pairs={{0,8},{2,10},{4,12},{6,14},{8,0},{10,2},{12,4},{14,6},{16,24},{18,... | collective-permute-start | bytes 430088 | tf_op jit(solution)/shard_map/ppermute | solution.py:977
  23.4 11.6 %collective-permute-start = (bf16[544,128]{1,0:T(8,128)(2,1)S(1)}, bf16[544,128]{1,0:T(8,128)(2,1)S(1)}, u32[]{:S(2)}, u32[]{:S(2)}) collective-permute-start(bf16[544,128]{1,0:T(8,128)(2,1)S(1)} %get-tuple-element.472), channel_id=1, source_target_pairs={{0,8},{2,10},{4,12},{6,14},{8,0},{10,2},{12,4},{14,6},{16,24},{18,... | collective-permute-start | bytes 417800 | tf_op jit(solution)/shard_map/ppermute | solution.py:977
  35.7 41.3 %collective-permute-start.3 = (bf16[1120,128]{1,0:T(8,128)(2,1)}, bf16[1120,128]{1,0:T(8,128)(2,1)S(1)}, u32[]{:S(2)}, u32[]{:S(2)}) collective-permute-start(bf16[1120,128]{1,0:T(8,128)(2,1)} %pad_maximum_fusion.5), channel_id=1, source_target_pairs={{0,16},{2,18},{4,20},{6,22},{8,24},{10,26},{12,28},{14,30},{16,0},... | collective-permute-start | bytes 860168 | tf_op jit(solution)/shard_map/ppermute | solution.py:977
  41.9 35.2 %collective-permute-start.2 = (bf16[1088,128]{1,0:T(8,128)(2,1)}, bf16[1088,128]{1,0:T(8,128)(2,1)S(1)}, u32[]{:S(2)}, u32[]{:S(2)}) collective-permute-start(bf16[1088,128]{1,0:T(8,128)(2,1)} %pad_maximum_fusion.6), channel_id=1, source_target_pairs={{0,16},{2,18},{4,20},{6,22},{8,24},{10,26},{12,28},{14,30},{16,0},... | collective-permute-start | bytes 835592 | tf_op jit(solution)/shard_map/ppermute | solution.py:977
  77.1 14.5 %collective-permute-start.4 = (bf16[2176,128]{1,0:T(8,128)(2,1)S(1)}, bf16[2176,128]{1,0:T(8,128)(2,1)S(1)}, u32[]{:S(2)}, u32[]{:S(2)}) collective-permute-start(bf16[2176,128]{1,0:T(8,128)(2,1)S(1)} %pad_maximum_fusion.4), channel_id=1, source_target_pairs={{0,2},{2,0},{4,6},{6,4},{8,10},{10,8},{12,14},{14,12},{16,18},{18,... | collective-permute-start | bytes 1671176 | tf_op jit(solution)/shard_map/ppermute | solution.py:977
  78.6 12.9 %collective-permute-start.5 = (bf16[2240,128]{1,0:T(8,128)(2,1)S(1)}, bf16[2240,128]{1,0:T(8,128)(2,1)S(1)}, u32[]{:S(2)}, u32[]{:S(2)}) collective-permute-start(bf16[2240,128]{1,0:T(8,128)(2,1)S(1)} %pad_maximum_fusion.3), channel_id=1, source_target_pairs={{0,4},{2,6},{4,0},{6,2},{8,12},{10,14},{12,8},{14,10},{16,20},{18,... | collective-permute-start | bytes 1720328 | tf_op jit(solution)/shard_map/ppermute | solution.py:977
  91.6 42.2 %collective-permute-start.6 = (bf16[4352,128]{1,0:T(8,128)(2,1)S(1)}, bf16[4352,128]{1,0:T(8,128)(2,1)S(1)}, u32[]{:S(2)}, u32[]{:S(2)}) collective-permute-start(bf16[4352,128]{1,0:T(8,128)(2,1)S(1)} %pad_maximum_fusion.2), channel_id=1, source_target_pairs={{0,4},{2,6},{4,0},{6,2},{8,12},{10,14},{12,8},{14,10},{16,20},{18,... | collective-permute-start | bytes 3342344 | tf_op jit(solution)/shard_map/ppermute | solution.py:977
  93.2 44.8 %collective-permute-start.7 = (bf16[4480,128]{1,0:T(8,128)(2,1)S(1)}, bf16[4480,128]{1,0:T(8,128)(2,1)S(1)}, u32[]{:S(2)}, u32[]{:S(2)}) collective-permute-start(bf16[4480,128]{1,0:T(8,128)(2,1)S(1)} %pad_maximum_fusion), channel_id=1, source_target_pairs={{0,2},{2,0},{4,6},{6,4},{8,10},{10,8},{12,14},{14,12},{16,18},{18,... | collective-permute-start | bytes 3440648 | tf_op jit(solution)/shard_map/ppermute | solution.py:977
  96.9 7.0 copy-start.42
  96.9 7.0 copy-start.38
  139.2 13.5 %collective-permute-start.9 = (bf16[8960,128]{1,0:T(8,128)(2,1)}, bf16[8960,128]{1,0:T(8,128)(2,1)S(1)}, u32[]{:S(2)}, u32[]{:S(2)}) collective-permute-start(bf16[8960,128]{1,0:T(8,128)(2,1)} %constant_dynamic-update-slice_fusion.5.refs_1_), channel_id=1, source_target_pairs={{0,1},{1,0},{2,3},{3,2},{4,5},{5,4},{6,7},{7,6},{8,9},{9,8},{10,11... | collective-permute-start | bytes 6881288 | tf_op jit(solution)/shard_map/ppermute | solution.py:1070
  140.3 12.4 %collective-permute-start.8 = (bf16[8704,128]{1,0:T(8,128)(2,1)}, bf16[8704,128]{1,0:T(8,128)(2,1)}, u32[]{:S(2)}, u32[]{:S(2)}) collective-permute-start(bf16[8704,128]{1,0:T(8,128)(2,1)} %constant_dynamic-update-slice_fusion.refs_0_), channel_id=1, source_target_pairs={{0,1},{1,0},{2,3},{3,2},{4,5},{5,4},{6,7},{7,6},{8,9},{9,8},{10,11... | collective-permute-start | bytes 6684680 | tf_op jit(solution)/shard_map/ppermute | solution.py:1070
  143.6 3.5 collective-permute-start.10
  148.4 3.7 collective-permute-start.11
  197.8 21.6 %collective-permute-start.12 = (f32[1]{0:T(128)}, f32[1]{0:T(128)}, u32[]{:S(2)}, u32[]{:S(2)}) collective-permute-start(f32[1]{0:T(128)} %add.337), channel_id=1, source_target_pairs={{0,4},{2,6},{4,0},{6,2},{8,12},{10,14},{12,8},{14,10},{16,20},{18,... | collective-permute-start | bytes 20 | tf_op jit(solution)/shard_map/ppermute | solution.py:1216
  220.0 3.7 collective-permute-start.13
  224.3 110.0 %collective-permute-start.14 = (f32[1]{0:T(128)}, f32[1]{0:T(128)}, u32[]{:S(2)}, u32[]{:S(2)}) collective-permute-start(f32[1]{0:T(128)} %add.339), channel_id=1, source_target_pairs={{0,16},{2,18},{4,20},{6,22},{8,24},{10,26},{12,28},{14,30},{16,0},... | collective-permute-start | bytes 20 | tf_op jit(solution)/shard_map/ppermute | solution.py:1216
  335.1 40.1 %all-to-all-start = ((bf16[16,128,384]{2,1,0:T(8,128)(2,1)}), bf16[16,128,384]{2,1,0:T(8,128)(2,1)S(1)}, u32[]{:S(2)}, u32[]{:S(2)}) async-start(bf16[16,128,384]{2,1,0:T(8,128)(2,1)} %get-tuple-element.213), calls=%async_computation | async-start | bytes 3145728 | tf_op jit(solution)/shard_map/all_to_all | solution.py:1102
  376.3 48.8 %all-to-all-start.1 = ((bf16[16,128,384]{2,1,0:T(8,128)(2,1)}), bf16[16,128,384]{2,1,0:T(8,128)(2,1)S(1)}, u32[]{:S(2)}, u32[]{:S(2)}) async-start(bf16[16,128,384]{2,1,0:T(8,128)(2,1)} %get-tuple-element.227), calls=%async_computation.1 | async-start | bytes 3145728 | tf_op jit(solution)/shard_map/all_to_all | solution.py:1102
  426.3 40.5 %all-to-all-start.2 = ((bf16[16,128,384]{2,1,0:T(8,128)(2,1)}), bf16[16,128,384]{2,1,0:T(8,128)(2,1)S(1)}, u32[]{:S(2)}, u32[]{:S(2)}) async-start(bf16[16,128,384]{2,1,0:T(8,128)(2,1)} %get-tuple-element.237), calls=%async_computation.2 | async-start | bytes 3145728 | tf_op jit(solution)/shard_map/all_to_all | solution.py:1102
  467.9 46.8 %all-to-all-start.3 = ((bf16[16,128,384]{2,1,0:T(8,128)(2,1)}), bf16[16,128,384]{2,1,0:T(8,128)(2,1)S(1)}, u32[]{:S(2)}, u32[]{:S(2)}) async-start(bf16[16,128,384]{2,1,0:T(8,128)(2,1)} %get-tuple-element.241.refs_0_), calls=%async_computation.3 | async-start | bytes 3145728 | tf_op jit(solution)/shard_map/all_to_all | solution.py:1102
  515.9 40.6 %all-to-all-start.4 = ((bf16[16,128,384]{2,1,0:T(8,128)(2,1)}), bf16[16,128,384]{2,1,0:T(8,128)(2,1)S(1)}, u32[]{:S(2)}, u32[]{:S(2)}) async-start(bf16[16,128,384]{2,1,0:T(8,128)(2,1)} %get-tuple-element.250.refs_1_), calls=%async_computation.4 | async-start | bytes 3145728 | tf_op jit(solution)/shard_map/all_to_all | solution.py:1102
  556.4 8.5 %copy-start.41 = (f32[384,128]{1,0:T(8,128)S(1)}, f32[384,128]{1,0:T(8,128)}, u32[]{:S(2)}) copy-start(f32[384,128]{1,0:T(8,128)} %get-tuple-element.281) | copy-start | bytes 589828
  556.4 8.6 %copy-start.40 = (f32[384,16]{1,0:T(8,128)S(1)}, f32[384,16]{1,0:T(8,128)}, u32[]{:S(2)}) copy-start(f32[384,16]{1,0:T(8,128)} %get-tuple-element.280) | copy-start | bytes 73732
  557.6 53.0 %all-to-all-start.5 = ((bf16[16,128,384]{2,1,0:T(8,128)(2,1)}), bf16[16,128,384]{2,1,0:T(8,128)(2,1)S(1)}, u32[]{:S(2)}, u32[]{:S(2)}) async-start(bf16[16,128,384]{2,1,0:T(8,128)(2,1)} %get-tuple-element.263.refs_2_), calls=%async_computation.5 | async-start | bytes 3145728 | tf_op jit(solution)/shard_map/all_to_all | solution.py:1102
  610.6 17.5 %copy-start.28 = (bf16[16,128,384]{2,1,0:T(8,128)(2,1)}, bf16[16,128,384]{2,1,0:T(8,128)(2,1)S(1)}, u32[]{:S(2)}) copy-start(bf16[16,128,384]{2,1,0:T(8,128)(2,1)S(1)} %all-to-all-done.5) | copy-start | bytes 4718596
  628.1 7.9 collective-permute-start.17
  642.8 93.5 %all-to-all-start.6 = ((bf16[16,1104,128]{2,1,0:T(8,128)(2,1)}), bf16[16,1104,128]{2,1,0:T(8,128)(2,1)}, u32[]{:S(2)}, u32[]{:S(2)}) async-start(bf16[16,1104,128]{2,1,0:T(8,128)(2,1)} %fusion), calls=%async_computation.6 | async-start | bytes 9043968 | tf_op jit(solution)/shard_map/all_to_all | solution.py:1102
  683.3 28.1 %collective-permute-start.15 = (bf16[384,768]{1,0:T(8,128)(2,1)S(1)}, bf16[384,768]{1,0:T(8,128)(2,1)S(1)}, u32[]{:S(2)}, u32[]{:S(2)}) collective-permute-start(bf16[384,768]{1,0:T(8,128)(2,1)S(1)} %convert_element_type.86), channel_id=1, source_target_pairs={{0,1},{1,0},{2,3},{3,2},{4,5},{5,4},{6,7},{7,6},{8,9},{9,8},{10,11... | collective-permute-start | bytes 1769480 | tf_op jit(solution)/shard_map/ppermute | solution.py:1070
  683.6 27.9 %collective-permute-start.16 = (bf16[768,384]{1,0:T(8,128)(2,1)S(1)}, bf16[768,384]{1,0:T(8,128)(2,1)S(1)}, u32[]{:S(2)}, u32[]{:S(2)}) collective-permute-start(bf16[768,384]{1,0:T(8,128)(2,1)S(1)} %convert_element_type.87), channel_id=1, source_target_pairs={{0,1},{1,0},{2,3},{3,2},{4,5},{5,4},{6,7},{7,6},{8,9},{9,8},{10,11... | collective-permute-start | bytes 1769480 | tf_op jit(solution)/shard_map/ppermute | solution.py:1070
  711.4 31.4 %copy-start.18 = (bf16[384,768]{1,0:T(8,128)(2,1)}, bf16[384,768]{1,0:T(8,128)(2,1)S(1)}, u32[]{:S(2)}) copy-start(bf16[384,768]{1,0:T(8,128)(2,1)S(1)} %collective-permute-done.15) | copy-start | bytes 1769476
  711.4 32.3 %copy-start.20 = (bf16[768,384]{1,0:T(8,128)(2,1)}, bf16[768,384]{1,0:T(8,128)(2,1)S(1)}, u32[]{:S(2)}) copy-start(bf16[768,384]{1,0:T(8,128)(2,1)S(1)} %collective-permute-done.16) | copy-start | bytes 1769476
  740.1 4.5 collective-permute-start.18
  746.0 36.4 %copy-start.5 = (f32[279312]{0:T(1024)S(1)}, f32[279312]{0:T(1024)}, u32[]{:S(2)}) copy-start(f32[279312]{0:T(1024)} %param.30) | copy-start | bytes 3351748
  749.0 1.7 collective-permute-start.19
  750.7 4.4 collective-permute-start.20
  755.1 8.3 collective-permute-start.21
  763.4 13.2 %collective-permute-start.22 = (f32[48]{0:T(128)S(1)}, f32[48]{0:T(128)S(1)}, u32[]{:S(2)}, u32[]{:S(2)}) collective-permute-start(f32[48]{0:T(128)S(1)} %add.352), channel_id=1, source_target_pairs={{0,8},{2,10},{4,12},{6,14},{8,0},{10,2},{12,4},{14,6},{16,24},{18,... | collective-permute-start | bytes 584 | tf_op jit(solution)/shard_map/ppermute | solution.py:1096
  776.6 4.4 collective-permute-start.23
  798.8 1.2 collective-permute-start.24
  800.0 3.5 collective-permute-start.25
  803.5 3.5 collective-permute-start.26
  807.1 3.5 collective-permute-start.27
  810.6 4.4 collective-permute-start.28
  (38 other events, 98.2 us)
Sparse Core Ops, SparseCore 0:
  11.5 164.5 all-gather.2
  179.6 122.4 all-gather.4
